TPU v7x, 512 devices: a whole 4x8x8 slice. The times are simulated.
512 devices in a mesh: tm: 8 (over y), rows: 64 (over z, x, core).
Axes of the slice: x: 4, y: 8, z: 8, core: 2. Of those that a mesh axis runs over, the one named last changes fastest.
Arguments:
- latent: bfloat16 [16, 64, 32, 384], P('tm', 'rows'), may hold values from -6 to 6
- gain_one: float32 [384], replicated, may hold values from 0.1 to 1.9
- weight_one: bfloat16 [3, 3, 3, 384, 384], P(None, None, None, None, 'rows'), may hold values from -0.0625 to 0.0625
- bias_one: float32 [384], replicated, may hold values from -1.2 to 1.2
- gain_two: float32 [384], replicated, may hold values from 0.1 to 1.9
- weight_two: bfloat16 [3, 3, 3, 384, 384], P(None, None, None, None, 'rows'), may hold values from -0.0625 to 0.0625
- bias_two: float32 [384], replicated, may hold values from -1.2 to 1.2
Outputs:
- block_out: bfloat16 [16, 64, 32, 384], P('tm', 'rows')
All inputs are finite; a program needn't handle non-finite values.
Results may differ from a plain program's by a relative error of at most 0.01.
Values may be sent and summed in bfloat16 or wider, within the bound.
No kernel may reach another device: no remote copies, remote signals or barrier semaphores. Data moves between devices by JAX's collectives and lax.ppermute only.
A program may use at most 128 MiB of HBM per device.

v0:
```python
import jax
import jax.numpy as jnp
from jax import lax
from jax.sharding import PartitionSpec as P


def from_behind(value, axis, by):
    peers = lax.axis_size(axis)
    pairs = [(i, i + by) for i in range(peers) if 0 <= i + by < peers]
    return lax.ppermute(value, axis, pairs)


def with_halo(value, sides, width):
    for axis, dim in sides:
        peers, length = (lax.axis_size(axis), value.shape[dim])
        up = [(i, (i + 1) % peers) for i in range(peers - 1)]
        down = [(j, i) for i, j in up]
        last = lax.slice_in_dim(value, length - width, length, axis=dim)
        initial = lax.slice_in_dim(value, 0, width, axis=dim)
        before = lax.ppermute(last, axis, up)
        after = lax.ppermute(initial, axis, down)
        value = jnp.concatenate([before, value, after], axis=dim)
    return value


def rms_silu(values, gain):
    square_mean = jnp.mean(values * values, axis=-1, keepdims=True)
    normed = values * lax.rsqrt(square_mean + 1e-06) * gain
    return jax.nn.silu(normed).astype(jnp.bfloat16)


def unfold(padded):
    frames = padded.shape[0] - 2
    height = padded.shape[1] - 2
    width = padded.shape[2] - 2
    windows = []
    for tap_t in range(3):
        for tap_h in range(3):
            for tap_w in range(3):
                windows.append(
                    padded[tap_t : tap_t + frames, tap_h : tap_h + height, tap_w : tap_w + width]
                )
    return jnp.concatenate(windows, axis=-1)


def convolve(padded, weight):
    stacked = unfold(padded)
    frames, height, width, depth = stacked.shape
    kernel = weight.reshape(depth, weight.shape[4])
    total = jnp.dot(stacked.reshape(-1, depth), kernel, preferred_element_type=jnp.float32)
    return total.reshape(frames, height, width, -1)


def conv_layer(field, weight, bias):
    earlier = from_behind(field, "tm", 1)
    extended = jnp.concatenate([earlier, field], axis=0)
    rimmed = with_halo(extended, (("rows", 1),), 1)
    padded = jnp.pad(rimmed, ((0, 0), (0, 0), (1, 1), (0, 0)))
    whole_kernel = lax.all_gather(weight, "rows", axis=4, tiled=True)
    return convolve(padded, whole_kernel) + bias


def per_device(latent, gain_one, weight_one, bias_one, gain_two, weight_two, bias_two):
    hidden_one = rms_silu(latent.astype(jnp.float32), gain_one)
    middle = conv_layer(hidden_one, weight_one, bias_one).astype(jnp.bfloat16)
    hidden_two = rms_silu(middle.astype(jnp.float32), gain_two)
    result = latent.astype(jnp.float32) + conv_layer(hidden_two, weight_two, bias_two)
    return result.astype(jnp.bfloat16)


def solution(mesh):
    in_specs = (
        P("tm", "rows", None, None),
        P(),
        P(None, None, None, None, "rows"),
        P(),
        P(),
        P(None, None, None, None, "rows"),
        P(),
    )
    out_specs = P("tm", "rows", None, None)
    return jax.shard_map(
        per_device, mesh=mesh, in_specs=in_specs, out_specs=out_specs, check_vma=False
    )
```

profile of v0, /device:TPU:1, one launch (start us, length us, event | category | flops | bytes accessed | tf_op | source)
XLA Modules:
  0.0 233.7 jit_solution(16421080992686537392)
XLA Ops:
  6.5 1.6 copy.13
  8.2 0.0 all-gather.3.cloned.1.call-update
  8.2 0.0 all-gather.5.cloned.1.call-start
  8.3 1.6 copy.15
  9.9 0.0 all-gather.5.cloned.1.call-update
  9.9 0.9 fusion.39
  10.8 0.9 fusion.46
  11.7 4.0 %collective-permute-start = (bf16[2,1,32,384]{3,2,0,1:T(8,128)(2,1)S(1)}, bf16[2,1,32,384]{3,2,0,1:T(8,128)(2,1)S(1)}, u32[]{:S(2)}, u32[]{:S(2)}) collective-permute-start(bf16[2,1,32,384]{3,2,0,1:T(8,128)(2,1)S(1)} %fusion.46), channel_id=1, source_target_pairs={{0,64},{64,128},{128,192},{192,256},{256,320},{320,384},{384,448},... | collective-permute-start | bytes 147464 | tf_op jit(solution)/shard_map/ppermute | solution.py:10
  15.8 1.2 collective-permute-done
  17.0 0.0 copy-start
  17.0 0.0 copy-start.2
  17.0 4.7 %collective-permute-start.1 = (bf16[4,1,32,384]{3,2,0,1:T(8,128)(2,1)S(1)}, bf16[4,1,32,384]{3,2,0,1:T(8,128)(2,1)S(1)}, u32[]{:S(2)}, u32[]{:S(2)}) collective-permute-start(bf16[4,1,32,384]{3,2,0,1:T(8,128)(2,1)S(1)} %pad_maximum_fusion), channel_id=1, source_target_pairs={{0,1},{1,2},{2,3},{3,4},{4,5},{5,6},{6,7},{7,8},{8,9},{9,10},{10,1... | collective-permute-start | bytes 294920 | tf_op jit(solution)/shard_map/ppermute | solution.py:20
  21.7 3.4 %collective-permute-start.2 = (bf16[4,1,32,384]{3,2,0,1:T(8,128)(2,1)S(1)}, bf16[4,1,32,384]{3,2,0,1:T(8,128)(2,1)S(1)}, u32[]{:S(2)}, u32[]{:S(2)}) collective-permute-start(bf16[4,1,32,384]{3,2,0,1:T(8,128)(2,1)S(1)} %pad_maximum_fusion), channel_id=1, source_target_pairs={{1,0},{2,1},{3,2},{4,3},{5,4},{6,5},{7,6},{8,7},{9,8},{10,9},{11,1... | collective-permute-start | bytes 294920 | tf_op jit(solution)/shard_map/ppermute | solution.py:21
  25.0 0.0 collective-permute-done.1
  25.1 2.5 %collective-permute-done.2 = bf16[4,1,32,384]{3,2,0,1:T(8,128)(2,1)S(1)} collective-permute-done((bf16[4,1,32,384]{3,2,0,1:T(8,128)(2,1)S(1)}, bf16[4,1,32,384]{3,2,0,1:T(8,128)(2,1)S(1)}, u32[]{:S(2)}, u32[]{:S(2)}) %collective-permute-start.2) | collective-permute-done | bytes 98336 | tf_op jit(solution)/shard_map/ppermute | solution.py:21
  27.6 0.1 fusion.36
  28.2 0.1 constant_dynamic-update-slice_fusion.4
  28.4 0.0 copy-start.3
  28.4 80.6 %all-gather.3.cloned.1.call-done = bf16[3,3,3,384,384]{3,2,1,0,4:T(4,128)(2,1)} async-done(((bf16[3,3,3,384,6]{3,2,1,0,4:T(4,128)(2,1)}), bf16[3,3,3,384,384]{3,2,1,0,4:T(4,128)(2,1)}) %all-gather.3.cloned.1.call-update) | async-done | bytes 7962640 | tf_op jit(solution)/shard_map/all_gather | solution.py:59
  109.0 19.6 %copy.14 = bf16[3,3,3,384,384]{4,3,2,1,0:T(8,128)(2,1)} copy(bf16[3,3,3,384,384]{3,2,1,0,4:T(4,128)(2,1)} %all-gather.3.cloned.1.call-done) | data formatting | bytes 15925248 | tf_op jit(solution)/shard_map/all_gather | solution.py:59
  128.6 4.7 %multiply_reduce_fusion = (f32[2,32]{1,0:T(2,128)S(1)}, f32[2,32,384]{2,1,0:T(8,128)S(1)}) fusion(f32[384]{0:T(512)S(1)} %copy-done.3, bf16[10368,384,1]{1,0,2:T(8,128)(2,1)} %bitcast.52, bf16[2,1,32,10368]{3,2,0,1:T(8,128)(2,1)S(1)} %constant_dynamic-update-slice_fusion), kind=kOutput, calls=%fused_computation.98 | convolution fusion | flops 509730752 | bytes 9389824 | tf_op jit(solution)/shard_map/dot_general | solution.py:50
  133.3 0.1 fusion.49
  133.4 3.1 %collective-permute-start.3 = (bf16[2,1,32,384]{3,2,0,1:T(8,128)(2,1)S(1)}, bf16[2,1,32,384]{3,2,0,1:T(8,128)(2,1)S(1)}, u32[]{:S(2)}, u32[]{:S(2)}) collective-permute-start(bf16[2,1,32,384]{3,2,0,1:T(8,128)(2,1)S(1)} %fusion.49), channel_id=1, source_target_pairs={{0,64},{64,128},{128,192},{192,256},{256,320},{320,384},{384,448},... | collective-permute-start | bytes 147464 | tf_op jit(solution)/shard_map/ppermute | solution.py:10
  136.6 1.2 collective-permute-done.3
  137.7 2.8 %collective-permute-start.4 = (bf16[4,1,32,384]{3,2,0,1:T(8,128)(2,1)S(1)}, bf16[4,1,32,384]{3,2,0,1:T(8,128)(2,1)S(1)}, u32[]{:S(2)}, u32[]{:S(2)}) collective-permute-start(bf16[4,1,32,384]{3,2,0,1:T(8,128)(2,1)S(1)} %pad_maximum_fusion.1), channel_id=1, source_target_pairs={{0,1},{1,2},{2,3},{3,4},{4,5},{5,6},{6,7},{7,8},{8,9},{9,10},{10,1... | collective-permute-start | bytes 294920 | tf_op jit(solution)/shard_map/ppermute | solution.py:20
  140.5 1.9 collective-permute-start.5
  142.5 58.8 %all-gather.5.cloned.1.call-done = bf16[3,3,3,384,384]{3,2,1,0,4:T(4,128)(2,1)} async-done(((bf16[3,3,3,384,6]{3,2,1,0,4:T(4,128)(2,1)}), bf16[3,3,3,384,384]{3,2,1,0,4:T(4,128)(2,1)}) %all-gather.5.cloned.1.call-update) | async-done | bytes 7962640 | tf_op jit(solution)/shard_map/all_gather | solution.py:59
  201.2 19.5 %copy.16 = bf16[3,3,3,384,384]{4,3,2,1,0:T(8,128)(2,1)} copy(bf16[3,3,3,384,384]{3,2,1,0,4:T(4,128)(2,1)} %all-gather.5.cloned.1.call-done) | data formatting | bytes 15925248 | tf_op jit(solution)/shard_map/all_gather | solution.py:59
  220.8 0.1 select_maximum_fusion
  220.9 0.0 copy-start.4
  221.4 0.1 constant_dynamic-update-slice_fusion.31
  221.6 5.2 %fusion.25 = bf16[2,1,32,384]{3,2,1,0:T(8,128)(2,1)} fusion(bf16[10368,384,1]{1,0,2:T(8,128)(2,1)} %bitcast.53, bf16[2,1,32,10368]{3,2,0,1:T(8,128)(2,1)S(1)} %constant_dynamic-update-slice_fusion.27, bf16[2,1,32,384]{3,2,1,0:T(8,128)(2,1)S(1)} %copy-done, f32[384]{0:T(512)S(1)} %copy-done.4), kind=kOutput, calls=%fused_computation.11 | convolution fusion | flops 509706240 | bytes 9389568 | tf_op jit(solution)/shard_map/dot_general | solution.py:50
  (65 shorter events, 0.9 us)
Async XLA Ops:
  6.5 102.5 %all-gather.3.cloned.1.call-start = ((), (), s32[]{:S(2)}) async-start(), calls=%async_computation | async-start | bytes 10782720 | tf_op jit(solution)/shard_map/all_gather | solution.py:59
  8.2 193.0 %all-gather.5.cloned.1.call-start = ((), (), s32[]{:S(2)}) async-start(), calls=%async_computation.1 | async-start | bytes 10782720 | tf_op jit(solution)/shard_map/all_gather | solution.py:59
  11.7 5.2 %collective-permute-start = (bf16[2,1,32,384]{3,2,0,1:T(8,128)(2,1)S(1)}, bf16[2,1,32,384]{3,2,0,1:T(8,128)(2,1)S(1)}, u32[]{:S(2)}, u32[]{:S(2)}) collective-permute-start(bf16[2,1,32,384]{3,2,0,1:T(8,128)(2,1)S(1)} %fusion.46), channel_id=1, source_target_pairs={{0,64},{64,128},{128,192},{192,256},{256,320},{320,384},{384,448},... | collective-permute-start | bytes 147464 | tf_op jit(solution)/shard_map/ppermute | solution.py:10
  17.0 11.2 %copy-start = (bf16[2,1,32,384]{3,2,1,0:T(8,128)(2,1)S(1)}, bf16[2,1,32,384]{3,2,1,0:T(8,128)(2,1)}, u32[]{:S(2)}) copy-start(bf16[2,1,32,384]{3,2,1,0:T(8,128)(2,1)} %param.7) | copy-start | bytes 147460
  17.0 11.2 %copy-start.2 = (f32[384]{0:T(512)S(1)}, f32[384]{0:T(512)}, u32[]{:S(2)}) copy-start(f32[384]{0:T(512)} %param.8) | copy-start | bytes 4612
  17.0 8.1 %collective-permute-start.1 = (bf16[4,1,32,384]{3,2,0,1:T(8,128)(2,1)S(1)}, bf16[4,1,32,384]{3,2,0,1:T(8,128)(2,1)S(1)}, u32[]{:S(2)}, u32[]{:S(2)}) collective-permute-start(bf16[4,1,32,384]{3,2,0,1:T(8,128)(2,1)S(1)} %pad_maximum_fusion), channel_id=1, source_target_pairs={{0,1},{1,2},{2,3},{3,4},{4,5},{5,6},{6,7},{7,8},{8,9},{9,10},{10,1... | collective-permute-start | bytes 294920 | tf_op jit(solution)/shard_map/ppermute | solution.py:20
  21.7 5.9 %collective-permute-start.2 = (bf16[4,1,32,384]{3,2,0,1:T(8,128)(2,1)S(1)}, bf16[4,1,32,384]{3,2,0,1:T(8,128)(2,1)S(1)}, u32[]{:S(2)}, u32[]{:S(2)}) collective-permute-start(bf16[4,1,32,384]{3,2,0,1:T(8,128)(2,1)S(1)} %pad_maximum_fusion), channel_id=1, source_target_pairs={{1,0},{2,1},{3,2},{4,3},{5,4},{6,5},{7,6},{8,7},{9,8},{10,9},{11,1... | collective-permute-start | bytes 294920 | tf_op jit(solution)/shard_map/ppermute | solution.py:21
  28.4 100.2 %copy-start.3 = (f32[384]{0:T(512)S(1)}, f32[384]{0:T(512)}, u32[]{:S(2)}) copy-start(f32[384]{0:T(512)} %param.10) | copy-start | bytes 4612
  128.6 4.7 %copy-start.1 = (f32[384]{0:T(512)S(1)}, f32[384]{0:T(512)}, u32[]{:S(2)}) copy-start(f32[384]{0:T(512)} %param.11) | copy-start | bytes 4612
  133.4 4.3 %collective-permute-start.3 = (bf16[2,1,32,384]{3,2,0,1:T(8,128)(2,1)S(1)}, bf16[2,1,32,384]{3,2,0,1:T(8,128)(2,1)S(1)}, u32[]{:S(2)}, u32[]{:S(2)}) collective-permute-start(bf16[2,1,32,384]{3,2,0,1:T(8,128)(2,1)S(1)} %fusion.49), channel_id=1, source_target_pairs={{0,64},{64,128},{128,192},{192,256},{256,320},{320,384},{384,448},... | collective-permute-start | bytes 147464 | tf_op jit(solution)/shard_map/ppermute | solution.py:10
  137.7 83.0 %collective-permute-start.4 = (bf16[4,1,32,384]{3,2,0,1:T(8,128)(2,1)S(1)}, bf16[4,1,32,384]{3,2,0,1:T(8,128)(2,1)S(1)}, u32[]{:S(2)}, u32[]{:S(2)}) collective-permute-start(bf16[4,1,32,384]{3,2,0,1:T(8,128)(2,1)S(1)} %pad_maximum_fusion.1), channel_id=1, source_target_pairs={{0,1},{1,2},{2,3},{3,4},{4,5},{5,6},{6,7},{7,8},{8,9},{9,10},{10,1... | collective-permute-start | bytes 294920 | tf_op jit(solution)/shard_map/ppermute | solution.py:20
  140.5 80.2 %collective-permute-start.5 = (bf16[4,1,32,384]{3,2,0,1:T(8,128)(2,1)S(1)}, bf16[4,1,32,384]{3,2,0,1:T(8,128)(2,1)S(1)}, u32[]{:S(2)}, u32[]{:S(2)}) collective-permute-start(bf16[4,1,32,384]{3,2,0,1:T(8,128)(2,1)S(1)} %pad_maximum_fusion.1), channel_id=1, source_target_pairs={{1,0},{2,1},{3,2},{4,3},{5,4},{6,5},{7,6},{8,7},{9,8},{10,9},{11,1... | collective-permute-start | bytes 294920 | tf_op jit(solution)/shard_map/ppermute | solution.py:21
  220.9 0.7 copy-start.4
Sparse Core Ops, SparseCore 0:
  10.6 98.3 all-gather.2
  112.3 88.9 all-gather.4
where the time goes:
time: 235 us; the launch traced here: 234 us
  waiting for transfers between devices  144 us (61%)
  local copies, waits for them, and re-layouts  43.3 us (18%)
  starting transfers between devices  19.9 us (8%)
  between operations  13.8 us (6%)
  matrix products  9.93 us (4%)
  other arithmetic  2.45 us (1%)
    all_gather x2, waiting for transfers between devices, conv_layer(): whole_kernel = lax.all_gather(weight, 'rows', axis=4, tiled=True)  139 us
    all_gather x2, local copies, waits for them, and re-layouts, conv_layer(): whole_kernel = lax.all_gather(weight, 'rows', axis=4, tiled=True)  39.1 us
    dot_general x2, matrix products, convolve(): jnp.dot(stacked.reshape(-1, depth), kernel, preferred_element_type=jnp.fl...  9.93 us
    ppermute x2, starting transfers between devices, with_halo(): before = lax.ppermute(last, axis, up)  7.46 us
    ppermute x2, starting transfers between devices, from_behind(): return lax.ppermute(value, axis, pairs)  7.14 us
    ppermute x2, starting transfers between devices, with_halo(): after = lax.ppermute(initial, axis, down)  5.3 us
  transfers between devices with their start and end apart: 8, of which 5 were waited for; matrix products, arithmetic and copies ran while one was open for 21% of the time, Pallas kernels for 0%

commit v1 on v0

v1 whole, which is shorter than its diff:
```python
import jax
import jax.numpy as jnp
from jax import lax
from jax.experimental import pallas as pl
from jax.experimental.pallas import tpu as pltpu
from jax.sharding import Mesh
from jax.sharding import PartitionSpec as P

CHANNELS = 384
BLOCK = 48
SLOT = 224
LANES = 512
VMEM = 48 * 1024 * 1024
F32 = jnp.float32
BF16 = jnp.bfloat16


def call(kernel, out_shape, scratch=(), smem=0, n=0):
    specs = [pl.BlockSpec(memory_space=pltpu.SMEM)] * smem
    specs += [pl.BlockSpec(memory_space=pltpu.VMEM)] * (n - smem)
    multiple = isinstance(out_shape, (list, tuple))
    vmem = pl.BlockSpec(memory_space=pltpu.VMEM)
    return pl.pallas_call(
        kernel,
        out_shape=out_shape,
        in_specs=specs,
        out_specs=[vmem] * len(out_shape) if multiple else vmem,
        scratch_shapes=list(scratch),
        compiler_params=pltpu.CompilerParams(vmem_limit_bytes=VMEM),
    )


def shape(dims, dtype):
    return jax.ShapeDtypeStruct(dims, dtype)


def silu(v):
    return v / (1.0 + jnp.exp(-v))


def prepare_kernel(latent, gain, weight_one, weight_two, hidden, slot_one, slot_two, rows):
    values = latent[...].astype(F32)
    mean = jnp.mean(values * values, axis=1, keepdims=True)
    result = silu(values * lax.rsqrt(mean + 1e-6) * gain[...]).astype(BF16)
    for z in range(8):
        hidden[z] = result
    for weight, slot in ((weight_one, slot_one), (weight_two, slot_two)):
        rows[...] = jnp.zeros_like(rows)
        for tap in range(27):
            rows[8 * tap : 8 * tap + 6, :] = weight[tap].astype(F32)
        slot[...] = rows[...].astype(BF16)


def place_weights(ids, own, ahead, behind, across, swapped, whole):
    x, c = ids[1], ids[2]
    for shift, piece in ((0, own), (1, ahead), (2, across), (3, behind)):
        position = lax.rem(x + 4 - shift, 4) * 2
        whole[position + c] = piece[...]
        whole[position + 1 - c] = swapped[shift]


def taps(ids, products, keep, partner, pair):
    c = ids[2]
    column = lax.rem(lax.broadcasted_iota(jnp.int32, (8, 2 * LANES), 1), 32)
    half = LANES // 2
    for two in range(4):
        parts = ([], [], [])
        for slot in (2 * two, 2 * two + 1):
            for j in range(3):
                sums = []
                for l in range(3):
                    k = [
                        products[pl.ds(slot * SLOT + 8 * (9 * i + 3 * j + l), 8), :]
                        for i in range(3)
                    ]
                    sums.append(
                        jnp.concatenate(
                            [
                                k[2][:, :half],
                                k[2][:, half:] + k[1][:, :half],
                                k[1][:, half:] + k[0][:, :half],
                                k[0][:, half:],
                            ],
                            axis=1,
                        )
                    )
                left = jnp.where(column == 0, 0.0, pltpu.roll(sums[0], 1, 1))
                right = jnp.where(column == 31, 0.0, pltpu.roll(sums[2], 2 * LANES - 1, 1))
                parts[j].append(sums[1] + left + right)
        below, level, above = [jnp.concatenate(p, axis=0) for p in parts]
        at = pl.ds(16 * two, 16)
        keep[at, :] = level
        partner[at, :] = jnp.where(c == 0, below, above).astype(BF16)
        pair[at, :] = jnp.where(c == 0, above, below).astype(BF16)


def conv_one_kernel(ids, gathered, own, ahead, behind, across, swapped, keep, partner, pair, whole, field, products):
    place_weights(ids, own, ahead, behind, across, swapped, whole)
    for z in range(8):
        for f in range(2):
            field[pl.ds(256 * f + 32 * z, 32), :] = gathered[z, pl.ds(32 * f, 32), :]
    products[...] = lax.dot_general(
        whole[...].reshape(8 * SLOT, CHANNELS),
        field[...],
        (((1,), (1,)), ((), ())),
        preferred_element_type=F32,
    )
    taps(ids, products, keep, partner, pair)


def conv_two_kernel(ids, gathered, gain, own, ahead, behind, across, swapped, keep, partner, pair, whole, products):
    place_weights(ids, own, ahead, behind, across, swapped, whole)
    values = gathered[...].reshape(CHANNELS, LANES).astype(F32)
    mean = jnp.mean(values * values, axis=0, keepdims=True)
    square = (CHANNELS, CHANNELS)
    same = lax.broadcasted_iota(jnp.int32, square, 0) == lax.broadcasted_iota(jnp.int32, square, 1)
    scale = jnp.sum(jnp.where(same, gain[...], 0.0), axis=1, keepdims=True)
    hidden = silu(values * lax.rsqrt(mean + 1e-6) * scale).astype(BF16)
    products[...] = jnp.dot(
        whole[...].reshape(8 * SLOT, CHANNELS), hidden, preferred_element_type=F32
    )
    taps(ids, products, keep, partner, pair)


def rows_kernel(ids, keep, partner, pair, own, later):
    position = 2 * ids[1] + ids[2]
    got = pair[...].astype(F32)
    place = lax.rem(lax.broadcasted_iota(jnp.int32, got.shape, 1) // 32, 8)
    down = jnp.where(place == 0, 0.0, pltpu.roll(got, 32, 1))
    up = jnp.where(place == 7, 0.0, pltpu.roll(got, 2 * LANES - 32, 1))
    got = jnp.where(position == 0, down, jnp.where(position == 7, up, got))
    total = keep[...] + partner[...].astype(F32) + got
    own[...] = total[:, :LANES]
    later[...] = total[:, LANES:].astype(BF16)


def block_values(ids, own, earlier, bias):
    row = lax.broadcasted_iota(jnp.int32, (64, CHANNELS), 0)
    channel = lax.broadcasted_iota(jnp.int32, (64, CHANNELS), 1)
    wanted = BLOCK * ids[0] + 6 * (row // 8) + lax.rem(row, 8)
    chosen = (channel == wanted) & (lax.rem(row, 8) < 6)
    column = jnp.sum(jnp.where(chosen, bias[...], 0.0), axis=1, keepdims=True)
    total = (own[...] + earlier[...].astype(F32) + column).astype(BF16)
    to = lax.broadcasted_iota(jnp.int32, (BLOCK, 64), 0)
    frm = lax.broadcasted_iota(jnp.int32, (BLOCK, 64), 1)
    pick = (frm == 8 * (to // 6) + lax.rem(to, 6)).astype(BF16)
    return jnp.dot(pick, total, preferred_element_type=F32).astype(BF16)


def middle_kernel(ids, own, earlier, bias, middle):
    result = block_values(ids, own, earlier, bias)
    for z in range(8):
        middle[z] = result


def spread_kernel(ids, own, earlier, bias, pieces):
    result = block_values(ids, own, earlier, bias)
    for z in range(8):
        frames = [result[:, 256 * f + 32 * z : 256 * f + 32 * z + 32] for f in range(2)]
        pieces[z] = jnp.concatenate(frames, axis=1)


def finish_kernel(latent, gathered, out):
    square = (CHANNELS, CHANNELS)
    same = lax.broadcasted_iota(jnp.int32, square, 0) == lax.broadcasted_iota(jnp.int32, square, 1)
    conv = lax.dot_general(
        gathered[...].reshape(CHANNELS, 64),
        same.astype(BF16),
        (((0,), (0,)), ((), ())),
        preferred_element_type=F32,
    )
    out[...] = (latent[...].astype(F32) + conv).astype(BF16)


def gather_weights(slot):
    shifted = [
        lax.ppermute(slot, "x", [(i, (i + by) % 4) for i in range(4)]) for by in (1, 2, 3)
    ]
    own = jnp.stack([slot] + shifted)
    swapped = lax.ppermute(own, "core", [(0, 1), (1, 0)])
    return slot, shifted[0], shifted[2], shifted[1], swapped


def exchange(ids, keep, partner, pair):
    partner = lax.ppermute(partner, "core", [(0, 1), (1, 0)])
    swaps = []
    for x in range(4):
        swaps += [(2 * x + 1, 2 * ((x + 1) % 4)), (2 * ((x + 1) % 4), 2 * x + 1)]
    pair = lax.ppermute(pair, ("x", "core"), swaps)
    own, later = call(
        rows_kernel,
        [shape((64, LANES), F32), shape((64, LANES), BF16)],
        smem=1,
        n=4,
    )(ids, keep, partner, pair)
    earlier = lax.ppermute(later, "t", [(i, i + 1) for i in range(7)])
    return own, earlier


def per_device(latent, gain_one, weight_one, bias_one, gain_two, weight_two, bias_two):
    ids = jnp.stack([lax.axis_index(a) for a in ("z", "x", "core")]).astype(jnp.int32)
    latent = latent.reshape(64, CHANNELS)
    weight_one, weight_two = [
        jnp.transpose(w, (0, 1, 2, 4, 3)).reshape(27, 6, CHANNELS)
        for w in (weight_one, weight_two)
    ]
    gain_one, bias_one, gain_two, bias_two = [
        v.reshape(1, CHANNELS) for v in (gain_one, bias_one, gain_two, bias_two)
    ]
    slot = shape((SLOT, CHANNELS), BF16)
    hidden, slot_one, slot_two = call(
        prepare_kernel,
        [shape((8, 64, CHANNELS), BF16), slot, slot],
        [pltpu.VMEM((SLOT, CHANNELS), F32)],
        n=4,
    )(latent, gain_one, weight_one, weight_two)
    weights_one = gather_weights(slot_one)
    hidden = lax.all_to_all(hidden, "z", 0, 0)
    weights_two = gather_weights(slot_two)

    sums = [
        shape((64, 2 * LANES), F32),
        shape((64, 2 * LANES), BF16),
        shape((64, 2 * LANES), BF16),
    ]
    whole = pltpu.VMEM((8, SLOT, CHANNELS), BF16)
    products = pltpu.VMEM((8 * SLOT, LANES), F32)
    sums_one = call(
        conv_one_kernel,
        sums,
        [whole, pltpu.VMEM((LANES, CHANNELS), BF16), products],
        smem=1,
        n=7,
    )(ids, hidden, *weights_one)
    own, earlier = exchange(ids, *sums_one)
    middle = call(middle_kernel, shape((8, BLOCK, LANES), BF16), smem=1, n=4)(
        ids, own, earlier, bias_one
    )
    middle = lax.all_to_all(middle, "z", 0, 0)
    sums_two = call(conv_two_kernel, sums, [whole, products], smem=1, n=8)(
        ids, middle, gain_two, *weights_two
    )
    own, earlier = exchange(ids, *sums_two)
    pieces = call(spread_kernel, shape((8, BLOCK, 64), BF16), smem=1, n=4)(
        ids, own, earlier, bias_two
    )
    pieces = lax.all_to_all(pieces, "z", 0, 0)
    out = call(finish_kernel, shape((64, CHANNELS), BF16), n=2)(latent, pieces)
    return out.reshape(2, 1, 32, CHANNELS)


def solution(mesh):
    mesh = Mesh(mesh.devices.reshape(8, 8, 4, 2), ("t", "z", "x", "core"))
    rows = ("z", "x", "core")
    kernel = P(None, None, None, None, rows)
    field = P("t", rows, None, None)
    return jax.shard_map(
        per_device,
        mesh=mesh,
        in_specs=(field, P(), kernel, P(), P(), kernel, P()),
        out_specs=field,
        check_vma=False,
    )
```

time: 235 us -> 113 us (0.48)
  the two profiles are of different devices: /device:TPU:1 before, /device:TPU:24 now
where the time goes in v1:
time: 113 us; the launch traced here: 112 us
  starting transfers between devices  58.4 us (52%)
  waiting for transfers between devices  28.4 us (25%)
  blocking collectives  10.6 us (9%)
  Pallas kernels  9.54 us (8%)
  local copies, waits for them, and re-layouts  4.25 us (4%)
    ppermute x6, starting transfers between devices, gather_weights(): lax.ppermute(slot, 'x', [(i, (i + by) % 4) for i in range(4)])  20.3 us
    all_to_all x1, waiting for transfers between devices, per_device(): middle = lax.all_to_all(middle, 'z', 0, 0)  15.3 us
    all_to_all x1, blocking collectives, per_device(): pieces = lax.all_to_all(pieces, 'z', 0, 0)  10.6 us
    all_to_all x1, starting transfers between devices, per_device(): hidden = lax.all_to_all(hidden, 'z', 0, 0)  10.3 us
    ppermute x2, waiting for transfers between devices, exchange(): pair = lax.ppermute(pair, ('x', 'core'), swaps)  7.96 us
    ppermute x2, starting transfers between devices, exchange(): earlier = lax.ppermute(later, 't', [(i, i + 1) for i in range(7)])  7.88 us
    ppermute x2, starting transfers between devices, exchange(): pair = lax.ppermute(pair, ('x', 'core'), swaps)  6.97 us
    all_to_all x1, starting transfers between devices, per_device(): middle = lax.all_to_all(middle, 'z', 0, 0)  5.22 us
  transfers between devices with their start and end apart: 16, of which 5 were waited for; matrix products, arithmetic and copies ran while one was open for 0% of the time, Pallas kernels for 4%

profile of v1, /device:TPU:24, one launch (start us, length us, event | category | flops | bytes accessed | tf_op | source)
XLA Modules:
  0.0 111.8 jit_solution(2664140035605394074)
XLA Ops:
  0.7 0.8 copy-done
  1.5 0.9 copy-done.2
  2.4 0.9 copy-done.3
  3.3 0.9 shard_map.73
  4.3 4.9 %collective-permute-start.2 = (bf16[224,384]{1,0:T(8,128)(2,1)S(1)}, bf16[224,384]{1,0:T(8,128)(2,1)S(1)}, u32[]{:S(2)}, u32[]{:S(2)}) collective-permute-start(bf16[224,384]{1,0:T(8,128)(2,1)S(1)} %get-tuple-element.19.own), channel_id=1, source_target_pairs={{0,4},{2,6},{4,0},{6,2},{1,5},{3,7},{5,1},{7,3},{8,12},{10,14},{12... | collective-permute-start | bytes 516104 | tf_op jit(solution)/shard_map/ppermute | solution.py:177
  9.2 3.0 %collective-permute-start.1 = (bf16[224,384]{1,0:T(8,128)(2,1)S(1)}, bf16[224,384]{1,0:T(8,128)(2,1)S(1)}, u32[]{:S(2)}, u32[]{:S(2)}) collective-permute-start(bf16[224,384]{1,0:T(8,128)(2,1)S(1)} %get-tuple-element.19.own), channel_id=1, source_target_pairs={{0,6},{2,0},{4,2},{6,4},{1,7},{3,1},{5,3},{7,5},{8,14},{10,8},{12,... | collective-permute-start | bytes 516104 | tf_op jit(solution)/shard_map/ppermute | solution.py:177
  12.2 2.8 %collective-permute-start = (bf16[224,384]{1,0:T(8,128)(2,1)S(1)}, bf16[224,384]{1,0:T(8,128)(2,1)S(1)}, u32[]{:S(2)}, u32[]{:S(2)}) collective-permute-start(bf16[224,384]{1,0:T(8,128)(2,1)S(1)} %get-tuple-element.19.own), channel_id=1, source_target_pairs={{0,2},{2,4},{4,6},{6,0},{1,3},{3,5},{5,7},{7,1},{8,10},{10,12},{12... | collective-permute-start | bytes 516104 | tf_op jit(solution)/shard_map/ppermute | solution.py:177
  15.0 10.3 %all-to-all-start = ((bf16[8,64,384]{2,1,0:T(8,128)(2,1)}), bf16[8,64,384]{2,1,0:T(8,128)(2,1)S(1)}, u32[]{:S(2)}, u32[]{:S(2)}) async-start(bf16[8,64,384]{2,1,0:T(8,128)(2,1)} %get-tuple-element.18), calls=%async_computation | async-start | bytes 786432 | tf_op jit(solution)/shard_map/all_to_all | solution.py:218
  25.5 1.9 %collective-permute-start.3 = (bf16[4,224,384]{2,1,0:T(8,128)(2,1)S(1)}, bf16[4,224,384]{2,1,0:T(8,128)(2,1)S(1)}, u32[]{:S(2)}, u32[]{:S(2)}) collective-permute-start(bf16[4,224,384]{2,1,0:T(8,128)(2,1)S(1)} %pad_maximum_fusion), channel_id=1, source_target_pairs={{0,1},{1,0},{2,3},{3,2},{4,5},{5,4},{6,7},{7,6},{8,9},{9,8},{10,11... | collective-permute-start | bytes 2064392 | tf_op jit(solution)/shard_map/ppermute | solution.py:180
  27.4 2.5 %collective-permute-start.7 = (bf16[224,384]{1,0:T(8,128)(2,1)S(1)}, bf16[224,384]{1,0:T(8,128)(2,1)S(1)}, u32[]{:S(2)}, u32[]{:S(2)}) collective-permute-start(bf16[224,384]{1,0:T(8,128)(2,1)S(1)} %get-tuple-element.25.own), channel_id=1, source_target_pairs={{0,2},{2,4},{4,6},{6,0},{1,3},{3,5},{5,7},{7,1},{8,10},{10,12},{12... | collective-permute-start | bytes 516104 | tf_op jit(solution)/shard_map/ppermute | solution.py:177
  30.0 5.1 %collective-permute-start.9 = (bf16[224,384]{1,0:T(8,128)(2,1)S(1)}, bf16[224,384]{1,0:T(8,128)(2,1)S(1)}, u32[]{:S(2)}, u32[]{:S(2)}) collective-permute-start(bf16[224,384]{1,0:T(8,128)(2,1)S(1)} %get-tuple-element.25.own), channel_id=1, source_target_pairs={{0,4},{2,6},{4,0},{6,2},{1,5},{3,7},{5,1},{7,3},{8,12},{10,14},{12... | collective-permute-start | bytes 516104 | tf_op jit(solution)/shard_map/ppermute | solution.py:177
  35.1 1.9 %collective-permute-start.8 = (bf16[224,384]{1,0:T(8,128)(2,1)S(1)}, bf16[224,384]{1,0:T(8,128)(2,1)S(1)}, u32[]{:S(2)}, u32[]{:S(2)}) collective-permute-start(bf16[224,384]{1,0:T(8,128)(2,1)S(1)} %get-tuple-element.25.own), channel_id=1, source_target_pairs={{0,6},{2,0},{4,2},{6,4},{1,7},{3,1},{5,3},{7,5},{8,14},{10,8},{12,... | collective-permute-start | bytes 516104 | tf_op jit(solution)/shard_map/ppermute | solution.py:177
  37.1 2.1 %all-to-all-done.gathered = bf16[8,64,384]{2,1,0:T(8,128)(2,1)S(1)} async-done(((bf16[8,64,384]{2,1,0:T(8,128)(2,1)}), bf16[8,64,384]{2,1,0:T(8,128)(2,1)S(1)}, u32[]{:S(2)}, u32[]{:S(2)}) %all-to-all-start) | async-done | bytes 393248 | tf_op jit(solution)/shard_map/all_to_all | solution.py:218
  39.2 1.8 %shard_map.74 = (f32[64,1024]{1,0:T(8,128)S(1)}, bf16[64,1024]{1,0:T(8,128)(2,1)S(1)}, bf16[64,1024]{1,0:T(8,128)(2,1)S(1)}) custom-call(s32[3]{0:T(128)S(1)} %pad_add_fusion.ids, bf16[8,64,384]{2,1,0:T(8,128)(2,1)S(1)} %all-to-all-done.gathered, bf16[224,384]{1,0:T(8,128)(2,1)S(1)} %get-tuple-element.19.own, ...), custom_call_target="tpu_custom_call" | custom-call | tf_op jit(solution)/shard_map/pallas_call | solution.py:228
  41.1 1.9 %collective-permute-start.4 = (bf16[64,1024]{1,0:T(8,128)(2,1)S(1)}, bf16[64,1024]{1,0:T(8,128)(2,1)S(1)}, u32[]{:S(2)}, u32[]{:S(2)}) collective-permute-start(bf16[64,1024]{1,0:T(8,128)(2,1)S(1)} %get-tuple-element.21), channel_id=1, source_target_pairs={{0,1},{1,0},{2,3},{3,2},{4,5},{5,4},{6,7},{7,6},{8,9},{9,8},{10,11... | collective-permute-start | bytes 393224 | tf_op jit(solution)/shard_map/ppermute | solution.py:185
  43.0 4.4 %collective-permute-start.5 = (bf16[64,1024]{1,0:T(8,128)(2,1)S(1)}, bf16[64,1024]{1,0:T(8,128)(2,1)S(1)}, u32[]{:S(2)}, u32[]{:S(2)}) collective-permute-start(bf16[64,1024]{1,0:T(8,128)(2,1)S(1)} %get-tuple-element.22), channel_id=1, source_target_pairs={{1,2},{2,1},{3,4},{4,3},{5,6},{6,5},{7,0},{0,7},{9,10},{10,9},{11,... | collective-permute-start | bytes 393224 | tf_op jit(solution)/shard_map/ppermute | solution.py:189
  47.4 3.1 %collective-permute-done.5.pair = bf16[64,1024]{1,0:T(8,128)(2,1)S(1)} collective-permute-done((bf16[64,1024]{1,0:T(8,128)(2,1)S(1)}, bf16[64,1024]{1,0:T(8,128)(2,1)S(1)}, u32[]{:S(2)}, u32[]{:S(2)}) %collective-permute-start.5) | collective-permute-done | bytes 131104 | tf_op jit(solution)/shard_map/ppermute | solution.py:189
  50.5 0.7 shard_map.75
  51.2 4.7 %collective-permute-start.6 = (bf16[64,512]{1,0:T(8,128)(2,1)S(1)}, bf16[64,512]{1,0:T(8,128)(2,1)S(1)}, u32[]{:S(2)}, u32[]{:S(2)}) collective-permute-start(bf16[64,512]{1,0:T(8,128)(2,1)S(1)} %get-tuple-element.24), channel_id=1, source_target_pairs={{0,64},{64,128},{128,192},{192,256},{256,320},{320,384},{384,448},... | collective-permute-start | bytes 196616 | tf_op jit(solution)/shard_map/ppermute | solution.py:196
  56.1 1.9 %collective-permute-start.10 = (bf16[4,224,384]{2,1,0:T(8,128)(2,1)S(1)}, bf16[4,224,384]{2,1,0:T(8,128)(2,1)S(1)}, u32[]{:S(2)}, u32[]{:S(2)}) collective-permute-start(bf16[4,224,384]{2,1,0:T(8,128)(2,1)S(1)} %pad_maximum_fusion.1), channel_id=1, source_target_pairs={{0,1},{1,0},{2,3},{3,2},{4,5},{5,4},{6,7},{7,6},{8,9},{9,8},{10,11... | collective-permute-start | bytes 2064392 | tf_op jit(solution)/shard_map/ppermute | solution.py:180
  58.0 1.5 %shard_map.76 = bf16[8,48,512]{2,1,0:T(8,128)(2,1)} custom-call(s32[3]{0:T(128)S(1)} %pad_add_fusion.ids, f32[64,512]{1,0:T(8,128)S(1)} %get-tuple-element.23.own, bf16[64,512]{1,0:T(8,128)(2,1)S(1)} %collective-permute-done.6.earlier, f32[1,384]{1,0:T(1,128)S(1)} %reshape.28.bias), custom_call_target="tpu_custom_call" | custom-call | tf_op jit(solution)/shard_map/pallas_call | solution.py:236
  59.6 5.2 %all-to-all-start.1 = ((bf16[8,48,512]{2,1,0:T(8,128)(2,1)}), bf16[8,48,512]{2,1,0:T(8,128)(2,1)S(1)}, u32[]{:S(2)}, u32[]{:S(2)}) async-start(bf16[8,48,512]{2,1,0:T(8,128)(2,1)} %shard_map.76), calls=%async_computation.1 | async-start | bytes 786432 | tf_op jit(solution)/shard_map/all_to_all | solution.py:239
  64.8 15.3 %all-to-all-done.1.gathered = bf16[8,48,512]{2,1,0:T(8,128)(2,1)S(1)} async-done(((bf16[8,48,512]{2,1,0:T(8,128)(2,1)}), bf16[8,48,512]{2,1,0:T(8,128)(2,1)S(1)}, u32[]{:S(2)}, u32[]{:S(2)}) %all-to-all-start.1) | async-done | bytes 393248 | tf_op jit(solution)/shard_map/all_to_all | solution.py:239
  80.1 2.1 %shard_map.77 = (f32[64,1024]{1,0:T(8,128)S(1)}, bf16[64,1024]{1,0:T(8,128)(2,1)S(1)}, bf16[64,1024]{1,0:T(8,128)(2,1)S(1)}) custom-call(s32[3]{0:T(128)S(1)} %pad_add_fusion.ids, bf16[8,48,512]{2,1,0:T(8,128)(2,1)S(1)} %all-to-all-done.1.gathered, f32[1,384]{1,0:T(1,128)S(1)} %reshape.29.gain, bf16[224,384]{1,0:T(8,128)(2,1)S(1)} %get-tuple-element.25.own, ...), custom_call_target="tpu_custom_call" | custom-call | tf_op jit(solution)/shard_map/pallas_call | solution.py:240
  82.2 2.0 %collective-permute-start.11 = (bf16[64,1024]{1,0:T(8,128)(2,1)S(1)}, bf16[64,1024]{1,0:T(8,128)(2,1)S(1)}, u32[]{:S(2)}, u32[]{:S(2)}) collective-permute-start(bf16[64,1024]{1,0:T(8,128)(2,1)S(1)} %get-tuple-element.27), channel_id=1, source_target_pairs={{0,1},{1,0},{2,3},{3,2},{4,5},{5,4},{6,7},{7,6},{8,9},{9,8},{10,11... | collective-permute-start | bytes 393224 | tf_op jit(solution)/shard_map/ppermute | solution.py:185
  84.2 2.6 %collective-permute-start.12 = (bf16[64,1024]{1,0:T(8,128)(2,1)S(1)}, bf16[64,1024]{1,0:T(8,128)(2,1)S(1)}, u32[]{:S(2)}, u32[]{:S(2)}) collective-permute-start(bf16[64,1024]{1,0:T(8,128)(2,1)S(1)} %get-tuple-element.28), channel_id=1, source_target_pairs={{1,2},{2,1},{3,4},{4,3},{5,6},{6,5},{7,0},{0,7},{9,10},{10,9},{11,... | collective-permute-start | bytes 393224 | tf_op jit(solution)/shard_map/ppermute | solution.py:189
  86.8 4.9 %collective-permute-done.12.pair = bf16[64,1024]{1,0:T(8,128)(2,1)S(1)} collective-permute-done((bf16[64,1024]{1,0:T(8,128)(2,1)S(1)}, bf16[64,1024]{1,0:T(8,128)(2,1)S(1)}, u32[]{:S(2)}, u32[]{:S(2)}) %collective-permute-start.12) | collective-permute-done | bytes 131104 | tf_op jit(solution)/shard_map/ppermute | solution.py:189
  92.4 3.2 %collective-permute-start.13 = (bf16[64,512]{1,0:T(8,128)(2,1)S(1)}, bf16[64,512]{1,0:T(8,128)(2,1)S(1)}, u32[]{:S(2)}, u32[]{:S(2)}) collective-permute-start(bf16[64,512]{1,0:T(8,128)(2,1)S(1)} %get-tuple-element.30), channel_id=1, source_target_pairs={{0,64},{64,128},{128,192},{192,256},{256,320},{320,384},{384,448},... | collective-permute-start | bytes 196616 | tf_op jit(solution)/shard_map/ppermute | solution.py:196
  95.6 3.0 %collective-permute-done.13.earlier = bf16[64,512]{1,0:T(8,128)(2,1)S(1)} collective-permute-done((bf16[64,512]{1,0:T(8,128)(2,1)S(1)}, bf16[64,512]{1,0:T(8,128)(2,1)S(1)}, u32[]{:S(2)}, u32[]{:S(2)}) %collective-permute-start.13) | collective-permute-done | bytes 65568 | tf_op jit(solution)/shard_map/ppermute | solution.py:196
  98.6 0.9 shard_map.79
  99.6 10.6 %all_to_all.15 = bf16[8,2,1536]{2,1,0:T(2,128)(2,1)S(1)} all-to-all(bf16[8,2,1536]{2,1,0:T(2,128)(2,1)S(1)} %reshape.32), channel_id=1, replica_groups=mesh['t'=8,'z'=8,'x'=4,'core'=2] {'z'}, dimensions={0} | all-to-all | bytes 98304 | tf_op jit(solution)/shard_map/all_to_all | solution.py:247
  110.9 0.8 shard_map.80
  (32 shorter events, 2.7 us)
Async XLA Ops:
  0.7 0.8 copy-start
  1.5 0.9 copy-start.2
  2.4 0.9 copy-start.3
  4.3 21.1 %collective-permute-start.2 = (bf16[224,384]{1,0:T(8,128)(2,1)S(1)}, bf16[224,384]{1,0:T(8,128)(2,1)S(1)}, u32[]{:S(2)}, u32[]{:S(2)}) collective-permute-start(bf16[224,384]{1,0:T(8,128)(2,1)S(1)} %get-tuple-element.19.own), channel_id=1, source_target_pairs={{0,4},{2,6},{4,0},{6,2},{1,5},{3,7},{5,1},{7,3},{8,12},{10,14},{12... | collective-permute-start | bytes 516104 | tf_op jit(solution)/shard_map/ppermute | solution.py:177
  9.2 16.2 %collective-permute-start.1 = (bf16[224,384]{1,0:T(8,128)(2,1)S(1)}, bf16[224,384]{1,0:T(8,128)(2,1)S(1)}, u32[]{:S(2)}, u32[]{:S(2)}) collective-permute-start(bf16[224,384]{1,0:T(8,128)(2,1)S(1)} %get-tuple-element.19.own), channel_id=1, source_target_pairs={{0,6},{2,0},{4,2},{6,4},{1,7},{3,1},{5,3},{7,5},{8,14},{10,8},{12,... | collective-permute-start | bytes 516104 | tf_op jit(solution)/shard_map/ppermute | solution.py:177
  12.2 13.1 %collective-permute-start = (bf16[224,384]{1,0:T(8,128)(2,1)S(1)}, bf16[224,384]{1,0:T(8,128)(2,1)S(1)}, u32[]{:S(2)}, u32[]{:S(2)}) collective-permute-start(bf16[224,384]{1,0:T(8,128)(2,1)S(1)} %get-tuple-element.19.own), channel_id=1, source_target_pairs={{0,2},{2,4},{4,6},{6,0},{1,3},{3,5},{5,7},{7,1},{8,10},{10,12},{12... | collective-permute-start | bytes 516104 | tf_op jit(solution)/shard_map/ppermute | solution.py:177
  15.0 24.2 %all-to-all-start = ((bf16[8,64,384]{2,1,0:T(8,128)(2,1)}), bf16[8,64,384]{2,1,0:T(8,128)(2,1)S(1)}, u32[]{:S(2)}, u32[]{:S(2)}) async-start(bf16[8,64,384]{2,1,0:T(8,128)(2,1)} %get-tuple-element.18), calls=%async_computation | async-start | bytes 786432 | tf_op jit(solution)/shard_map/all_to_all | solution.py:218
  25.5 13.7 %collective-permute-start.3 = (bf16[4,224,384]{2,1,0:T(8,128)(2,1)S(1)}, bf16[4,224,384]{2,1,0:T(8,128)(2,1)S(1)}, u32[]{:S(2)}, u32[]{:S(2)}) collective-permute-start(bf16[4,224,384]{2,1,0:T(8,128)(2,1)S(1)} %pad_maximum_fusion), channel_id=1, source_target_pairs={{0,1},{1,0},{2,3},{3,2},{4,5},{5,4},{6,7},{7,6},{8,9},{9,8},{10,11... | collective-permute-start | bytes 2064392 | tf_op jit(solution)/shard_map/ppermute | solution.py:180
  27.4 28.5 %collective-permute-start.7 = (bf16[224,384]{1,0:T(8,128)(2,1)S(1)}, bf16[224,384]{1,0:T(8,128)(2,1)S(1)}, u32[]{:S(2)}, u32[]{:S(2)}) collective-permute-start(bf16[224,384]{1,0:T(8,128)(2,1)S(1)} %get-tuple-element.25.own), channel_id=1, source_target_pairs={{0,2},{2,4},{4,6},{6,0},{1,3},{3,5},{5,7},{7,1},{8,10},{10,12},{12... | collective-permute-start | bytes 516104 | tf_op jit(solution)/shard_map/ppermute | solution.py:177
  30.0 26.0 %collective-permute-start.9 = (bf16[224,384]{1,0:T(8,128)(2,1)S(1)}, bf16[224,384]{1,0:T(8,128)(2,1)S(1)}, u32[]{:S(2)}, u32[]{:S(2)}) collective-permute-start(bf16[224,384]{1,0:T(8,128)(2,1)S(1)} %get-tuple-element.25.own), channel_id=1, source_target_pairs={{0,4},{2,6},{4,0},{6,2},{1,5},{3,7},{5,1},{7,3},{8,12},{10,14},{12... | collective-permute-start | bytes 516104 | tf_op jit(solution)/shard_map/ppermute | solution.py:177
  35.1 20.9 %collective-permute-start.8 = (bf16[224,384]{1,0:T(8,128)(2,1)S(1)}, bf16[224,384]{1,0:T(8,128)(2,1)S(1)}, u32[]{:S(2)}, u32[]{:S(2)}) collective-permute-start(bf16[224,384]{1,0:T(8,128)(2,1)S(1)} %get-tuple-element.25.own), channel_id=1, source_target_pairs={{0,6},{2,0},{4,2},{6,4},{1,7},{3,1},{5,3},{7,5},{8,14},{10,8},{12,... | collective-permute-start | bytes 516104 | tf_op jit(solution)/shard_map/ppermute | solution.py:177
  41.1 6.3 %copy-start.4 = (f32[384]{0:T(512)S(1)}, f32[384]{0:T(512)}, u32[]{:S(2)}) copy-start(f32[384]{0:T(512)} %param.10) | copy-start | bytes 4612
  41.1 6.3 %collective-permute-start.4 = (bf16[64,1024]{1,0:T(8,128)(2,1)S(1)}, bf16[64,1024]{1,0:T(8,128)(2,1)S(1)}, u32[]{:S(2)}, u32[]{:S(2)}) collective-permute-start(bf16[64,1024]{1,0:T(8,128)(2,1)S(1)} %get-tuple-element.21), channel_id=1, source_target_pairs={{0,1},{1,0},{2,3},{3,2},{4,5},{5,4},{6,7},{7,6},{8,9},{9,8},{10,11... | collective-permute-start | bytes 393224 | tf_op jit(solution)/shard_map/ppermute | solution.py:185
  43.0 7.5 %collective-permute-start.5 = (bf16[64,1024]{1,0:T(8,128)(2,1)S(1)}, bf16[64,1024]{1,0:T(8,128)(2,1)S(1)}, u32[]{:S(2)}, u32[]{:S(2)}) collective-permute-start(bf16[64,1024]{1,0:T(8,128)(2,1)S(1)} %get-tuple-element.22), channel_id=1, source_target_pairs={{1,2},{2,1},{3,4},{4,3},{5,6},{6,5},{7,0},{0,7},{9,10},{10,9},{11,... | collective-permute-start | bytes 393224 | tf_op jit(solution)/shard_map/ppermute | solution.py:189
  51.2 6.8 %collective-permute-start.6 = (bf16[64,512]{1,0:T(8,128)(2,1)S(1)}, bf16[64,512]{1,0:T(8,128)(2,1)S(1)}, u32[]{:S(2)}, u32[]{:S(2)}) collective-permute-start(bf16[64,512]{1,0:T(8,128)(2,1)S(1)} %get-tuple-element.24), channel_id=1, source_target_pairs={{0,64},{64,128},{128,192},{192,256},{256,320},{320,384},{384,448},... | collective-permute-start | bytes 196616 | tf_op jit(solution)/shard_map/ppermute | solution.py:196
  56.1 8.7 %collective-permute-start.10 = (bf16[4,224,384]{2,1,0:T(8,128)(2,1)S(1)}, bf16[4,224,384]{2,1,0:T(8,128)(2,1)S(1)}, u32[]{:S(2)}, u32[]{:S(2)}) collective-permute-start(bf16[4,224,384]{2,1,0:T(8,128)(2,1)S(1)} %pad_maximum_fusion.1), channel_id=1, source_target_pairs={{0,1},{1,0},{2,3},{3,2},{4,5},{5,4},{6,7},{7,6},{8,9},{9,8},{10,11... | collective-permute-start | bytes 2064392 | tf_op jit(solution)/shard_map/ppermute | solution.py:180
  59.6 5.2 %copy-start.5 = (f32[384]{0:T(512)S(1)}, f32[384]{0:T(512)}, u32[]{:S(2)}) copy-start(f32[384]{0:T(512)} %param.11) | copy-start | bytes 4612
  59.6 20.6 %all-to-all-start.1 = ((bf16[8,48,512]{2,1,0:T(8,128)(2,1)}), bf16[8,48,512]{2,1,0:T(8,128)(2,1)S(1)}, u32[]{:S(2)}, u32[]{:S(2)}) async-start(bf16[8,48,512]{2,1,0:T(8,128)(2,1)} %shard_map.76), calls=%async_computation.1 | async-start | bytes 786432 | tf_op jit(solution)/shard_map/all_to_all | solution.py:239
  82.2 4.6 %collective-permute-start.11 = (bf16[64,1024]{1,0:T(8,128)(2,1)S(1)}, bf16[64,1024]{1,0:T(8,128)(2,1)S(1)}, u32[]{:S(2)}, u32[]{:S(2)}) collective-permute-start(bf16[64,1024]{1,0:T(8,128)(2,1)S(1)} %get-tuple-element.27), channel_id=1, source_target_pairs={{0,1},{1,0},{2,3},{3,2},{4,5},{5,4},{6,7},{7,6},{8,9},{9,8},{10,11... | collective-permute-start | bytes 393224 | tf_op jit(solution)/shard_map/ppermute | solution.py:185
  84.2 7.5 %collective-permute-start.12 = (bf16[64,1024]{1,0:T(8,128)(2,1)S(1)}, bf16[64,1024]{1,0:T(8,128)(2,1)S(1)}, u32[]{:S(2)}, u32[]{:S(2)}) collective-permute-start(bf16[64,1024]{1,0:T(8,128)(2,1)S(1)} %get-tuple-element.28), channel_id=1, source_target_pairs={{1,2},{2,1},{3,4},{4,3},{5,6},{6,5},{7,0},{0,7},{9,10},{10,9},{11,... | collective-permute-start | bytes 393224 | tf_op jit(solution)/shard_map/ppermute | solution.py:189
  91.7 3.9 %copy-start.6 = (f32[384]{0:T(512)S(1)}, f32[384]{0:T(512)}, u32[]{:S(2)}) copy-start(f32[384]{0:T(512)} %param.13) | copy-start | bytes 4612
  92.4 6.2 %collective-permute-start.13 = (bf16[64,512]{1,0:T(8,128)(2,1)S(1)}, bf16[64,512]{1,0:T(8,128)(2,1)S(1)}, u32[]{:S(2)}, u32[]{:S(2)}) collective-permute-start(bf16[64,512]{1,0:T(8,128)(2,1)S(1)} %get-tuple-element.30), channel_id=1, source_target_pairs={{0,64},{64,128},{128,192},{192,256},{256,320},{320,384},{384,448},... | collective-permute-start | bytes 196616 | tf_op jit(solution)/shard_map/ppermute | solution.py:196
  110.1 0.8 copy-start.1

commit v2 on v1

v2 whole, which is shorter than its diff:
```python
import functools

import jax
import jax.numpy as jnp
from jax import lax
from jax.experimental import pallas as pl
from jax.experimental.pallas import tpu as pltpu
from jax.sharding import Mesh
from jax.sharding import PartitionSpec as P

CHANNELS = 384
BLOCK = 48
PIECE = 176
SLOT = 80
DEPTH = 3 * CHANNELS
LANES = 512
VMEM = 48 * 1024 * 1024
LONG = 10**11
F32 = jnp.float32
BF16 = jnp.bfloat16


def call(kernel, out_shape, scratch=(), smem=0, anywhere=0, n=0, flops=0):
    specs = [pl.BlockSpec(memory_space=pltpu.SMEM)] * smem
    specs += [pl.BlockSpec(memory_space=pl.ANY)] * anywhere
    specs += [pl.BlockSpec(memory_space=pltpu.VMEM)] * (n - len(specs))
    multiple = isinstance(out_shape, (list, tuple))
    vmem = pl.BlockSpec(memory_space=pltpu.VMEM)
    return pl.pallas_call(
        kernel,
        out_shape=out_shape,
        in_specs=specs,
        out_specs=[vmem] * len(out_shape) if multiple else vmem,
        scratch_shapes=list(scratch),
        compiler_params=pltpu.CompilerParams(vmem_limit_bytes=VMEM),
        cost_estimate=pl.CostEstimate(flops=flops, bytes_accessed=0, transcendentals=0),
    )


def shape(dims, dtype):
    return jax.ShapeDtypeStruct(dims, dtype)


def iota(dims, axis):
    return lax.broadcasted_iota(jnp.int32, dims, axis)


def silu(v):
    return v / (1.0 + jnp.exp(-v))


def norm_kernel(latent, gain, hidden):
    values = latent[...].astype(F32)
    mean = jnp.mean(values * values, axis=1, keepdims=True)
    scale = lax.rsqrt(mean + 1e-6) * gain[...].reshape(1, CHANNELS)
    result = silu(values * scale).astype(BF16)
    for z in range(8):
        hidden[z] = result


def prepare_kernel(after, weight, piece, rows):
    for tap in range(27):
        rows[6 * tap : 6 * tap + 6, :] = weight[tap].astype(F32)
    rows[162:PIECE, :] = jnp.zeros((PIECE - 162, CHANNELS), F32)
    piece[...] = rows[...].astype(BF16)


def place_weights(ids, own, ahead, behind, across, swapped, whole):
    x, c = ids[1], ids[2]
    row = iota((3 * SLOT, PIECE), 0)
    j, a, k = row // SLOT, lax.rem(row, SLOT) // 8, lax.rem(row, 8)
    source = 6 * (9 * (a // 3) + 3 * j + lax.rem(a, 3)) + k
    wanted = (source == iota((3 * SLOT, PIECE), 1)) & (a < 9) & (k < 6)
    spread = wanted.astype(F32).astype(BF16)

    def place(position, value):
        rows = jnp.dot(spread, value, preferred_element_type=F32).astype(BF16)
        at = pl.ds(pl.multiple_of(position * SLOT, 16), SLOT)
        for j in range(3):
            whole[at, pl.ds(CHANNELS * j, CHANNELS)] = rows[SLOT * j : SLOT * j + SLOT]

    for shift, piece in ((0, own), (1, ahead), (2, across), (3, behind)):
        position = lax.rem(x + 4 - shift, 4) * 2
        place(position + c, piece[...])
        place(position + 1 - c, swapped[shift])


def taps(products, own, later):
    column = lax.rem(iota((8, 2 * LANES), 1), 32)
    half = LANES // 2
    for two in range(4):
        rows = []
        for slot in (2 * two, 2 * two + 1):
            sums = []
            for l in range(3):
                k = [products[pl.ds(slot * SLOT + 8 * (3 * i + l), 8), :] for i in range(3)]
                parts = [
                    k[2][:, :half],
                    k[2][:, half:] + k[1][:, :half],
                    k[1][:, half:] + k[0][:, :half],
                    k[0][:, half:],
                ]
                sums.append(jnp.concatenate(parts, axis=1))
            left = jnp.where(column == 0, 0.0, pltpu.roll(sums[0], 1, 1))
            right = jnp.where(column == 31, 0.0, pltpu.roll(sums[2], 2 * LANES - 1, 1))
            rows.append(sums[1] + left + right)
        both = jnp.concatenate(rows, axis=0)
        at = pl.ds(16 * two, 16)
        own[at, :] = both[:, :LANES]
        later[at, :] = both[:, LANES:].astype(BF16)


def conv_one_kernel(ids, level, partner, pair, *rest):
    *pieces, own, later, whole, field, products = rest
    place_weights(ids, *pieces, whole)
    c = ids[2]
    position = 2 * ids[1] + c
    step = jnp.where(position == 0, -1, jnp.where(position == 7, 1, 0))
    for z in range(8):
        other = z + step
        inside = ((other >= 0) & (other < 8)).astype(BF16)
        beyond = pair[jnp.clip(other, 0, 7)] * inside

        def put(j, value):
            for f in range(2):
                at = pl.ds(256 * f + 32 * z, 32)
                field[at, pl.ds(CHANNELS * j, CHANNELS)] = value[32 * f : 32 * f + 32]

        put(1, level[z])

        @pl.when(c == 0)
        def _():
            put(0, beyond)
            put(2, partner[z])

        @pl.when(c == 1)
        def _():
            put(0, partner[z])
            put(2, beyond)

    products[...] = lax.dot_general(
        whole[...], field[...], (((1,), (1,)), ((), ())), preferred_element_type=F32
    )
    taps(products, own, later)


def field_two_kernel(gathered, gain, field):
    values = gathered[...].reshape(CHANNELS, LANES).astype(F32)
    mean = jnp.mean(values * values, axis=0, keepdims=True)
    square = (CHANNELS, CHANNELS)
    same = iota(square, 0) == iota(square, 1)
    gains = jnp.where(same, gain[...].reshape(1, CHANNELS), 0.0)
    scale = jnp.sum(gains, axis=1, keepdims=True)
    field[...] = silu(values * lax.rsqrt(mean + 1e-6) * scale).astype(BF16)


def conv_two_kernel(ids, level, partner, pair, *rest):
    *pieces, own, later, whole, field, products = rest
    place_weights(ids, *pieces, whole)
    c = ids[2]
    position = 2 * ids[1] + c
    field[pl.ds(CHANNELS, CHANNELS), :] = level[...]
    at_pair = pl.ds(pl.multiple_of(2 * CHANNELS * c, CHANNELS), CHANNELS)
    at_partner = pl.ds(pl.multiple_of(2 * CHANNELS * (1 - c), CHANNELS), CHANNELS)
    field[at_partner, :] = partner[...]
    place = lax.rem(iota((CHANNELS, LANES), 1) // 32, 8)

    @pl.when((position > 0) & (position < 7))
    def _():
        field[at_pair, :] = pair[...]

    @pl.when(position == 0)
    def _():
        moved = pltpu.roll(pair[...].astype(F32), 32, 1)
        field[at_pair, :] = jnp.where(place == 0, 0.0, moved).astype(BF16)

    @pl.when(position == 7)
    def _():
        moved = pltpu.roll(pair[...].astype(F32), LANES - 32, 1)
        field[at_pair, :] = jnp.where(place == 7, 0.0, moved).astype(BF16)

    products[...] = jnp.dot(whole[...], field[...], preferred_element_type=F32)
    taps(products, own, later)


def block_values(ids, own, earlier, bias):
    row = iota((64, CHANNELS), 0)
    wanted = BLOCK * ids[0] + 6 * (row // 8) + lax.rem(row, 8)
    chosen = (iota((64, CHANNELS), 1) == wanted) & (lax.rem(row, 8) < 6)
    biases = jnp.where(chosen, bias[...].reshape(1, CHANNELS), 0.0)
    column = jnp.sum(biases, axis=1, keepdims=True)
    total = (own[...] + earlier[...].astype(F32) + column).astype(BF16)
    to, frm = iota((BLOCK, 64), 0), iota((BLOCK, 64), 1)
    pick = (frm == 8 * (to // 6) + lax.rem(to, 6)).astype(BF16)
    return jnp.dot(pick, total, preferred_element_type=F32).astype(BF16)


def middle_kernel(ids, own, earlier, bias, middle):
    result = block_values(ids, own, earlier, bias)
    for z in range(8):
        middle[z] = result


def spread_kernel(ids, own, earlier, bias, latent, pieces, kept):
    result = block_values(ids, own, earlier, bias)
    for z in range(8):
        frames = [result[:, 256 * f + 32 * z : 256 * f + 32 * z + 32] for f in range(2)]
        pieces[z] = jnp.concatenate(frames, axis=1)
    kept[...] = latent[...]


def finish_kernel(latent, gathered, out):
    square = (CHANNELS, CHANNELS)
    same = iota(square, 0) == iota(square, 1)
    conv = lax.dot_general(
        gathered[...].reshape(CHANNELS, 64),
        same.astype(BF16),
        (((0,), (0,)), ((), ())),
        preferred_element_type=F32,
    )
    out[...] = (latent[...].astype(F32) + conv).astype(BF16)


def swap_cores(value):
    return lax.ppermute(value, "core", [(0, 1), (1, 0)])


def swap_chips(value):
    pairs = []
    for x in range(4):
        last, first = 2 * x + 1, 2 * ((x + 1) % 4)
        pairs += [(last, first), (first, last)]
    return lax.ppermute(value, ("x", "core"), pairs)


def pack_kernel(own, one, two, three, out):
    for i, piece in enumerate((own, one, two, three)):
        out[i] = piece[...]


def gather_weights(piece):
    one, two, three = [
        lax.ppermute(piece, "x", [(i, (i + by) % 4) for i in range(4)]) for by in (1, 2, 3)
    ]
    packed = call(pack_kernel, shape((4, PIECE, CHANNELS), BF16), n=4)(piece, one, two, three)
    return piece, one, three, two, swap_cores(packed)


def per_device(latent, gain_one, weight_one, bias_one, gain_two, weight_two, bias_two):
    ids = jnp.stack([lax.axis_index(a) for a in ("z", "x", "core")]).astype(jnp.int32)
    latent = latent.reshape(64, CHANNELS)
    weight_one, weight_two = [
        jnp.transpose(w, (0, 1, 2, 4, 3)).reshape(27, 6, CHANNELS)
        for w in (weight_one, weight_two)
    ]
    prepare = call(
        prepare_kernel,
        shape((PIECE, CHANNELS), BF16),
        [pltpu.VMEM((PIECE, CHANNELS), F32)],
        anywhere=1,
        n=2,
    )
    sums = [shape((64, LANES), F32), shape((64, LANES), BF16)]
    whole = pltpu.VMEM((8 * SLOT, DEPTH), BF16)
    products = pltpu.VMEM((8 * SLOT, LANES), F32)
    later_to_next = lambda v: lax.ppermute(v, "t", [(i, i + 1) for i in range(7)])

    hidden = call(norm_kernel, shape((8, 64, CHANNELS), BF16), n=2)(latent, gain_one)
    weights = gather_weights(prepare(hidden, weight_one))
    level = lax.all_to_all(hidden, "z", 0, 0)
    own, later = call(
        conv_one_kernel,
        sums,
        [whole, pltpu.VMEM((LANES, DEPTH), BF16), products],
        smem=1,
        n=9,
    )(ids, level, swap_cores(level), swap_chips(level), *weights)
    middle = call(middle_kernel, shape((8, BLOCK, LANES), BF16), smem=1, n=4)(
        ids, own, later_to_next(later), bias_one
    )

    weights = gather_weights(prepare(middle, weight_two))
    level = call(field_two_kernel, shape((CHANNELS, LANES), BF16), n=2)(
        lax.all_to_all(middle, "z", 0, 0), gain_two
    )
    own, later = call(
        conv_two_kernel,
        sums,
        [whole, pltpu.VMEM((DEPTH, LANES), BF16), products],
        smem=1,
        n=9,
    )(ids, level, swap_cores(level), swap_chips(level), *weights)
    pieces, kept = call(
        spread_kernel,
        [shape((8, BLOCK, 64), BF16), shape((64, CHANNELS), BF16)],
        smem=1,
        n=5,
    )(ids, own, later_to_next(later), bias_two, latent)
    pieces = lax.all_to_all(pieces, "z", 0, 0)
    out = call(finish_kernel, shape((64, CHANNELS), BF16), n=2)(kept, pieces)
    return out.reshape(2, 1, 32, CHANNELS)


def solution(mesh):
    mesh = Mesh(mesh.devices.reshape(8, 8, 4, 2), ("t", "z", "x", "core"))
    rows = ("z", "x", "core")
    kernel = P(None, None, None, None, rows)
    field = P("t", rows, None, None)
    return jax.shard_map(
        per_device,
        mesh=mesh,
        in_specs=(field, P(), kernel, P(), P(), kernel, P()),
        out_specs=field,
        check_vma=False,
    )
```

time: 113 us -> 119 us (1.053)
  the two profiles are of different devices: /device:TPU:24 before, /device:TPU:32 now
where the time goes in v2:
time: 119 us; the launch traced here: 118 us
  starting transfers between devices  55.6 us (47%)
  waiting for transfers between devices  35.6 us (30%)
  blocking collectives  15.1 us (13%)
  Pallas kernels  10 us (8%)
  local copies, waits for them, and re-layouts  1.76 us (1%)
    ppermute x6, starting transfers between devices, gather_weights(): lax.ppermute(piece, 'x', [(i, (i + by) % 4) for i in range(4)])  18.5 us
    all_to_all x1, blocking collectives, per_device(): pieces = lax.all_to_all(pieces, 'z', 0, 0)  15.1 us
    ppermute x2, waiting for transfers between devices, swap_chips(): return lax.ppermute(value, ('x', 'core'), pairs)  14.5 us
    ppermute x6, waiting for transfers between devices, gather_weights(): lax.ppermute(piece, 'x', [(i, (i + by) % 4) for i in range(4)])  10.9 us
    all_to_all x1, starting transfers between devices, per_device(): level = lax.all_to_all(hidden, 'z', 0, 0)  10.4 us
    ppermute x2, waiting for transfers between devices, per_device(): lax.ppermute(v, 't', [(i, i + 1) for i in range(7)])  10.2 us
    ppermute x4, starting transfers between devices, swap_cores(): return lax.ppermute(value, 'core', [(0, 1), (1, 0)])  8.79 us
    all_to_all x1, starting transfers between devices, per_device(): lax.all_to_all(middle, 'z', 0, 0)  7.33 us
  transfers between devices with their start and end apart: 16, of which 8 were waited for; matrix products, arithmetic and copies ran while one was open for 0% of the time, Pallas kernels for 0%

profile of v2, /device:TPU:32, one launch (start us, length us, event | category | flops | bytes accessed | tf_op | source)
XLA Modules:
  0.0 118.5 jit_solution(7350166855481665157)
XLA Ops:
  0.0 0.8 copy-done
  0.8 0.7 copy-done.4
  1.5 0.9 shard_map.73.after
  2.4 10.4 %all-to-all-start = ((bf16[8,64,384]{2,1,0:T(8,128)(2,1)}), bf16[8,64,384]{2,1,0:T(8,128)(2,1)S(1)}, u32[]{:S(2)}, u32[]{:S(2)}) async-start(bf16[8,64,384]{2,1,0:T(8,128)(2,1)} %shard_map.73.after), calls=%async_computation | async-start | bytes 786432 | tf_op jit(solution)/shard_map/all_to_all | solution.py:270
  12.9 3.4 %collective-permute-start.2 = (bf16[176,384]{1,0:T(8,128)(2,1)S(1)}, bf16[176,384]{1,0:T(8,128)(2,1)S(1)}, u32[]{:S(2)}, u32[]{:S(2)}) collective-permute-start(bf16[176,384]{1,0:T(8,128)(2,1)S(1)} %shard_map.74.own.rest_0_), channel_id=1, source_target_pairs={{0,2},{2,4},{4,6},{6,0},{1,3},{3,5},{5,7},{7,1},{8,10},{10,12},{12... | collective-permute-start | bytes 405512 | tf_op jit(solution)/shard_map/ppermute | solution.py:243
  16.3 3.7 %collective-permute-start.3 = (bf16[176,384]{1,0:T(8,128)(2,1)S(1)}, bf16[176,384]{1,0:T(8,128)(2,1)S(1)}, u32[]{:S(2)}, u32[]{:S(2)}) collective-permute-start(bf16[176,384]{1,0:T(8,128)(2,1)S(1)} %shard_map.74.own.rest_0_), channel_id=1, source_target_pairs={{0,6},{2,0},{4,2},{6,4},{1,7},{3,1},{5,3},{7,5},{8,14},{10,8},{12,... | collective-permute-start | bytes 405512 | tf_op jit(solution)/shard_map/ppermute | solution.py:243
  20.0 3.7 %collective-permute-start.4 = (bf16[176,384]{1,0:T(8,128)(2,1)S(1)}, bf16[176,384]{1,0:T(8,128)(2,1)S(1)}, u32[]{:S(2)}, u32[]{:S(2)}) collective-permute-start(bf16[176,384]{1,0:T(8,128)(2,1)S(1)} %shard_map.74.own.rest_0_), channel_id=1, source_target_pairs={{0,4},{2,6},{4,0},{6,2},{1,5},{3,7},{5,1},{7,3},{8,12},{10,14},{12... | collective-permute-start | bytes 405512 | tf_op jit(solution)/shard_map/ppermute | solution.py:243
  23.7 4.7 %collective-permute-done.4.two.rest_3_ = bf16[176,384]{1,0:T(8,128)(2,1)S(1)} collective-permute-done((bf16[176,384]{1,0:T(8,128)(2,1)S(1)}, bf16[176,384]{1,0:T(8,128)(2,1)S(1)}, u32[]{:S(2)}, u32[]{:S(2)}) %collective-permute-start.4) | collective-permute-done | bytes 135200 | tf_op jit(solution)/shard_map/ppermute | solution.py:243
  28.4 1.9 %collective-permute-start.5 = (bf16[4,176,384]{2,1,0:T(8,128)(2,1)S(1)}, bf16[4,176,384]{2,1,0:T(8,128)(2,1)S(1)}, u32[]{:S(2)}, u32[]{:S(2)}) collective-permute-start(bf16[4,176,384]{2,1,0:T(8,128)(2,1)S(1)} %shard_map.75), channel_id=1, source_target_pairs={{0,1},{1,0},{2,3},{3,2},{4,5},{5,4},{6,7},{7,6},{8,9},{9,8},{10,11... | collective-permute-start | bytes 1622024 | tf_op jit(solution)/shard_map/ppermute | solution.py:225
  30.4 2.4 %collective-permute-start = (bf16[8,64,384]{2,1,0:T(8,128)(2,1)S(1)}, bf16[8,64,384]{2,1,0:T(8,128)(2,1)S(1)}, u32[]{:S(2)}, u32[]{:S(2)}) collective-permute-start(bf16[8,64,384]{2,1,0:T(8,128)(2,1)S(1)} %all-to-all-done.level), channel_id=1, source_target_pairs={{0,1},{1,0},{2,3},{3,2},{4,5},{5,4},{6,7},{7,6},{8,9},{9,8},{10,11... | collective-permute-start | bytes 1179656 | tf_op jit(solution)/shard_map/ppermute | solution.py:225
  32.8 3.1 %collective-permute-start.1 = (bf16[8,64,384]{2,1,0:T(8,128)(2,1)S(1)}, bf16[8,64,384]{2,1,0:T(8,128)(2,1)S(1)}, u32[]{:S(2)}, u32[]{:S(2)}) collective-permute-start(bf16[8,64,384]{2,1,0:T(8,128)(2,1)S(1)} %all-to-all-done.level), channel_id=1, source_target_pairs={{1,2},{2,1},{3,4},{4,3},{5,6},{6,5},{7,0},{0,7},{9,10},{10,9},{11,... | collective-permute-start | bytes 1179656 | tf_op jit(solution)/shard_map/ppermute | solution.py:233
  36.0 7.1 %collective-permute-done.1.pair = bf16[8,64,384]{2,1,0:T(8,128)(2,1)S(1)} collective-permute-done((bf16[8,64,384]{2,1,0:T(8,128)(2,1)S(1)}, bf16[8,64,384]{2,1,0:T(8,128)(2,1)S(1)}, u32[]{:S(2)}, u32[]{:S(2)}) %collective-permute-start.1) | collective-permute-done | bytes 393248 | tf_op jit(solution)/shard_map/ppermute | solution.py:233
  43.1 2.6 %shard_map.76 = (f32[64,512]{1,0:T(8,128)S(1)}, bf16[64,512]{1,0:T(8,128)(2,1)S(1)}) custom-call(s32[3]{0:T(128)S(1)} %pad_add_fusion.ids, bf16[8,64,384]{2,1,0:T(8,128)(2,1)S(1)} %all-to-all-done.level, bf16[8,64,384]{2,1,0:T(8,128)(2,1)S(1)} %collective-permute-done.partner, bf16[8,64,384]{2,1,0:T(8,128)(2,1)S(1)} %collective-permute-done.1.pair, ...), custom_call_target="tpu_custom_call" | custom-call | tf_op jit(solution)/shard_map/pallas_call | solution.py:271
  45.8 2.6 %collective-permute-start.6 = (bf16[64,512]{1,0:T(8,128)(2,1)S(1)}, bf16[64,512]{1,0:T(8,128)(2,1)S(1)}, u32[]{:S(2)}, u32[]{:S(2)}) collective-permute-start(bf16[64,512]{1,0:T(8,128)(2,1)S(1)} %get-tuple-element.12), channel_id=1, source_target_pairs={{0,64},{64,128},{128,192},{192,256},{256,320},{320,384},{384,448},... | collective-permute-start | bytes 196616 | tf_op jit(solution)/shard_map/ppermute | solution.py:266
  48.3 4.8 %collective-permute-done.6.earlier = bf16[64,512]{1,0:T(8,128)(2,1)S(1)} collective-permute-done((bf16[64,512]{1,0:T(8,128)(2,1)S(1)}, bf16[64,512]{1,0:T(8,128)(2,1)S(1)}, u32[]{:S(2)}, u32[]{:S(2)}) %collective-permute-start.6) | collective-permute-done | bytes 65568 | tf_op jit(solution)/shard_map/ppermute | solution.py:266
  53.1 1.5 %shard_map.77.after = bf16[8,48,512]{2,1,0:T(8,128)(2,1)} custom-call(s32[3]{0:T(128)S(1)} %pad_add_fusion.ids, f32[64,512]{1,0:T(8,128)S(1)} %get-tuple-element.11.own, bf16[64,512]{1,0:T(8,128)(2,1)S(1)} %collective-permute-done.6.earlier, f32[384]{0:T(512)S(1)} %copy-done.5), custom_call_target="tpu_custom_call" | custom-call | tf_op jit(solution)/shard_map/pallas_call | solution.py:278
  54.7 7.3 %all-to-all-start.1 = ((bf16[8,48,512]{2,1,0:T(8,128)(2,1)}), bf16[8,48,512]{2,1,0:T(8,128)(2,1)S(1)}, u32[]{:S(2)}, u32[]{:S(2)}) async-start(bf16[8,48,512]{2,1,0:T(8,128)(2,1)} %shard_map.77.after), calls=%async_computation.1 | async-start | bytes 786432 | tf_op jit(solution)/shard_map/all_to_all | solution.py:284
  62.1 2.7 %collective-permute-start.10 = (bf16[176,384]{1,0:T(8,128)(2,1)S(1)}, bf16[176,384]{1,0:T(8,128)(2,1)S(1)}, u32[]{:S(2)}, u32[]{:S(2)}) collective-permute-start(bf16[176,384]{1,0:T(8,128)(2,1)S(1)} %shard_map.79.own.rest_0_), channel_id=1, source_target_pairs={{0,6},{2,0},{4,2},{6,4},{1,7},{3,1},{5,3},{7,5},{8,14},{10,8},{12,... | collective-permute-start | bytes 405512 | tf_op jit(solution)/shard_map/ppermute | solution.py:243
  64.8 2.3 %collective-permute-start.11 = (bf16[176,384]{1,0:T(8,128)(2,1)S(1)}, bf16[176,384]{1,0:T(8,128)(2,1)S(1)}, u32[]{:S(2)}, u32[]{:S(2)}) collective-permute-start(bf16[176,384]{1,0:T(8,128)(2,1)S(1)} %shard_map.79.own.rest_0_), channel_id=1, source_target_pairs={{0,4},{2,6},{4,0},{6,2},{1,5},{3,7},{5,1},{7,3},{8,12},{10,14},{12... | collective-permute-start | bytes 405512 | tf_op jit(solution)/shard_map/ppermute | solution.py:243
  67.1 2.8 %collective-permute-start.9 = (bf16[176,384]{1,0:T(8,128)(2,1)S(1)}, bf16[176,384]{1,0:T(8,128)(2,1)S(1)}, u32[]{:S(2)}, u32[]{:S(2)}) collective-permute-start(bf16[176,384]{1,0:T(8,128)(2,1)S(1)} %shard_map.79.own.rest_0_), channel_id=1, source_target_pairs={{0,2},{2,4},{4,6},{6,0},{1,3},{3,5},{5,7},{7,1},{8,10},{10,12},{12... | collective-permute-start | bytes 405512 | tf_op jit(solution)/shard_map/ppermute | solution.py:243
  70.1 4.1 %collective-permute-done.11.two.rest_3_ = bf16[176,384]{1,0:T(8,128)(2,1)S(1)} collective-permute-done((bf16[176,384]{1,0:T(8,128)(2,1)S(1)}, bf16[176,384]{1,0:T(8,128)(2,1)S(1)}, u32[]{:S(2)}, u32[]{:S(2)}) %collective-permute-start.11) | collective-permute-done | bytes 135200 | tf_op jit(solution)/shard_map/ppermute | solution.py:243
  74.3 1.9 %collective-permute-done.9.one.rest_1_ = bf16[176,384]{1,0:T(8,128)(2,1)S(1)} collective-permute-done((bf16[176,384]{1,0:T(8,128)(2,1)S(1)}, bf16[176,384]{1,0:T(8,128)(2,1)S(1)}, u32[]{:S(2)}, u32[]{:S(2)}) %collective-permute-start.9) | collective-permute-done | bytes 135200 | tf_op jit(solution)/shard_map/ppermute | solution.py:243
  76.2 1.9 %collective-permute-start.12 = (bf16[4,176,384]{2,1,0:T(8,128)(2,1)S(1)}, bf16[4,176,384]{2,1,0:T(8,128)(2,1)S(1)}, u32[]{:S(2)}, u32[]{:S(2)}) collective-permute-start(bf16[4,176,384]{2,1,0:T(8,128)(2,1)S(1)} %shard_map.80), channel_id=1, source_target_pairs={{0,1},{1,0},{2,3},{3,2},{4,5},{5,4},{6,7},{7,6},{8,9},{9,8},{10,11... | collective-permute-start | bytes 1622024 | tf_op jit(solution)/shard_map/ppermute | solution.py:225
  78.5 2.5 %collective-permute-start.7 = (bf16[384,512]{1,0:T(8,128)(2,1)S(1)}, bf16[384,512]{1,0:T(8,128)(2,1)S(1)}, u32[]{:S(2)}, u32[]{:S(2)}) collective-permute-start(bf16[384,512]{1,0:T(8,128)(2,1)S(1)} %shard_map.78.level), channel_id=1, source_target_pairs={{0,1},{1,0},{2,3},{3,2},{4,5},{5,4},{6,7},{7,6},{8,9},{9,8},{10,11... | collective-permute-start | bytes 1179656 | tf_op jit(solution)/shard_map/ppermute | solution.py:225
  81.0 2.9 %collective-permute-start.8 = (bf16[384,512]{1,0:T(8,128)(2,1)S(1)}, bf16[384,512]{1,0:T(8,128)(2,1)S(1)}, u32[]{:S(2)}, u32[]{:S(2)}) collective-permute-start(bf16[384,512]{1,0:T(8,128)(2,1)S(1)} %shard_map.78.level), channel_id=1, source_target_pairs={{1,2},{2,1},{3,4},{4,3},{5,6},{6,5},{7,0},{0,7},{9,10},{10,9},{11,... | collective-permute-start | bytes 1179656 | tf_op jit(solution)/shard_map/ppermute | solution.py:233
  84.0 7.4 %collective-permute-done.8.pair = bf16[384,512]{1,0:T(8,128)(2,1)S(1)} collective-permute-done((bf16[384,512]{1,0:T(8,128)(2,1)S(1)}, bf16[384,512]{1,0:T(8,128)(2,1)S(1)}, u32[]{:S(2)}, u32[]{:S(2)}) %collective-permute-start.8) | collective-permute-done | bytes 393248 | tf_op jit(solution)/shard_map/ppermute | solution.py:233
  91.3 2.7 %shard_map.81 = (f32[64,512]{1,0:T(8,128)S(1)}, bf16[64,512]{1,0:T(8,128)(2,1)S(1)}) custom-call(s32[3]{0:T(128)S(1)} %pad_add_fusion.ids, bf16[384,512]{1,0:T(8,128)(2,1)S(1)} %shard_map.78.level, bf16[384,512]{1,0:T(8,128)(2,1)S(1)} %collective-permute-done.7.partner, bf16[384,512]{1,0:T(8,128)(2,1)S(1)} %collective-permute-done.8.pair, ...), custom_call_target="tpu_custom_call" | custom-call | tf_op jit(solution)/shard_map/pallas_call | solution.py:286
  94.0 1.9 %collective-permute-start.13 = (bf16[64,512]{1,0:T(8,128)(2,1)S(1)}, bf16[64,512]{1,0:T(8,128)(2,1)S(1)}, u32[]{:S(2)}, u32[]{:S(2)}) collective-permute-start(bf16[64,512]{1,0:T(8,128)(2,1)S(1)} %get-tuple-element.14), channel_id=1, source_target_pairs={{0,64},{64,128},{128,192},{192,256},{256,320},{320,384},{384,448},... | collective-permute-start | bytes 196616 | tf_op jit(solution)/shard_map/ppermute | solution.py:266
  95.9 5.4 %collective-permute-done.13.earlier = bf16[64,512]{1,0:T(8,128)(2,1)S(1)} collective-permute-done((bf16[64,512]{1,0:T(8,128)(2,1)S(1)}, bf16[64,512]{1,0:T(8,128)(2,1)S(1)}, u32[]{:S(2)}, u32[]{:S(2)}) %collective-permute-start.13) | collective-permute-done | bytes 65568 | tf_op jit(solution)/shard_map/ppermute | solution.py:266
  101.4 0.9 shard_map.82
  102.4 15.1 %all_to_all.15 = bf16[8,2,1536]{2,1,0:T(2,128)(2,1)S(1)} all-to-all(bf16[8,2,1536]{2,1,0:T(2,128)(2,1)S(1)} %reshape.16), channel_id=1, replica_groups=mesh['t'=8,'z'=8,'x'=4,'core'=2] {'z'}, dimensions={0} | all-to-all | bytes 98304 | tf_op jit(solution)/shard_map/all_to_all | solution.py:299
  117.6 0.8 shard_map.83
  (31 shorter events, 1.2 us)
Async XLA Ops:
  0.0 0.8 copy-start
  0.8 0.7 copy-start.4
  2.4 10.5 %copy-start.2 = (bf16[3,3,3,384,6]{3,4,2,1,0:T(8,128)(2,1)S(1)}, bf16[3,3,3,384,6]{3,4,2,1,0:T(8,128)(2,1)}, u32[]{:S(2)}) copy-start(bf16[3,3,3,384,6]{3,4,2,1,0:T(8,128)(2,1)} %param.9) | copy-start | bytes 373252
  2.4 28.0 %all-to-all-start = ((bf16[8,64,384]{2,1,0:T(8,128)(2,1)}), bf16[8,64,384]{2,1,0:T(8,128)(2,1)S(1)}, u32[]{:S(2)}, u32[]{:S(2)}) async-start(bf16[8,64,384]{2,1,0:T(8,128)(2,1)} %shard_map.73.after), calls=%async_computation | async-start | bytes 786432 | tf_op jit(solution)/shard_map/all_to_all | solution.py:270
  12.9 10.8 %collective-permute-start.2 = (bf16[176,384]{1,0:T(8,128)(2,1)S(1)}, bf16[176,384]{1,0:T(8,128)(2,1)S(1)}, u32[]{:S(2)}, u32[]{:S(2)}) collective-permute-start(bf16[176,384]{1,0:T(8,128)(2,1)S(1)} %shard_map.74.own.rest_0_), channel_id=1, source_target_pairs={{0,2},{2,4},{4,6},{6,0},{1,3},{3,5},{5,7},{7,1},{8,10},{10,12},{12... | collective-permute-start | bytes 405512 | tf_op jit(solution)/shard_map/ppermute | solution.py:243
  16.3 7.4 %collective-permute-start.3 = (bf16[176,384]{1,0:T(8,128)(2,1)S(1)}, bf16[176,384]{1,0:T(8,128)(2,1)S(1)}, u32[]{:S(2)}, u32[]{:S(2)}) collective-permute-start(bf16[176,384]{1,0:T(8,128)(2,1)S(1)} %shard_map.74.own.rest_0_), channel_id=1, source_target_pairs={{0,6},{2,0},{4,2},{6,4},{1,7},{3,1},{5,3},{7,5},{8,14},{10,8},{12,... | collective-permute-start | bytes 405512 | tf_op jit(solution)/shard_map/ppermute | solution.py:243
  20.0 8.4 %collective-permute-start.4 = (bf16[176,384]{1,0:T(8,128)(2,1)S(1)}, bf16[176,384]{1,0:T(8,128)(2,1)S(1)}, u32[]{:S(2)}, u32[]{:S(2)}) collective-permute-start(bf16[176,384]{1,0:T(8,128)(2,1)S(1)} %shard_map.74.own.rest_0_), channel_id=1, source_target_pairs={{0,4},{2,6},{4,0},{6,2},{1,5},{3,7},{5,1},{7,3},{8,12},{10,14},{12... | collective-permute-start | bytes 405512 | tf_op jit(solution)/shard_map/ppermute | solution.py:243
  28.4 7.5 %collective-permute-start.5 = (bf16[4,176,384]{2,1,0:T(8,128)(2,1)S(1)}, bf16[4,176,384]{2,1,0:T(8,128)(2,1)S(1)}, u32[]{:S(2)}, u32[]{:S(2)}) collective-permute-start(bf16[4,176,384]{2,1,0:T(8,128)(2,1)S(1)} %shard_map.75), channel_id=1, source_target_pairs={{0,1},{1,0},{2,3},{3,2},{4,5},{5,4},{6,7},{7,6},{8,9},{9,8},{10,11... | collective-permute-start | bytes 1622024 | tf_op jit(solution)/shard_map/ppermute | solution.py:225
  30.4 5.6 %collective-permute-start = (bf16[8,64,384]{2,1,0:T(8,128)(2,1)S(1)}, bf16[8,64,384]{2,1,0:T(8,128)(2,1)S(1)}, u32[]{:S(2)}, u32[]{:S(2)}) collective-permute-start(bf16[8,64,384]{2,1,0:T(8,128)(2,1)S(1)} %all-to-all-done.level), channel_id=1, source_target_pairs={{0,1},{1,0},{2,3},{3,2},{4,5},{5,4},{6,7},{7,6},{8,9},{9,8},{10,11... | collective-permute-start | bytes 1179656 | tf_op jit(solution)/shard_map/ppermute | solution.py:225
  32.8 10.3 %collective-permute-start.1 = (bf16[8,64,384]{2,1,0:T(8,128)(2,1)S(1)}, bf16[8,64,384]{2,1,0:T(8,128)(2,1)S(1)}, u32[]{:S(2)}, u32[]{:S(2)}) collective-permute-start(bf16[8,64,384]{2,1,0:T(8,128)(2,1)S(1)} %all-to-all-done.level), channel_id=1, source_target_pairs={{1,2},{2,1},{3,4},{4,3},{5,6},{6,5},{7,0},{0,7},{9,10},{10,9},{11,... | collective-permute-start | bytes 1179656 | tf_op jit(solution)/shard_map/ppermute | solution.py:233
  45.7 7.4 %copy-start.5 = (f32[384]{0:T(512)S(1)}, f32[384]{0:T(512)}, u32[]{:S(2)}) copy-start(f32[384]{0:T(512)} %bias.2) | copy-start | bytes 4612
  45.8 7.4 %collective-permute-start.6 = (bf16[64,512]{1,0:T(8,128)(2,1)S(1)}, bf16[64,512]{1,0:T(8,128)(2,1)S(1)}, u32[]{:S(2)}, u32[]{:S(2)}) collective-permute-start(bf16[64,512]{1,0:T(8,128)(2,1)S(1)} %get-tuple-element.12), channel_id=1, source_target_pairs={{0,64},{64,128},{128,192},{192,256},{256,320},{320,384},{384,448},... | collective-permute-start | bytes 196616 | tf_op jit(solution)/shard_map/ppermute | solution.py:266
  54.7 7.3 %copy-start.3 = (bf16[3,3,3,384,6]{3,4,2,1,0:T(8,128)(2,1)S(1)}, bf16[3,3,3,384,6]{3,4,2,1,0:T(8,128)(2,1)}, u32[]{:S(2)}) copy-start(bf16[3,3,3,384,6]{3,4,2,1,0:T(8,128)(2,1)} %param.12) | copy-start | bytes 373252
  54.7 23.4 %all-to-all-start.1 = ((bf16[8,48,512]{2,1,0:T(8,128)(2,1)}), bf16[8,48,512]{2,1,0:T(8,128)(2,1)S(1)}, u32[]{:S(2)}, u32[]{:S(2)}) async-start(bf16[8,48,512]{2,1,0:T(8,128)(2,1)} %shard_map.77.after), calls=%async_computation.1 | async-start | bytes 786432 | tf_op jit(solution)/shard_map/all_to_all | solution.py:284
  62.1 16.0 %copy-start.6 = (f32[384]{0:T(512)S(1)}, f32[384]{0:T(512)}, u32[]{:S(2)}) copy-start(f32[384]{0:T(512)} %gain.3) | copy-start | bytes 4612
  62.1 8.0 %collective-permute-start.10 = (bf16[176,384]{1,0:T(8,128)(2,1)S(1)}, bf16[176,384]{1,0:T(8,128)(2,1)S(1)}, u32[]{:S(2)}, u32[]{:S(2)}) collective-permute-start(bf16[176,384]{1,0:T(8,128)(2,1)S(1)} %shard_map.79.own.rest_0_), channel_id=1, source_target_pairs={{0,6},{2,0},{4,2},{6,4},{1,7},{3,1},{5,3},{7,5},{8,14},{10,8},{12,... | collective-permute-start | bytes 405512 | tf_op jit(solution)/shard_map/ppermute | solution.py:243
  64.8 9.5 %collective-permute-start.11 = (bf16[176,384]{1,0:T(8,128)(2,1)S(1)}, bf16[176,384]{1,0:T(8,128)(2,1)S(1)}, u32[]{:S(2)}, u32[]{:S(2)}) collective-permute-start(bf16[176,384]{1,0:T(8,128)(2,1)S(1)} %shard_map.79.own.rest_0_), channel_id=1, source_target_pairs={{0,4},{2,6},{4,0},{6,2},{1,5},{3,7},{5,1},{7,3},{8,12},{10,14},{12... | collective-permute-start | bytes 405512 | tf_op jit(solution)/shard_map/ppermute | solution.py:243
  67.1 9.1 %collective-permute-start.9 = (bf16[176,384]{1,0:T(8,128)(2,1)S(1)}, bf16[176,384]{1,0:T(8,128)(2,1)S(1)}, u32[]{:S(2)}, u32[]{:S(2)}) collective-permute-start(bf16[176,384]{1,0:T(8,128)(2,1)S(1)} %shard_map.79.own.rest_0_), channel_id=1, source_target_pairs={{0,2},{2,4},{4,6},{6,0},{1,3},{3,5},{5,7},{7,1},{8,10},{10,12},{12... | collective-permute-start | bytes 405512 | tf_op jit(solution)/shard_map/ppermute | solution.py:243
  76.2 7.8 %collective-permute-start.12 = (bf16[4,176,384]{2,1,0:T(8,128)(2,1)S(1)}, bf16[4,176,384]{2,1,0:T(8,128)(2,1)S(1)}, u32[]{:S(2)}, u32[]{:S(2)}) collective-permute-start(bf16[4,176,384]{2,1,0:T(8,128)(2,1)S(1)} %shard_map.80), channel_id=1, source_target_pairs={{0,1},{1,0},{2,3},{3,2},{4,5},{5,4},{6,7},{7,6},{8,9},{9,8},{10,11... | collective-permute-start | bytes 1622024 | tf_op jit(solution)/shard_map/ppermute | solution.py:225
  78.4 22.9 %copy-start.1 = (bf16[2,1,32,384]{3,2,1,0:T(8,128)(2,1)S(1)}, bf16[2,1,32,384]{3,2,1,0:T(8,128)(2,1)}, u32[]{:S(2)}) copy-start(bf16[2,1,32,384]{3,2,1,0:T(8,128)(2,1)} %param.7) | copy-start | bytes 147460
  78.5 5.5 %collective-permute-start.7 = (bf16[384,512]{1,0:T(8,128)(2,1)S(1)}, bf16[384,512]{1,0:T(8,128)(2,1)S(1)}, u32[]{:S(2)}, u32[]{:S(2)}) collective-permute-start(bf16[384,512]{1,0:T(8,128)(2,1)S(1)} %shard_map.78.level), channel_id=1, source_target_pairs={{0,1},{1,0},{2,3},{3,2},{4,5},{5,4},{6,7},{7,6},{8,9},{9,8},{10,11... | collective-permute-start | bytes 1179656 | tf_op jit(solution)/shard_map/ppermute | solution.py:225
  81.0 10.3 %collective-permute-start.8 = (bf16[384,512]{1,0:T(8,128)(2,1)S(1)}, bf16[384,512]{1,0:T(8,128)(2,1)S(1)}, u32[]{:S(2)}, u32[]{:S(2)}) collective-permute-start(bf16[384,512]{1,0:T(8,128)(2,1)S(1)} %shard_map.78.level), channel_id=1, source_target_pairs={{1,2},{2,1},{3,4},{4,3},{5,6},{6,5},{7,0},{0,7},{9,10},{10,9},{11,... | collective-permute-start | bytes 1179656 | tf_op jit(solution)/shard_map/ppermute | solution.py:233
  94.0 7.4 %copy-start.7 = (f32[384]{0:T(512)S(1)}, f32[384]{0:T(512)}, u32[]{:S(2)}) copy-start(f32[384]{0:T(512)} %bias.3) | copy-start | bytes 4612
  94.0 7.4 %collective-permute-start.13 = (bf16[64,512]{1,0:T(8,128)(2,1)S(1)}, bf16[64,512]{1,0:T(8,128)(2,1)S(1)}, u32[]{:S(2)}, u32[]{:S(2)}) collective-permute-start(bf16[64,512]{1,0:T(8,128)(2,1)S(1)} %get-tuple-element.14), channel_id=1, source_target_pairs={{0,64},{64,128},{128,192},{192,256},{256,320},{320,384},{384,448},... | collective-permute-start | bytes 196616 | tf_op jit(solution)/shard_map/ppermute | solution.py:266

commit v3 on v1

v3 whole, which is shorter than its diff:
```python
import jax
import jax.numpy as jnp
from jax import lax
from jax.experimental import pallas as pl
from jax.experimental.pallas import tpu as pltpu
from jax.sharding import Mesh
from jax.sharding import PartitionSpec as P

CHANNELS = 384
BLOCK = 48
PIECE = 176
SLOT = 224
LANES = 512
VMEM = 48 * 1024 * 1024
F32 = jnp.float32
BF16 = jnp.bfloat16


def call(kernel, out_shape, scratch=(), smem=0, anywhere=0, n=0, flops=0):
    specs = [pl.BlockSpec(memory_space=pltpu.SMEM)] * smem
    specs += [pl.BlockSpec(memory_space=pl.ANY)] * anywhere
    specs += [pl.BlockSpec(memory_space=pltpu.VMEM)] * (n - len(specs))
    multiple = isinstance(out_shape, (list, tuple))
    vmem = pl.BlockSpec(memory_space=pltpu.VMEM)
    return pl.pallas_call(
        kernel,
        out_shape=out_shape,
        in_specs=specs,
        out_specs=[vmem] * len(out_shape) if multiple else vmem,
        scratch_shapes=list(scratch),
        compiler_params=pltpu.CompilerParams(vmem_limit_bytes=VMEM),
        cost_estimate=pl.CostEstimate(flops=flops, bytes_accessed=0, transcendentals=0),
    )


def shape(dims, dtype):
    return jax.ShapeDtypeStruct(dims, dtype)


def iota(dims, axis):
    return lax.broadcasted_iota(jnp.int32, dims, axis)


def silu(v):
    return v / (1.0 + jnp.exp(-v))


def norm_kernel(latent, gain, hidden):
    values = latent[...].astype(F32)
    mean = jnp.mean(values * values, axis=1, keepdims=True)
    scale = lax.rsqrt(mean + 1e-6) * gain[...].reshape(1, CHANNELS)
    result = silu(values * scale).astype(BF16)
    for z in range(8):
        hidden[z] = result


def prepare_kernel(weight_one, weight_two, piece_one, piece_two, rows):
    for weight, piece in ((weight_one, piece_one), (weight_two, piece_two)):
        for tap in range(27):
            rows[6 * tap : 6 * tap + 6, :] = weight[tap].astype(F32)
        rows[162:PIECE, :] = jnp.zeros((PIECE - 162, CHANNELS), F32)
        piece[...] = rows[...].astype(BF16)


def place_weights(ids, own, ahead, behind, across, swapped, whole):
    x, c = ids[1], ids[2]
    row = iota((SLOT, PIECE), 0)
    wanted = (iota((SLOT, PIECE), 1) == 6 * (row // 8) + lax.rem(row, 8)) & (lax.rem(row, 8) < 6)
    spread = wanted.astype(F32).astype(BF16)

    def place(position, value):
        whole[position] = jnp.dot(spread, value, preferred_element_type=F32).astype(BF16)

    for shift, piece in ((0, own), (1, ahead), (2, across), (3, behind)):
        position = lax.rem(x + 4 - shift, 4) * 2
        place(position + c, piece[...])
        place(position + 1 - c, swapped[shift])


def taps(ids, products, keep, partner, pair):
    c = ids[2]
    column = lax.rem(iota((8, 2 * LANES), 1), 32)
    half = LANES // 2
    for two in range(4):
        parts = ([], [], [])
        for slot in (2 * two, 2 * two + 1):
            for j in range(3):
                sums = []
                for l in range(3):
                    k = [
                        products[pl.ds(slot * SLOT + 8 * (9 * i + 3 * j + l), 8), :]
                        for i in range(3)
                    ]
                    frames = [
                        k[2][:, :half],
                        k[2][:, half:] + k[1][:, :half],
                        k[1][:, half:] + k[0][:, :half],
                        k[0][:, half:],
                    ]
                    sums.append(jnp.concatenate(frames, axis=1))
                left = jnp.where(column == 0, 0.0, pltpu.roll(sums[0], 1, 1))
                right = jnp.where(column == 31, 0.0, pltpu.roll(sums[2], 2 * LANES - 1, 1))
                parts[j].append(sums[1] + left + right)
        below, level, above = [jnp.concatenate(p, axis=0) for p in parts]
        at = pl.ds(16 * two, 16)
        keep[at, :] = level
        partner[at, :] = jnp.where(c == 0, below, above).astype(BF16)
        pair[at, :] = jnp.where(c == 0, above, below).astype(BF16)


def conv_one_kernel(ids, gathered, *rest):
    *pieces, keep, partner, pair, whole, field, products = rest
    place_weights(ids, *pieces, whole)
    for z in range(8):
        for f in range(2):
            field[pl.ds(256 * f + 32 * z, 32), :] = gathered[z, pl.ds(32 * f, 32), :]
    products[...] = lax.dot_general(
        whole[...].reshape(8 * SLOT, CHANNELS),
        field[...],
        (((1,), (1,)), ((), ())),
        preferred_element_type=F32,
    )
    taps(ids, products, keep, partner, pair)


def conv_two_kernel(ids, gathered, gain, *rest):
    *pieces, keep, partner, pair, whole, products = rest
    place_weights(ids, *pieces, whole)
    values = gathered[...].reshape(CHANNELS, LANES).astype(F32)
    mean = jnp.mean(values * values, axis=0, keepdims=True)
    square = (CHANNELS, CHANNELS)
    same = iota(square, 0) == iota(square, 1)
    gains = jnp.where(same, gain[...].reshape(1, CHANNELS), 0.0)
    scale = jnp.sum(gains, axis=1, keepdims=True)
    field = silu(values * lax.rsqrt(mean + 1e-6) * scale).astype(BF16)
    products[...] = jnp.dot(
        whole[...].reshape(8 * SLOT, CHANNELS), field, preferred_element_type=F32
    )
    taps(ids, products, keep, partner, pair)


def rows_kernel(ids, keep, partners, pair, own, later):
    c = ids[2]
    position = 2 * ids[1] + c
    total = keep[...] + partners[1 - c].astype(F32)
    place = lax.rem(iota((64, 2 * LANES), 1) // 32, 8)

    def finish(got):
        result = total + got
        own[...] = result[:, :LANES]
        later[...] = result[:, LANES:].astype(BF16)

    @pl.when((position > 0) & (position < 7))
    def _():
        finish(pair[...].astype(F32))

    @pl.when(position == 0)
    def _():
        finish(jnp.where(place == 0, 0.0, pltpu.roll(pair[...].astype(F32), 32, 1)))

    @pl.when(position == 7)
    def _():
        got = pltpu.roll(pair[...].astype(F32), 2 * LANES - 32, 1)
        finish(jnp.where(place == 7, 0.0, got))


def block_values(ids, own, earlier, bias):
    row = iota((64, CHANNELS), 0)
    wanted = BLOCK * ids[0] + 6 * (row // 8) + lax.rem(row, 8)
    chosen = (iota((64, CHANNELS), 1) == wanted) & (lax.rem(row, 8) < 6)
    biases = jnp.where(chosen, bias[...].reshape(1, CHANNELS), 0.0)
    column = jnp.sum(biases, axis=1, keepdims=True)
    total = (own[...] + earlier[...].astype(F32) + column).astype(BF16)
    to, frm = iota((BLOCK, 64), 0), iota((BLOCK, 64), 1)
    pick = (frm == 8 * (to // 6) + lax.rem(to, 6)).astype(BF16)
    return jnp.dot(pick, total, preferred_element_type=F32).astype(BF16)


def middle_kernel(ids, after, own, earlier, bias, middle):
    result = block_values(ids, own, earlier, bias)
    for z in range(8):
        middle[z] = result


def spread_kernel(ids, own, earlier, bias, latent, pieces, kept):
    result = block_values(ids, own, earlier, bias)
    for z in range(8):
        frames = [result[:, 256 * f + 32 * z : 256 * f + 32 * z + 32] for f in range(2)]
        pieces[z] = jnp.concatenate(frames, axis=1)
    kept[...] = latent[...]


def finish_kernel(latent, gathered, out):
    square = (CHANNELS, CHANNELS)
    same = iota(square, 0) == iota(square, 1)
    conv = lax.dot_general(
        gathered[...].reshape(CHANNELS, 64),
        same.astype(BF16),
        (((0,), (0,)), ((), ())),
        preferred_element_type=F32,
    )
    out[...] = (latent[...].astype(F32) + conv).astype(BF16)


def swap_cores(value):
    return lax.ppermute(value, "core", [(0, 1), (1, 0)])


def exchange(ids, keep, partner, pair):
    swaps = []
    for x in range(4):
        last, first = 2 * x + 1, 2 * ((x + 1) % 4)
        swaps += [(last, first), (first, last)]
    pair = lax.ppermute(pair, ("x", "core"), swaps)
    partners = lax.all_gather(partner, "core", axis=0)
    own, later = call(
        rows_kernel,
        [shape((64, LANES), F32), shape((64, LANES), BF16)],
        smem=1,
        n=4,
    )(ids, keep, partners, pair)
    return own, lax.ppermute(later, "t", [(i, i + 1) for i in range(7)])


def gather_weights(piece):
    one, two, three = [
        lax.ppermute(piece, "x", [(i, (i + by) % 4) for i in range(4)]) for by in (1, 2, 3)
    ]
    packed = jnp.stack([piece, one, two, three])
    return (piece, one, three, two), packed


def per_device(latent, gain_one, weight_one, bias_one, gain_two, weight_two, bias_two):
    ids = jnp.stack([lax.axis_index(a) for a in ("z", "x", "core")]).astype(jnp.int32)
    latent = latent.reshape(64, CHANNELS)
    weight_one, weight_two = [
        jnp.transpose(w, (0, 1, 2, 4, 3)).reshape(27, 6, CHANNELS)
        for w in (weight_one, weight_two)
    ]
    piece = shape((PIECE, CHANNELS), BF16)
    sums = [
        shape((64, 2 * LANES), F32),
        shape((64, 2 * LANES), BF16),
        shape((64, 2 * LANES), BF16),
    ]
    whole = pltpu.VMEM((8, SLOT, CHANNELS), BF16)
    products = pltpu.VMEM((8 * SLOT, LANES), F32)

    hidden = call(norm_kernel, shape((8, 64, CHANNELS), BF16), n=2)(latent, gain_one)
    pieces = call(prepare_kernel, [piece, piece], [pltpu.VMEM((PIECE, CHANNELS), F32)], n=2)(
        weight_one, weight_two
    )
    (weights_one, packed_one), (weights_two, packed_two) = [gather_weights(p) for p in pieces]
    gathered = lax.all_to_all(hidden, "z", 0, 0)
    sums_one = call(
        conv_one_kernel,
        sums,
        [whole, pltpu.VMEM((LANES, CHANNELS), BF16), products],
        smem=1,
        n=7,
    )(ids, gathered, *weights_one, swap_cores(packed_one))
    own, earlier = exchange(ids, *sums_one)
    middle = call(middle_kernel, shape((8, BLOCK, LANES), BF16), smem=1, anywhere=1, n=5)(
        ids, packed_two, own, earlier, bias_one
    )
    gathered = lax.all_to_all(middle, "z", 0, 0)
    sums_two = call(conv_two_kernel, sums, [whole, products], smem=1, n=8)(
        ids, gathered, gain_two, *weights_two, swap_cores(packed_two)
    )
    own, earlier = exchange(ids, *sums_two)
    pieces, kept = call(
        spread_kernel,
        [shape((8, BLOCK, 64), BF16), shape((64, CHANNELS), BF16)],
        smem=1,
        n=5,
    )(ids, own, earlier, bias_two, latent)
    pieces = lax.all_to_all(pieces, "z", 0, 0)
    out = call(finish_kernel, shape((64, CHANNELS), BF16), n=2)(kept, pieces)
    return out.reshape(2, 1, 32, CHANNELS)


def solution(mesh):
    mesh = Mesh(mesh.devices.reshape(8, 8, 4, 2), ("t", "z", "x", "core"))
    rows = ("z", "x", "core")
    kernel = P(None, None, None, None, rows)
    field = P("t", rows, None, None)
    return jax.shard_map(
        per_device,
        mesh=mesh,
        in_specs=(field, P(), kernel, P(), P(), kernel, P()),
        out_specs=field,
        check_vma=False,
    )
```

time: 113 us -> 107 us (0.947)
  the two profiles are of different devices: /device:TPU:24 before, /device:TPU:32 now
where the time goes in v3:
time: 107 us; the launch traced here: 106 us
  starting transfers between devices  50.2 us (47%)
  waiting for transfers between devices  28 us (26%)
  blocking collectives  14.9 us (14%)
  Pallas kernels  10.4 us (10%)
  local copies, waits for them, and re-layouts  2.11 us (2%)
    ppermute x6, starting transfers between devices, gather_weights(): lax.ppermute(piece, 'x', [(i, (i + by) % 4) for i in range(4)])  19.8 us
    all_to_all x1, blocking collectives, per_device(): pieces = lax.all_to_all(pieces, 'z', 0, 0)  10.6 us
    all_to_all x1, starting transfers between devices, per_device(): gathered = lax.all_to_all(hidden, 'z', 0, 0)  10.3 us
    ppermute x2, waiting for transfers between devices, exchange(): return (own, lax.ppermute(later, 't', [(i, i + 1) for i in range(7)]))  10.1 us
    all_to_all x1, waiting for transfers between devices, per_device(): gathered = lax.all_to_all(middle, 'z', 0, 0)  8.82 us
    ppermute x2, starting transfers between devices, exchange(): pair = lax.ppermute(pair, ('x', 'core'), swaps)  7.77 us
    ppermute x2, starting transfers between devices, exchange(): return (own, lax.ppermute(later, 't', [(i, i + 1) for i in range(7)]))  4.51 us
    all_gather x2, blocking collectives, exchange(): partners = lax.all_gather(partner, 'core', axis=0)  4.34 us
  transfers between devices with their start and end apart: 14, of which 7 were waited for; matrix products, arithmetic and copies ran while one was open for 0% of the time, Pallas kernels for 4%

profile of v3, /device:TPU:32, one launch (start us, length us, event | category | flops | bytes accessed | tf_op | source)
XLA Modules:
  0.0 106.1 jit_solution(10605559898904863955)
XLA Ops:
  0.0 0.9 copy-done.1
  0.9 0.9 copy-done.2
  1.9 3.4 %collective-permute-start.3 = (bf16[176,384]{1,0:T(8,128)(2,1)S(1)}, bf16[176,384]{1,0:T(8,128)(2,1)S(1)}, u32[]{:S(2)}, u32[]{:S(2)}) collective-permute-start(bf16[176,384]{1,0:T(8,128)(2,1)S(1)} %get-tuple-element.20.rest_0_), channel_id=1, source_target_pairs={{0,2},{2,4},{4,6},{6,0},{1,3},{3,5},{5,7},{7,1},{8,10},{10,12},{12... | collective-permute-start | bytes 405512 | tf_op jit(solution)/shard_map/ppermute | solution.py:227
  5.4 4.6 %collective-permute-start.5 = (bf16[176,384]{1,0:T(8,128)(2,1)S(1)}, bf16[176,384]{1,0:T(8,128)(2,1)S(1)}, u32[]{:S(2)}, u32[]{:S(2)}) collective-permute-start(bf16[176,384]{1,0:T(8,128)(2,1)S(1)} %get-tuple-element.20.rest_0_), channel_id=1, source_target_pairs={{0,4},{2,6},{4,0},{6,2},{1,5},{3,7},{5,1},{7,3},{8,12},{10,14},{12... | collective-permute-start | bytes 405512 | tf_op jit(solution)/shard_map/ppermute | solution.py:227
  10.0 3.3 %collective-permute-start.4 = (bf16[176,384]{1,0:T(8,128)(2,1)S(1)}, bf16[176,384]{1,0:T(8,128)(2,1)S(1)}, u32[]{:S(2)}, u32[]{:S(2)}) collective-permute-start(bf16[176,384]{1,0:T(8,128)(2,1)S(1)} %get-tuple-element.20.rest_0_), channel_id=1, source_target_pairs={{0,6},{2,0},{4,2},{6,4},{1,7},{3,1},{5,3},{7,5},{8,14},{10,8},{12,... | collective-permute-start | bytes 405512 | tf_op jit(solution)/shard_map/ppermute | solution.py:227
  13.4 0.9 shard_map.74
  14.3 10.3 %all-to-all-start = ((bf16[8,64,384]{2,1,0:T(8,128)(2,1)}), bf16[8,64,384]{2,1,0:T(8,128)(2,1)S(1)}, u32[]{:S(2)}, u32[]{:S(2)}) async-start(bf16[8,64,384]{2,1,0:T(8,128)(2,1)} %shard_map.74), calls=%async_computation | async-start | bytes 786432 | tf_op jit(solution)/shard_map/all_to_all | solution.py:254
  24.7 1.9 %collective-permute-start.6 = (bf16[4,176,384]{2,1,0:T(8,128)(2,1)S(1)}, bf16[4,176,384]{2,1,0:T(8,128)(2,1)S(1)}, u32[]{:S(2)}, u32[]{:S(2)}) collective-permute-start(bf16[4,176,384]{2,1,0:T(8,128)(2,1)S(1)} %pad_maximum_fusion.1), channel_id=1, source_target_pairs={{0,1},{1,0},{2,3},{3,2},{4,5},{5,4},{6,7},{7,6},{8,9},{9,8},{10,11... | collective-permute-start | bytes 1622024 | tf_op jit(solution)/shard_map/ppermute | solution.py:206
  26.6 1.9 %collective-permute-start.2 = (bf16[176,384]{1,0:T(8,128)(2,1)S(1)}, bf16[176,384]{1,0:T(8,128)(2,1)S(1)}, u32[]{:S(2)}, u32[]{:S(2)}) collective-permute-start(bf16[176,384]{1,0:T(8,128)(2,1)S(1)} %get-tuple-element.19.rest_0_), channel_id=1, source_target_pairs={{0,6},{2,0},{4,2},{6,4},{1,7},{3,1},{5,3},{7,5},{8,14},{10,8},{12,... | collective-permute-start | bytes 405512 | tf_op jit(solution)/shard_map/ppermute | solution.py:227
  28.6 3.9 %collective-permute-start = (bf16[176,384]{1,0:T(8,128)(2,1)S(1)}, bf16[176,384]{1,0:T(8,128)(2,1)S(1)}, u32[]{:S(2)}, u32[]{:S(2)}) collective-permute-start(bf16[176,384]{1,0:T(8,128)(2,1)S(1)} %get-tuple-element.19.rest_0_), channel_id=1, source_target_pairs={{0,2},{2,4},{4,6},{6,0},{1,3},{3,5},{5,7},{7,1},{8,10},{10,12},{12... | collective-permute-start | bytes 405512 | tf_op jit(solution)/shard_map/ppermute | solution.py:227
  32.5 2.6 %collective-permute-start.1 = (bf16[176,384]{1,0:T(8,128)(2,1)S(1)}, bf16[176,384]{1,0:T(8,128)(2,1)S(1)}, u32[]{:S(2)}, u32[]{:S(2)}) collective-permute-start(bf16[176,384]{1,0:T(8,128)(2,1)S(1)} %get-tuple-element.19.rest_0_), channel_id=1, source_target_pairs={{0,4},{2,6},{4,0},{6,2},{1,5},{3,7},{5,1},{7,3},{8,12},{10,14},{12... | collective-permute-start | bytes 405512 | tf_op jit(solution)/shard_map/ppermute | solution.py:227
  35.2 3.3 %all-to-all-done.gathered = bf16[8,64,384]{2,1,0:T(8,128)(2,1)S(1)} async-done(((bf16[8,64,384]{2,1,0:T(8,128)(2,1)}), bf16[8,64,384]{2,1,0:T(8,128)(2,1)S(1)}, u32[]{:S(2)}, u32[]{:S(2)}) %all-to-all-start) | async-done | bytes 393248 | tf_op jit(solution)/shard_map/all_to_all | solution.py:254
  38.4 2.3 %shard_map.75 = (f32[64,1024]{1,0:T(8,128)S(1)}, bf16[64,1024]{1,0:T(8,128)(2,1)S(1)}, bf16[64,1024]{1,0:T(8,128)(2,1)S(1)}) custom-call(s32[3]{0:T(128)S(1)} %pad_add_fusion.ids, bf16[8,64,384]{2,1,0:T(8,128)(2,1)S(1)} %all-to-all-done.gathered, bf16[176,384]{1,0:T(8,128)(2,1)S(1)} %get-tuple-element.20.rest_0_, ...), custom_call_target="tpu_custom_call" | custom-call | tf_op jit(solution)/shard_map/pallas_call | solution.py:255
  40.8 1.9 %collective-permute-start.7 = (bf16[64,1024]{1,0:T(8,128)(2,1)S(1)}, bf16[64,1024]{1,0:T(8,128)(2,1)S(1)}, u32[]{:S(2)}, u32[]{:S(2)}) collective-permute-start(bf16[64,1024]{1,0:T(8,128)(2,1)S(1)} %get-tuple-element.23), channel_id=1, source_target_pairs={{1,2},{2,1},{3,4},{4,3},{5,6},{6,5},{7,0},{0,7},{9,10},{10,9},{11,... | collective-permute-start | bytes 393224 | tf_op jit(solution)/shard_map/ppermute | solution.py:214
  42.7 2.3 %all-gather = bf16[128,1024]{1,0:T(8,128)(2,1)S(1)} all-gather(bf16[64,1024]{1,0:T(8,128)(2,1)S(1)} %get-tuple-element.22), channel_id=2, replica_groups=mesh['t'=8,'z'=8,'x'=4,'core'=2] {'core'}, dimensions={0}, use_global_device_ids=true | all-gather | bytes 393216 | tf_op jit(solution)/shard_map/all_gather | solution.py:215
  45.1 3.2 %collective-permute-done.7.pair = bf16[64,1024]{1,0:T(8,128)(2,1)S(1)} collective-permute-done((bf16[64,1024]{1,0:T(8,128)(2,1)S(1)}, bf16[64,1024]{1,0:T(8,128)(2,1)S(1)}, u32[]{:S(2)}, u32[]{:S(2)}) %collective-permute-start.7) | collective-permute-done | bytes 131104 | tf_op jit(solution)/shard_map/ppermute | solution.py:214
  48.3 0.7 shard_map.76
  49.0 2.6 %collective-permute-start.8 = (bf16[64,512]{1,0:T(8,128)(2,1)S(1)}, bf16[64,512]{1,0:T(8,128)(2,1)S(1)}, u32[]{:S(2)}, u32[]{:S(2)}) collective-permute-start(bf16[64,512]{1,0:T(8,128)(2,1)S(1)} %get-tuple-element.25), channel_id=1, source_target_pairs={{0,64},{64,128},{128,192},{192,256},{256,320},{320,384},{384,448},... | collective-permute-start | bytes 196616 | tf_op jit(solution)/shard_map/ppermute | solution.py:222
  51.7 4.6 %collective-permute-done.8.earlier = bf16[64,512]{1,0:T(8,128)(2,1)S(1)} collective-permute-done((bf16[64,512]{1,0:T(8,128)(2,1)S(1)}, bf16[64,512]{1,0:T(8,128)(2,1)S(1)}, u32[]{:S(2)}, u32[]{:S(2)}) %collective-permute-start.8) | collective-permute-done | bytes 65568 | tf_op jit(solution)/shard_map/ppermute | solution.py:222
  56.3 1.5 %shard_map.77 = bf16[8,48,512]{2,1,0:T(8,128)(2,1)} custom-call(s32[3]{0:T(128)S(1)} %pad_add_fusion.ids, bf16[4,176,384]{2,1,0:T(8,128)(2,1)S(1)} %pad_maximum_fusion.after, f32[64,512]{1,0:T(8,128)S(1)} %get-tuple-element.24.own, bf16[64,512]{1,0:T(8,128)(2,1)S(1)} %collective-permute-done.8.earlier, f32[384]{0:T(512)S(1)} %copy-done.4), custom_call_target="tpu_custom_call" | custom-call | tf_op jit(solution)/shard_map/pallas_call | solution.py:263
  57.9 4.0 %all-to-all-start.1 = ((bf16[8,48,512]{2,1,0:T(8,128)(2,1)}), bf16[8,48,512]{2,1,0:T(8,128)(2,1)S(1)}, u32[]{:S(2)}, u32[]{:S(2)}) async-start(bf16[8,48,512]{2,1,0:T(8,128)(2,1)} %shard_map.77), calls=%async_computation.1 | async-start | bytes 786432 | tf_op jit(solution)/shard_map/all_to_all | solution.py:266
  61.9 1.9 %collective-permute-start.9 = (bf16[4,176,384]{2,1,0:T(8,128)(2,1)S(1)}, bf16[4,176,384]{2,1,0:T(8,128)(2,1)S(1)}, u32[]{:S(2)}, u32[]{:S(2)}) collective-permute-start(bf16[4,176,384]{2,1,0:T(8,128)(2,1)S(1)} %pad_maximum_fusion.after), channel_id=1, source_target_pairs={{0,1},{1,0},{2,3},{3,2},{4,5},{5,4},{6,7},{7,6},{8,9},{9,8},{10,11... | collective-permute-start | bytes 1622024 | tf_op jit(solution)/shard_map/ppermute | solution.py:206
  63.9 1.9 %collective-permute-done.9.rest_4_ = bf16[4,176,384]{2,1,0:T(8,128)(2,1)S(1)} collective-permute-done((bf16[4,176,384]{2,1,0:T(8,128)(2,1)S(1)}, bf16[4,176,384]{2,1,0:T(8,128)(2,1)S(1)}, u32[]{:S(2)}, u32[]{:S(2)}) %collective-permute-start.9) | collective-permute-done | bytes 540704 | tf_op jit(solution)/shard_map/ppermute | solution.py:206
  65.8 8.8 %all-to-all-done.1.gathered = bf16[8,48,512]{2,1,0:T(8,128)(2,1)S(1)} async-done(((bf16[8,48,512]{2,1,0:T(8,128)(2,1)}), bf16[8,48,512]{2,1,0:T(8,128)(2,1)S(1)}, u32[]{:S(2)}, u32[]{:S(2)}) %all-to-all-start.1) | async-done | bytes 393248 | tf_op jit(solution)/shard_map/all_to_all | solution.py:266
  74.6 2.4 %shard_map.78 = (f32[64,1024]{1,0:T(8,128)S(1)}, bf16[64,1024]{1,0:T(8,128)(2,1)S(1)}, bf16[64,1024]{1,0:T(8,128)(2,1)S(1)}) custom-call(s32[3]{0:T(128)S(1)} %pad_add_fusion.ids, bf16[8,48,512]{2,1,0:T(8,128)(2,1)S(1)} %all-to-all-done.1.gathered, f32[384]{0:T(512)S(1)} %copy-done.5, bf16[176,384]{1,0:T(8,128)(2,1)S(1)} %get-tuple-element.19.rest_0_, ...), custom_call_target="tpu_custom_call" | custom-call | tf_op jit(solution)/shard_map/pallas_call | solution.py:267
  77.0 5.8 %collective-permute-start.10 = (bf16[64,1024]{1,0:T(8,128)(2,1)S(1)}, bf16[64,1024]{1,0:T(8,128)(2,1)S(1)}, u32[]{:S(2)}, u32[]{:S(2)}) collective-permute-start(bf16[64,1024]{1,0:T(8,128)(2,1)S(1)} %get-tuple-element.28), channel_id=1, source_target_pairs={{1,2},{2,1},{3,4},{4,3},{5,6},{6,5},{7,0},{0,7},{9,10},{10,9},{11,... | collective-permute-start | bytes 393224 | tf_op jit(solution)/shard_map/ppermute | solution.py:214
  82.9 2.0 %all-gather.1 = bf16[128,1024]{1,0:T(8,128)(2,1)S(1)} all-gather(bf16[64,1024]{1,0:T(8,128)(2,1)S(1)} %get-tuple-element.27), channel_id=3, replica_groups=mesh['t'=8,'z'=8,'x'=4,'core'=2] {'core'}, dimensions={0}, use_global_device_ids=true | all-gather | bytes 393216 | tf_op jit(solution)/shard_map/all_gather | solution.py:215
  86.2 1.9 %collective-permute-start.11 = (bf16[64,512]{1,0:T(8,128)(2,1)S(1)}, bf16[64,512]{1,0:T(8,128)(2,1)S(1)}, u32[]{:S(2)}, u32[]{:S(2)}) collective-permute-start(bf16[64,512]{1,0:T(8,128)(2,1)S(1)} %get-tuple-element.30), channel_id=1, source_target_pairs={{0,64},{64,128},{128,192},{192,256},{256,320},{320,384},{384,448},... | collective-permute-start | bytes 196616 | tf_op jit(solution)/shard_map/ppermute | solution.py:222
  88.2 5.4 %collective-permute-done.11.earlier = bf16[64,512]{1,0:T(8,128)(2,1)S(1)} collective-permute-done((bf16[64,512]{1,0:T(8,128)(2,1)S(1)}, bf16[64,512]{1,0:T(8,128)(2,1)S(1)}, u32[]{:S(2)}, u32[]{:S(2)}) %collective-permute-start.11) | collective-permute-done | bytes 65568 | tf_op jit(solution)/shard_map/ppermute | solution.py:222
  93.6 0.9 shard_map.80
  94.6 10.6 %all_to_all.15 = bf16[8,2,1536]{2,1,0:T(2,128)(2,1)S(1)} all-to-all(bf16[8,2,1536]{2,1,0:T(2,128)(2,1)S(1)} %reshape.18), channel_id=1, replica_groups=mesh['t'=8,'z'=8,'x'=4,'core'=2] {'z'}, dimensions={0} | all-to-all | bytes 98304 | tf_op jit(solution)/shard_map/all_to_all | solution.py:277
  105.3 0.8 shard_map.81
  (27 shorter events, 2.0 us)
Async XLA Ops:
  0.0 0.9 copy-start.1
  0.9 0.9 copy-start.2
  1.8 11.5 %copy-start = (bf16[2,1,32,384]{3,2,1,0:T(8,128)(2,1)S(1)}, bf16[2,1,32,384]{3,2,1,0:T(8,128)(2,1)}, u32[]{:S(2)}) copy-start(bf16[2,1,32,384]{3,2,1,0:T(8,128)(2,1)} %param.7) | copy-start | bytes 147460
  1.9 11.4 %copy-start.3 = (f32[384]{0:T(512)S(1)}, f32[384]{0:T(512)}, u32[]{:S(2)}) copy-start(f32[384]{0:T(512)} %gain.2) | copy-start | bytes 4612
  1.9 22.6 %collective-permute-start.3 = (bf16[176,384]{1,0:T(8,128)(2,1)S(1)}, bf16[176,384]{1,0:T(8,128)(2,1)S(1)}, u32[]{:S(2)}, u32[]{:S(2)}) collective-permute-start(bf16[176,384]{1,0:T(8,128)(2,1)S(1)} %get-tuple-element.20.rest_0_), channel_id=1, source_target_pairs={{0,2},{2,4},{4,6},{6,0},{1,3},{3,5},{5,7},{7,1},{8,10},{10,12},{12... | collective-permute-start | bytes 405512 | tf_op jit(solution)/shard_map/ppermute | solution.py:227
  5.4 19.2 %collective-permute-start.5 = (bf16[176,384]{1,0:T(8,128)(2,1)S(1)}, bf16[176,384]{1,0:T(8,128)(2,1)S(1)}, u32[]{:S(2)}, u32[]{:S(2)}) collective-permute-start(bf16[176,384]{1,0:T(8,128)(2,1)S(1)} %get-tuple-element.20.rest_0_), channel_id=1, source_target_pairs={{0,4},{2,6},{4,0},{6,2},{1,5},{3,7},{5,1},{7,3},{8,12},{10,14},{12... | collective-permute-start | bytes 405512 | tf_op jit(solution)/shard_map/ppermute | solution.py:227
  10.0 14.6 %collective-permute-start.4 = (bf16[176,384]{1,0:T(8,128)(2,1)S(1)}, bf16[176,384]{1,0:T(8,128)(2,1)S(1)}, u32[]{:S(2)}, u32[]{:S(2)}) collective-permute-start(bf16[176,384]{1,0:T(8,128)(2,1)S(1)} %get-tuple-element.20.rest_0_), channel_id=1, source_target_pairs={{0,6},{2,0},{4,2},{6,4},{1,7},{3,1},{5,3},{7,5},{8,14},{10,8},{12,... | collective-permute-start | bytes 405512 | tf_op jit(solution)/shard_map/ppermute | solution.py:227
  14.3 24.2 %all-to-all-start = ((bf16[8,64,384]{2,1,0:T(8,128)(2,1)}), bf16[8,64,384]{2,1,0:T(8,128)(2,1)S(1)}, u32[]{:S(2)}, u32[]{:S(2)}) async-start(bf16[8,64,384]{2,1,0:T(8,128)(2,1)} %shard_map.74), calls=%async_computation | async-start | bytes 786432 | tf_op jit(solution)/shard_map/all_to_all | solution.py:254
  24.7 10.4 %collective-permute-start.6 = (bf16[4,176,384]{2,1,0:T(8,128)(2,1)S(1)}, bf16[4,176,384]{2,1,0:T(8,128)(2,1)S(1)}, u32[]{:S(2)}, u32[]{:S(2)}) collective-permute-start(bf16[4,176,384]{2,1,0:T(8,128)(2,1)S(1)} %pad_maximum_fusion.1), channel_id=1, source_target_pairs={{0,1},{1,0},{2,3},{3,2},{4,5},{5,4},{6,7},{7,6},{8,9},{9,8},{10,11... | collective-permute-start | bytes 1622024 | tf_op jit(solution)/shard_map/ppermute | solution.py:206
  26.6 24.9 %collective-permute-start.2 = (bf16[176,384]{1,0:T(8,128)(2,1)S(1)}, bf16[176,384]{1,0:T(8,128)(2,1)S(1)}, u32[]{:S(2)}, u32[]{:S(2)}) collective-permute-start(bf16[176,384]{1,0:T(8,128)(2,1)S(1)} %get-tuple-element.19.rest_0_), channel_id=1, source_target_pairs={{0,6},{2,0},{4,2},{6,4},{1,7},{3,1},{5,3},{7,5},{8,14},{10,8},{12,... | collective-permute-start | bytes 405512 | tf_op jit(solution)/shard_map/ppermute | solution.py:227
  28.6 23.0 %collective-permute-start = (bf16[176,384]{1,0:T(8,128)(2,1)S(1)}, bf16[176,384]{1,0:T(8,128)(2,1)S(1)}, u32[]{:S(2)}, u32[]{:S(2)}) collective-permute-start(bf16[176,384]{1,0:T(8,128)(2,1)S(1)} %get-tuple-element.19.rest_0_), channel_id=1, source_target_pairs={{0,2},{2,4},{4,6},{6,0},{1,3},{3,5},{5,7},{7,1},{8,10},{10,12},{12... | collective-permute-start | bytes 405512 | tf_op jit(solution)/shard_map/ppermute | solution.py:227
  32.5 19.1 %collective-permute-start.1 = (bf16[176,384]{1,0:T(8,128)(2,1)S(1)}, bf16[176,384]{1,0:T(8,128)(2,1)S(1)}, u32[]{:S(2)}, u32[]{:S(2)}) collective-permute-start(bf16[176,384]{1,0:T(8,128)(2,1)S(1)} %get-tuple-element.19.rest_0_), channel_id=1, source_target_pairs={{0,4},{2,6},{4,0},{6,2},{1,5},{3,7},{5,1},{7,3},{8,12},{10,14},{12... | collective-permute-start | bytes 405512 | tf_op jit(solution)/shard_map/ppermute | solution.py:227
  40.8 7.5 %collective-permute-start.7 = (bf16[64,1024]{1,0:T(8,128)(2,1)S(1)}, bf16[64,1024]{1,0:T(8,128)(2,1)S(1)}, u32[]{:S(2)}, u32[]{:S(2)}) collective-permute-start(bf16[64,1024]{1,0:T(8,128)(2,1)S(1)} %get-tuple-element.23), channel_id=1, source_target_pairs={{1,2},{2,1},{3,4},{4,3},{5,6},{6,5},{7,0},{0,7},{9,10},{10,9},{11,... | collective-permute-start | bytes 393224 | tf_op jit(solution)/shard_map/ppermute | solution.py:214
  49.0 7.4 %collective-permute-start.8 = (bf16[64,512]{1,0:T(8,128)(2,1)S(1)}, bf16[64,512]{1,0:T(8,128)(2,1)S(1)}, u32[]{:S(2)}, u32[]{:S(2)}) collective-permute-start(bf16[64,512]{1,0:T(8,128)(2,1)S(1)} %get-tuple-element.25), channel_id=1, source_target_pairs={{0,64},{64,128},{128,192},{192,256},{256,320},{320,384},{384,448},... | collective-permute-start | bytes 196616 | tf_op jit(solution)/shard_map/ppermute | solution.py:222
  51.6 4.7 %copy-start.4 = (f32[384]{0:T(512)S(1)}, f32[384]{0:T(512)}, u32[]{:S(2)}) copy-start(f32[384]{0:T(512)} %bias.2) | copy-start | bytes 4612
  57.9 16.7 %copy-start.5 = (f32[384]{0:T(512)S(1)}, f32[384]{0:T(512)}, u32[]{:S(2)}) copy-start(f32[384]{0:T(512)} %gain.3) | copy-start | bytes 4612
  57.9 16.7 %all-to-all-start.1 = ((bf16[8,48,512]{2,1,0:T(8,128)(2,1)}), bf16[8,48,512]{2,1,0:T(8,128)(2,1)S(1)}, u32[]{:S(2)}, u32[]{:S(2)}) async-start(bf16[8,48,512]{2,1,0:T(8,128)(2,1)} %shard_map.77), calls=%async_computation.1 | async-start | bytes 786432 | tf_op jit(solution)/shard_map/all_to_all | solution.py:266
  61.9 3.8 %collective-permute-start.9 = (bf16[4,176,384]{2,1,0:T(8,128)(2,1)S(1)}, bf16[4,176,384]{2,1,0:T(8,128)(2,1)S(1)}, u32[]{:S(2)}, u32[]{:S(2)}) collective-permute-start(bf16[4,176,384]{2,1,0:T(8,128)(2,1)S(1)} %pad_maximum_fusion.after), channel_id=1, source_target_pairs={{0,1},{1,0},{2,3},{3,2},{4,5},{5,4},{6,7},{7,6},{8,9},{9,8},{10,11... | collective-permute-start | bytes 1622024 | tf_op jit(solution)/shard_map/ppermute | solution.py:206
  77.0 8.5 %collective-permute-start.10 = (bf16[64,1024]{1,0:T(8,128)(2,1)S(1)}, bf16[64,1024]{1,0:T(8,128)(2,1)S(1)}, u32[]{:S(2)}, u32[]{:S(2)}) collective-permute-start(bf16[64,1024]{1,0:T(8,128)(2,1)S(1)} %get-tuple-element.28), channel_id=1, source_target_pairs={{1,2},{2,1},{3,4},{4,3},{5,6},{6,5},{7,0},{0,7},{9,10},{10,9},{11,... | collective-permute-start | bytes 393224 | tf_op jit(solution)/shard_map/ppermute | solution.py:214
  86.2 7.4 %copy-start.6 = (f32[384]{0:T(512)S(1)}, f32[384]{0:T(512)}, u32[]{:S(2)}) copy-start(f32[384]{0:T(512)} %bias.3) | copy-start | bytes 4612
  86.2 7.4 %collective-permute-start.11 = (bf16[64,512]{1,0:T(8,128)(2,1)S(1)}, bf16[64,512]{1,0:T(8,128)(2,1)S(1)}, u32[]{:S(2)}, u32[]{:S(2)}) collective-permute-start(bf16[64,512]{1,0:T(8,128)(2,1)S(1)} %get-tuple-element.30), channel_id=1, source_target_pairs={{0,64},{64,128},{128,192},{192,256},{256,320},{320,384},{384,448},... | collective-permute-start | bytes 196616 | tf_op jit(solution)/shard_map/ppermute | solution.py:222

commit v4 on v3

--- a/solution.py
+++ b/solution.py
@@ -8,7 +8,6 @@
 
 CHANNELS = 384
 BLOCK = 48
-PIECE = 176
 SLOT = 224
 LANES = 512
 VMEM = 48 * 1024 * 1024
@@ -16,8 +15,9 @@
 BF16 = jnp.bfloat16
 
 
-def call(kernel, out_shape, scratch=(), smem=0, anywhere=0, n=0, flops=0):
+def call(kernel, out_shape, scratch=(), smem=0, hbm=0, anywhere=0, n=0, vmem_limit=VMEM):
     specs = [pl.BlockSpec(memory_space=pltpu.SMEM)] * smem
+    specs += [pl.BlockSpec(memory_space=pltpu.HBM)] * hbm
     specs += [pl.BlockSpec(memory_space=pl.ANY)] * anywhere
     specs += [pl.BlockSpec(memory_space=pltpu.VMEM)] * (n - len(specs))
     multiple = isinstance(out_shape, (list, tuple))
@@ -28,8 +28,7 @@
         in_specs=specs,
         out_specs=[vmem] * len(out_shape) if multiple else vmem,
         scratch_shapes=list(scratch),
-        compiler_params=pltpu.CompilerParams(vmem_limit_bytes=VMEM),
-        cost_estimate=pl.CostEstimate(flops=flops, bytes_accessed=0, transcendentals=0),
+        compiler_params=pltpu.CompilerParams(vmem_limit_bytes=vmem_limit),
     )
 
 
@@ -45,7 +44,27 @@
     return v / (1.0 + jnp.exp(-v))
 
 
-def norm_kernel(latent, gain, hidden):
+def first_kernel(
+    latent_hbm, one_hbm, two_hbm, gain_hbm, hidden, piece_one, piece_two, pieces, latent, gain, weights, rows, sems
+):
+    copies = [
+        pltpu.make_async_copy(one_hbm, weights.at[0], sems.at[0]),
+        pltpu.make_async_copy(two_hbm, weights.at[1], sems.at[1]),
+        pltpu.make_async_copy(latent_hbm, latent, sems.at[2]),
+        pltpu.make_async_copy(gain_hbm, gain, sems.at[3]),
+    ]
+    for copy in copies:
+        copy.start()
+    rows[...] = jnp.zeros_like(rows)
+    for conv, piece in enumerate((piece_one, piece_two)):
+        copies[conv].wait()
+        for tap in range(27):
+            rows[8 * tap : 8 * tap + 6, :] = weights[conv, tap].astype(F32)
+        packed = rows[...].astype(BF16)
+        piece[...] = packed
+        pieces[conv] = packed
+    copies[2].wait()
+    copies[3].wait()
     values = latent[...].astype(F32)
     mean = jnp.mean(values * values, axis=1, keepdims=True)
     scale = lax.rsqrt(mean + 1e-6) * gain[...].reshape(1, CHANNELS)
@@ -54,27 +73,21 @@
         hidden[z] = result
 
 
-def prepare_kernel(weight_one, weight_two, piece_one, piece_two, rows):
-    for weight, piece in ((weight_one, piece_one), (weight_two, piece_two)):
-        for tap in range(27):
-            rows[6 * tap : 6 * tap + 6, :] = weight[tap].astype(F32)
-        rows[162:PIECE, :] = jnp.zeros((PIECE - 162, CHANNELS), F32)
-        piece[...] = rows[...].astype(BF16)
-
-
-def place_weights(ids, own, ahead, behind, across, swapped, whole):
+def place_weights(conv, ids, both, near, far, swapped, whole):
     x, c = ids[1], ids[2]
-    row = iota((SLOT, PIECE), 0)
-    wanted = (iota((SLOT, PIECE), 1) == 6 * (row // 8) + lax.rem(row, 8)) & (lax.rem(row, 8) < 6)
-    spread = wanted.astype(F32).astype(BF16)
 
     def place(position, value):
-        whole[position] = jnp.dot(spread, value, preferred_element_type=F32).astype(BF16)
-
-    for shift, piece in ((0, own), (1, ahead), (2, across), (3, behind)):
-        position = lax.rem(x + 4 - shift, 4) * 2
-        place(position + c, piece[...])
-        place(position + 1 - c, swapped[shift])
+        whole[position] = value
+
+    chip = jnp.bitwise_xor(x, 1 + 2 * c)
+    other = jnp.bitwise_xor(x, 3 - 2 * c)
+    across = jnp.bitwise_xor(x, 2)
+    for i in range(2):
+        place(2 * x + i, both[i])
+        place(2 * chip + i, near[i])
+        place(2 * other + i, swapped[i])
+    place(2 * across + c, far[conv])
+    place(2 * across + 1 - c, swapped[2])
 
 
 def taps(ids, products, keep, partner, pair):
@@ -110,7 +123,7 @@
 
 def conv_one_kernel(ids, gathered, *rest):
     *pieces, keep, partner, pair, whole, field, products = rest
-    place_weights(ids, *pieces, whole)
+    place_weights(0, ids, *pieces, whole)
     for z in range(8):
         for f in range(2):
             field[pl.ds(256 * f + 32 * z, 32), :] = gathered[z, pl.ds(32 * f, 32), :]
@@ -125,7 +138,7 @@
 
 def conv_two_kernel(ids, gathered, gain, *rest):
     *pieces, keep, partner, pair, whole, products = rest
-    place_weights(ids, *pieces, whole)
+    place_weights(1, ids, *pieces, whole)
     values = gathered[...].reshape(CHANNELS, LANES).astype(F32)
     mean = jnp.mean(values * values, axis=0, keepdims=True)
     square = (CHANNELS, CHANNELS)
@@ -184,21 +197,29 @@
 
 def spread_kernel(ids, own, earlier, bias, latent, pieces, kept):
     result = block_values(ids, own, earlier, bias)
+    result = result.astype(F32)
     for z in range(8):
-        frames = [result[:, 256 * f + 32 * z : 256 * f + 32 * z + 32] for f in range(2)]
-        pieces[z] = jnp.concatenate(frames, axis=1)
+        parts = []
+        for first in (0, 24):
+            for f in range(2):
+                at = 256 * f + 32 * z
+                parts.append(result[first : first + 24, at : at + 32])
+        pieces[z] = jnp.concatenate(parts, axis=1).astype(BF16)
     kept[...] = latent[...]
 
 
 def finish_kernel(latent, gathered, out):
-    square = (CHANNELS, CHANNELS)
-    same = iota(square, 0) == iota(square, 1)
-    conv = lax.dot_general(
-        gathered[...].reshape(CHANNELS, 64),
-        same.astype(BF16),
-        (((0,), (0,)), ((), ())),
-        preferred_element_type=F32,
-    )
+    halves = gathered[...].reshape(8 * 24, 128)
+    frm, to = iota((8 * 24, CHANNELS), 0), iota((8 * 24, CHANNELS), 1)
+    conv = jnp.zeros((64, CHANNELS), F32)
+    for half in range(2):
+        pick = (to == BLOCK * (frm // 24) + lax.rem(frm, 24) + 24 * half).astype(F32).astype(BF16)
+        conv += lax.dot_general(
+            halves[:, 64 * half : 64 * half + 64],
+            pick,
+            (((0,), (0,)), ((), ())),
+            preferred_element_type=F32,
+        )
     out[...] = (latent[...].astype(F32) + conv).astype(BF16)
 
 
@@ -222,12 +243,17 @@
     return own, lax.ppermute(later, "t", [(i, i + 1) for i in range(7)])
 
 
-def gather_weights(piece):
-    one, two, three = [
-        lax.ppermute(piece, "x", [(i, (i + by) % 4) for i in range(4)]) for by in (1, 2, 3)
-    ]
-    packed = jnp.stack([piece, one, two, three])
-    return (piece, one, three, two), packed
+def gather_weights(piece_one, piece_two, pieces):
+    hops = []
+    for x in range(4):
+        hops += [(2 * x, 2 * (x ^ 1)), (2 * x + 1, 2 * (x ^ 3) + 1)]
+    far = lax.ppermute(pieces, "x", [(x, x ^ 2) for x in range(4)])
+    result = []
+    for conv, piece in enumerate((piece_one, piece_two)):
+        both = lax.all_gather(piece, "core", axis=0)
+        near = lax.ppermute(both, ("x", "core"), hops)
+        result.append(((both, near, far), jnp.concatenate([near, far[conv : conv + 1]])))
+    return result
 
 
 def per_device(latent, gain_one, weight_one, bias_one, gain_two, weight_two, bias_two):
@@ -237,7 +263,7 @@
         jnp.transpose(w, (0, 1, 2, 4, 3)).reshape(27, 6, CHANNELS)
         for w in (weight_one, weight_two)
     ]
-    piece = shape((PIECE, CHANNELS), BF16)
+    piece = shape((SLOT, CHANNELS), BF16)
     sums = [
         shape((64, 2 * LANES), F32),
         shape((64, 2 * LANES), BF16),
@@ -246,31 +272,46 @@
     whole = pltpu.VMEM((8, SLOT, CHANNELS), BF16)
     products = pltpu.VMEM((8 * SLOT, LANES), F32)
 
-    hidden = call(norm_kernel, shape((8, 64, CHANNELS), BF16), n=2)(latent, gain_one)
-    pieces = call(prepare_kernel, [piece, piece], [pltpu.VMEM((PIECE, CHANNELS), F32)], n=2)(
-        weight_one, weight_two
-    )
-    (weights_one, packed_one), (weights_two, packed_two) = [gather_weights(p) for p in pieces]
+    hidden, *pieces = call(
+        first_kernel,
+        [
+            shape((8, 64, CHANNELS), BF16),
+            piece,
+            piece,
+            shape((2, SLOT, CHANNELS), BF16),
+        ],
+        [
+            pltpu.VMEM((64, CHANNELS), BF16),
+            pltpu.VMEM((CHANNELS,), F32),
+            pltpu.VMEM((2, 27, 6, CHANNELS), BF16),
+            pltpu.VMEM((SLOT, CHANNELS), F32),
+            pltpu.SemaphoreType.DMA((4,)),
+        ],
+        hbm=4,
+        n=4,
+        vmem_limit=60 * 1024 * 1024,
+    )(latent, weight_one, weight_two, gain_one)
+    (weights_one, packed_one), (weights_two, packed_two) = gather_weights(*pieces)
     gathered = lax.all_to_all(hidden, "z", 0, 0)
     sums_one = call(
         conv_one_kernel,
         sums,
         [whole, pltpu.VMEM((LANES, CHANNELS), BF16), products],
         smem=1,
-        n=7,
+        n=6,
     )(ids, gathered, *weights_one, swap_cores(packed_one))
     own, earlier = exchange(ids, *sums_one)
     middle = call(middle_kernel, shape((8, BLOCK, LANES), BF16), smem=1, anywhere=1, n=5)(
         ids, packed_two, own, earlier, bias_one
     )
     gathered = lax.all_to_all(middle, "z", 0, 0)
-    sums_two = call(conv_two_kernel, sums, [whole, products], smem=1, n=8)(
+    sums_two = call(conv_two_kernel, sums, [whole, products], smem=1, n=7)(
         ids, gathered, gain_two, *weights_two, swap_cores(packed_two)
     )
     own, earlier = exchange(ids, *sums_two)
     pieces, kept = call(
         spread_kernel,
-        [shape((8, BLOCK, 64), BF16), shape((64, CHANNELS), BF16)],
+        [shape((8, 24, 128), BF16), shape((64, CHANNELS), BF16)],
         smem=1,
         n=5,
     )(ids, own, earlier, bias_two, latent)

time: 107 us -> 104 us (0.972)
  starting transfers between devices: 50.2 us -> 40.3 us
  waiting for transfers between devices: 28 us -> 32.6 us
  blocking collectives: 14.9 us -> 18.9 us
  local copies, waits for them, and re-layouts: 2.11 us -> 0.06 us
    ppermute x6 -> x3, starting transfers between devices: 19.8 us -> 10.7 us  [the longest x2 5.81 us: gather_weights(): near = lax.ppermute(both, ('x', 'core'), hops)]
    all_gather x0 -> x2, blocking collectives: none -> 4.32 us  [gather_weights(): both = lax.all_gather(piece, 'core', axis=0)]
    all_to_all x1, waiting for transfers between devices: 3.29 us -> 7.6 us  [per_device(): gathered = lax.all_to_all(hidden, 'z', 0, 0)]
    unnamed x16 -> x10, local copies, waits for them, and re-layouts: 2.11 us -> 0.02 us
    pallas_call x4 -> x3, Pallas kernels: 4.3 us -> 5.07 us  [the longest x1 2.12 us: per_device(): call(first_kernel, [shape((8, 64, CHANNELS), BF16), piece, piece, shape((...]
  transfers between devices with their start and end apart: 14 -> 11, of which waited for: 7 -> 7; matrix products, arithmetic and copies ran while one was open for 0% -> 0% of each run, Pallas kernels for 4% -> 2%
where the time goes in v4:
time: 104 us; the launch traced here: 103 us
  starting transfers between devices  40.3 us (39%)
  waiting for transfers between devices  32.6 us (31%)
  blocking collectives  18.9 us (18%)
  Pallas kernels  10.7 us (10%)
    all_to_all x1, blocking collectives, per_device(): pieces = lax.all_to_all(pieces, 'z', 0, 0)  10.6 us
    all_to_all x1, starting transfers between devices, per_device(): gathered = lax.all_to_all(hidden, 'z', 0, 0)  10.3 us
    ppermute x2, waiting for transfers between devices, exchange(): return (own, lax.ppermute(later, 't', [(i, i + 1) for i in range(7)]))  10.1 us
    all_to_all x1, waiting for transfers between devices, per_device(): gathered = lax.all_to_all(middle, 'z', 0, 0)  9.14 us
    all_to_all x1, waiting for transfers between devices, per_device(): gathered = lax.all_to_all(hidden, 'z', 0, 0)  7.6 us
    ppermute x2, starting transfers between devices, exchange(): pair = lax.ppermute(pair, ('x', 'core'), swaps)  7.14 us
    ppermute x2, starting transfers between devices, gather_weights(): near = lax.ppermute(both, ('x', 'core'), hops)  5.81 us
    ppermute x1, starting transfers between devices, gather_weights(): far = lax.ppermute(pieces, 'x', [(x, x ^ 2) for x in range(4)])  4.93 us
  transfers between devices with their start and end apart: 11, of which 7 were waited for; matrix products, arithmetic and copies ran while one was open for 0% of the time, Pallas kernels for 2%

profile of v4, /device:TPU:32, one launch (start us, length us, event | category | flops | bytes accessed | tf_op | source)
XLA Modules:
  0.0 103.0 jit_solution(15977288588857025078)
XLA Ops:
  0.0 2.1 %shard_map.73 = (bf16[8,64,384]{2,1,0:T(8,128)(2,1)}, bf16[224,384]{1,0:T(8,128)(2,1)}, bf16[224,384]{1,0:T(8,128)(2,1)}, bf16[2,224,384]{2,1,0:T(8,128)(2,1)}) custom-call(bf16[64,384]{1,0:T(8,128)(2,1)} %bitcast.23, bf16[27,6,384]{2,1,0:T(8,128)(2,1)} %bitcast.25, bf16[27,6,384]{2,1,0:T(8,128)(2,1)} %bitcast.26, f32[384]{0:T(512)} %gain_hbm.1), custom_call_target="tpu_custom_call" | custom-call | tf_op jit(solution)/shard_map/pallas_call | solution.py:275
  2.1 4.9 %collective-permute-start.1 = (bf16[2,224,384]{2,1,0:T(8,128)(2,1)}, bf16[2,224,384]{2,1,0:T(8,128)(2,1)S(1)}, u32[]{:S(2)}, u32[]{:S(2)}) collective-permute-start(bf16[2,224,384]{2,1,0:T(8,128)(2,1)} %get-tuple-element.22), channel_id=1, source_target_pairs={{0,4},{2,6},{4,0},{6,2},{1,5},{3,7},{5,1},{7,3},{8,12},{10,14},{12... | collective-permute-start | bytes 1032200 | tf_op jit(solution)/shard_map/ppermute | solution.py:250
  7.1 2.3 %all-gather.1 = bf16[448,384]{1,0:T(8,128)(2,1)S(1)} all-gather(bf16[224,384]{1,0:T(8,128)(2,1)} %get-tuple-element.24), channel_id=3, replica_groups=mesh['t'=8,'z'=8,'x'=4,'core'=2] {'core'}, dimensions={0}, use_global_device_ids=true | all-gather | bytes 516096 | tf_op jit(solution)/shard_map/all_gather | solution.py:253
  9.3 2.5 %collective-permute-start.2 = (bf16[2,224,384]{2,1,0:T(8,128)(2,1)S(1)}, bf16[2,224,384]{2,1,0:T(8,128)(2,1)S(1)}, u32[]{:S(2)}, u32[]{:S(2)}) collective-permute-start(bf16[2,224,384]{2,1,0:T(8,128)(2,1)S(1)} %bitcast.19), channel_id=1, source_target_pairs={{0,2},{1,7},{2,0},{3,5},{4,6},{5,3},{6,4},{7,1},{8,10},{9,15},{10,... | collective-permute-start | bytes 1032200 | tf_op jit(solution)/shard_map/ppermute | solution.py:254
  11.8 10.3 %all-to-all-start = ((bf16[8,64,384]{2,1,0:T(8,128)(2,1)}), bf16[8,64,384]{2,1,0:T(8,128)(2,1)S(1)}, u32[]{:S(2)}, u32[]{:S(2)}) async-start(bf16[8,64,384]{2,1,0:T(8,128)(2,1)} %get-tuple-element.23), calls=%async_computation | async-start | bytes 786432 | tf_op jit(solution)/shard_map/all_to_all | solution.py:295
  22.3 2.1 %collective-permute-start.3 = (bf16[3,224,384]{2,1,0:T(8,128)(2,1)S(1)}, bf16[3,224,384]{2,1,0:T(8,128)(2,1)S(1)}, u32[]{:S(2)}, u32[]{:S(2)}) collective-permute-start(bf16[3,224,384]{2,1,0:T(8,128)(2,1)S(1)} %pad_maximum_fusion.1), channel_id=1, source_target_pairs={{0,1},{1,0},{2,3},{3,2},{4,5},{5,4},{6,7},{7,6},{8,9},{9,8},{10,11... | collective-permute-start | bytes 1548296 | tf_op jit(solution)/shard_map/ppermute | solution.py:227
  24.4 2.1 %all-gather = bf16[448,384]{1,0:T(8,128)(2,1)S(1)} all-gather(bf16[224,384]{1,0:T(8,128)(2,1)S(1)} %copy-done.4), channel_id=2, replica_groups=mesh['t'=8,'z'=8,'x'=4,'core'=2] {'core'}, dimensions={0}, use_global_device_ids=true | all-gather | bytes 516096 | tf_op jit(solution)/shard_map/all_gather | solution.py:253
  26.4 3.3 %collective-permute-start = (bf16[2,224,384]{2,1,0:T(8,128)(2,1)S(1)}, bf16[2,224,384]{2,1,0:T(8,128)(2,1)S(1)}, u32[]{:S(2)}, u32[]{:S(2)}) collective-permute-start(bf16[2,224,384]{2,1,0:T(8,128)(2,1)S(1)} %bitcast.17), channel_id=1, source_target_pairs={{0,2},{1,7},{2,0},{3,5},{4,6},{5,3},{6,4},{7,1},{8,10},{9,15},{10,... | collective-permute-start | bytes 1032200 | tf_op jit(solution)/shard_map/ppermute | solution.py:254
  29.8 0.1 pad_add_fusion.ids
  29.8 7.6 %all-to-all-done.gathered = bf16[8,64,384]{2,1,0:T(8,128)(2,1)S(1)} async-done(((bf16[8,64,384]{2,1,0:T(8,128)(2,1)}), bf16[8,64,384]{2,1,0:T(8,128)(2,1)S(1)}, u32[]{:S(2)}, u32[]{:S(2)}) %all-to-all-start) | async-done | bytes 393248 | tf_op jit(solution)/shard_map/all_to_all | solution.py:295
  37.4 1.8 %shard_map.74 = (f32[64,1024]{1,0:T(8,128)S(1)}, bf16[64,1024]{1,0:T(8,128)(2,1)S(1)}, bf16[64,1024]{1,0:T(8,128)(2,1)S(1)}) custom-call(s32[3]{0:T(128)S(1)} %pad_add_fusion.ids, bf16[8,64,384]{2,1,0:T(8,128)(2,1)S(1)} %all-to-all-done.gathered, bf16[2,224,384]{2,1,0:T(8,128)(2,1)S(1)} %bitcast.20, bf16[2,224,384]{2,1,0:T(8,128)(2,1)S(1)} %collective-permute-done.2.rest_1_, ...), custom_call_target="tpu_custom_call" | custom-call | tf_op jit(solution)/shard_map/pallas_call | solution.py:296
  39.3 2.9 %collective-permute-start.4 = (bf16[64,1024]{1,0:T(8,128)(2,1)S(1)}, bf16[64,1024]{1,0:T(8,128)(2,1)S(1)}, u32[]{:S(2)}, u32[]{:S(2)}) collective-permute-start(bf16[64,1024]{1,0:T(8,128)(2,1)S(1)} %get-tuple-element.27), channel_id=1, source_target_pairs={{1,2},{2,1},{3,4},{4,3},{5,6},{6,5},{7,0},{0,7},{9,10},{10,9},{11,... | collective-permute-start | bytes 393224 | tf_op jit(solution)/shard_map/ppermute | solution.py:235
  42.2 2.0 %all-gather.2 = bf16[128,1024]{1,0:T(8,128)(2,1)S(1)} all-gather(bf16[64,1024]{1,0:T(8,128)(2,1)S(1)} %get-tuple-element.26), channel_id=4, replica_groups=mesh['t'=8,'z'=8,'x'=4,'core'=2] {'core'}, dimensions={0}, use_global_device_ids=true | all-gather | bytes 393216 | tf_op jit(solution)/shard_map/all_gather | solution.py:236
  44.2 2.6 %collective-permute-done.4.pair = bf16[64,1024]{1,0:T(8,128)(2,1)S(1)} collective-permute-done((bf16[64,1024]{1,0:T(8,128)(2,1)S(1)}, bf16[64,1024]{1,0:T(8,128)(2,1)S(1)}, u32[]{:S(2)}, u32[]{:S(2)}) %collective-permute-start.4) | collective-permute-done | bytes 131104 | tf_op jit(solution)/shard_map/ppermute | solution.py:235
  46.8 0.7 shard_map.75
  47.5 2.6 %collective-permute-start.5 = (bf16[64,512]{1,0:T(8,128)(2,1)S(1)}, bf16[64,512]{1,0:T(8,128)(2,1)S(1)}, u32[]{:S(2)}, u32[]{:S(2)}) collective-permute-start(bf16[64,512]{1,0:T(8,128)(2,1)S(1)} %get-tuple-element.29), channel_id=1, source_target_pairs={{0,64},{64,128},{128,192},{192,256},{256,320},{320,384},{384,448},... | collective-permute-start | bytes 196616 | tf_op jit(solution)/shard_map/ppermute | solution.py:243
  50.2 4.7 %collective-permute-done.5.earlier = bf16[64,512]{1,0:T(8,128)(2,1)S(1)} collective-permute-done((bf16[64,512]{1,0:T(8,128)(2,1)S(1)}, bf16[64,512]{1,0:T(8,128)(2,1)S(1)}, u32[]{:S(2)}, u32[]{:S(2)}) %collective-permute-start.5) | collective-permute-done | bytes 65568 | tf_op jit(solution)/shard_map/ppermute | solution.py:243
  54.9 1.5 %shard_map.76 = bf16[8,48,512]{2,1,0:T(8,128)(2,1)} custom-call(s32[3]{0:T(128)S(1)} %pad_add_fusion.ids, bf16[3,224,384]{2,1,0:T(8,128)(2,1)S(1)} %pad_maximum_fusion.after, f32[64,512]{1,0:T(8,128)S(1)} %get-tuple-element.28.own, bf16[64,512]{1,0:T(8,128)(2,1)S(1)} %collective-permute-done.5.earlier, f32[384]{0:T(512)S(1)} %copy-done.1), custom_call_target="tpu_custom_call" | custom-call | tf_op jit(solution)/shard_map/pallas_call | solution.py:304
  56.4 3.6 %all-to-all-start.1 = ((bf16[8,48,512]{2,1,0:T(8,128)(2,1)}), bf16[8,48,512]{2,1,0:T(8,128)(2,1)S(1)}, u32[]{:S(2)}, u32[]{:S(2)}) async-start(bf16[8,48,512]{2,1,0:T(8,128)(2,1)} %shard_map.76), calls=%async_computation.1 | async-start | bytes 786432 | tf_op jit(solution)/shard_map/all_to_all | solution.py:307
  60.0 1.9 %collective-permute-start.6 = (bf16[3,224,384]{2,1,0:T(8,128)(2,1)S(1)}, bf16[3,224,384]{2,1,0:T(8,128)(2,1)S(1)}, u32[]{:S(2)}, u32[]{:S(2)}) collective-permute-start(bf16[3,224,384]{2,1,0:T(8,128)(2,1)S(1)} %pad_maximum_fusion.after), channel_id=1, source_target_pairs={{0,1},{1,0},{2,3},{3,2},{4,5},{5,4},{6,7},{7,6},{8,9},{9,8},{10,11... | collective-permute-start | bytes 1548296 | tf_op jit(solution)/shard_map/ppermute | solution.py:227
  61.9 1.9 %collective-permute-done.6.rest_3_ = bf16[3,224,384]{2,1,0:T(8,128)(2,1)S(1)} collective-permute-done((bf16[3,224,384]{2,1,0:T(8,128)(2,1)S(1)}, bf16[3,224,384]{2,1,0:T(8,128)(2,1)S(1)}, u32[]{:S(2)}, u32[]{:S(2)}) %collective-permute-start.6) | collective-permute-done | bytes 516128 | tf_op jit(solution)/shard_map/ppermute | solution.py:227
  63.8 9.1 %all-to-all-done.1.gathered = bf16[8,48,512]{2,1,0:T(8,128)(2,1)S(1)} async-done(((bf16[8,48,512]{2,1,0:T(8,128)(2,1)}), bf16[8,48,512]{2,1,0:T(8,128)(2,1)S(1)}, u32[]{:S(2)}, u32[]{:S(2)}) %all-to-all-start.1) | async-done | bytes 393248 | tf_op jit(solution)/shard_map/all_to_all | solution.py:307
  72.9 2.1 %shard_map.77 = (f32[64,1024]{1,0:T(8,128)S(1)}, bf16[64,1024]{1,0:T(8,128)(2,1)S(1)}, bf16[64,1024]{1,0:T(8,128)(2,1)S(1)}) custom-call(s32[3]{0:T(128)S(1)} %pad_add_fusion.ids, bf16[8,48,512]{2,1,0:T(8,128)(2,1)S(1)} %all-to-all-done.1.gathered, f32[384]{0:T(512)S(1)} %copy-done.2, bf16[2,224,384]{2,1,0:T(8,128)(2,1)S(1)} %bitcast.18, ...), custom_call_target="tpu_custom_call" | custom-call | tf_op jit(solution)/shard_map/pallas_call | solution.py:308
  75.0 4.2 %collective-permute-start.7 = (bf16[64,1024]{1,0:T(8,128)(2,1)S(1)}, bf16[64,1024]{1,0:T(8,128)(2,1)S(1)}, u32[]{:S(2)}, u32[]{:S(2)}) collective-permute-start(bf16[64,1024]{1,0:T(8,128)(2,1)S(1)} %get-tuple-element.32), channel_id=1, source_target_pairs={{1,2},{2,1},{3,4},{4,3},{5,6},{6,5},{7,0},{0,7},{9,10},{10,9},{11,... | collective-permute-start | bytes 393224 | tf_op jit(solution)/shard_map/ppermute | solution.py:235
  79.2 2.0 %all-gather.3 = bf16[128,1024]{1,0:T(8,128)(2,1)S(1)} all-gather(bf16[64,1024]{1,0:T(8,128)(2,1)S(1)} %get-tuple-element.31), channel_id=5, replica_groups=mesh['t'=8,'z'=8,'x'=4,'core'=2] {'core'}, dimensions={0}, use_global_device_ids=true | all-gather | bytes 393216 | tf_op jit(solution)/shard_map/all_gather | solution.py:236
  81.2 1.3 %collective-permute-done.7.pair = bf16[64,1024]{1,0:T(8,128)(2,1)S(1)} collective-permute-done((bf16[64,1024]{1,0:T(8,128)(2,1)S(1)}, bf16[64,1024]{1,0:T(8,128)(2,1)S(1)}, u32[]{:S(2)}, u32[]{:S(2)}) %collective-permute-start.7) | collective-permute-done | bytes 131104 | tf_op jit(solution)/shard_map/ppermute | solution.py:235
  82.5 0.7 shard_map.78
  83.2 1.9 %collective-permute-start.8 = (bf16[64,512]{1,0:T(8,128)(2,1)S(1)}, bf16[64,512]{1,0:T(8,128)(2,1)S(1)}, u32[]{:S(2)}, u32[]{:S(2)}) collective-permute-start(bf16[64,512]{1,0:T(8,128)(2,1)S(1)} %get-tuple-element.34), channel_id=1, source_target_pairs={{0,64},{64,128},{128,192},{192,256},{256,320},{320,384},{384,448},... | collective-permute-start | bytes 196616 | tf_op jit(solution)/shard_map/ppermute | solution.py:243
  85.2 5.4 %collective-permute-done.8.earlier = bf16[64,512]{1,0:T(8,128)(2,1)S(1)} collective-permute-done((bf16[64,512]{1,0:T(8,128)(2,1)S(1)}, bf16[64,512]{1,0:T(8,128)(2,1)S(1)}, u32[]{:S(2)}, u32[]{:S(2)}) %collective-permute-start.8) | collective-permute-done | bytes 65568 | tf_op jit(solution)/shard_map/ppermute | solution.py:243
  90.6 0.9 shard_map.79
  91.5 10.6 %all_to_all.15.gathered = bf16[8,24,128]{2,1,0:T(8,128)(2,1)S(1)} all-to-all(bf16[8,24,128]{2,1,0:T(8,128)(2,1)S(1)} %get-tuple-element.36), channel_id=1, replica_groups=mesh['t'=8,'z'=8,'x'=4,'core'=2] {'z'}, dimensions={0} | all-to-all | bytes 98304 | tf_op jit(solution)/shard_map/all_to_all | solution.py:318
  102.0 0.9 shard_map.80
  (17 shorter events, 0.2 us)
Async XLA Ops:
  2.1 20.0 %collective-permute-start.1 = (bf16[2,224,384]{2,1,0:T(8,128)(2,1)}, bf16[2,224,384]{2,1,0:T(8,128)(2,1)S(1)}, u32[]{:S(2)}, u32[]{:S(2)}) collective-permute-start(bf16[2,224,384]{2,1,0:T(8,128)(2,1)} %get-tuple-element.22), channel_id=1, source_target_pairs={{0,4},{2,6},{4,0},{6,2},{1,5},{3,7},{5,1},{7,3},{8,12},{10,14},{12... | collective-permute-start | bytes 1032200 | tf_op jit(solution)/shard_map/ppermute | solution.py:250
  9.3 12.9 %collective-permute-start.2 = (bf16[2,224,384]{2,1,0:T(8,128)(2,1)S(1)}, bf16[2,224,384]{2,1,0:T(8,128)(2,1)S(1)}, u32[]{:S(2)}, u32[]{:S(2)}) collective-permute-start(bf16[2,224,384]{2,1,0:T(8,128)(2,1)S(1)} %bitcast.19), channel_id=1, source_target_pairs={{0,2},{1,7},{2,0},{3,5},{4,6},{5,3},{6,4},{7,1},{8,10},{9,15},{10,... | collective-permute-start | bytes 1032200 | tf_op jit(solution)/shard_map/ppermute | solution.py:254
  11.8 25.6 %all-to-all-start = ((bf16[8,64,384]{2,1,0:T(8,128)(2,1)}), bf16[8,64,384]{2,1,0:T(8,128)(2,1)S(1)}, u32[]{:S(2)}, u32[]{:S(2)}) async-start(bf16[8,64,384]{2,1,0:T(8,128)(2,1)} %get-tuple-element.23), calls=%async_computation | async-start | bytes 786432 | tf_op jit(solution)/shard_map/all_to_all | solution.py:295
  22.2 2.1 %copy-start.4 = (bf16[224,384]{1,0:T(8,128)(2,1)S(1)}, bf16[224,384]{1,0:T(8,128)(2,1)}, u32[]{:S(2)}) copy-start(bf16[224,384]{1,0:T(8,128)(2,1)} %get-tuple-element.21) | copy-start | bytes 516100
  22.3 15.1 %collective-permute-start.3 = (bf16[3,224,384]{2,1,0:T(8,128)(2,1)S(1)}, bf16[3,224,384]{2,1,0:T(8,128)(2,1)S(1)}, u32[]{:S(2)}, u32[]{:S(2)}) collective-permute-start(bf16[3,224,384]{2,1,0:T(8,128)(2,1)S(1)} %pad_maximum_fusion.1), channel_id=1, source_target_pairs={{0,1},{1,0},{2,3},{3,2},{4,5},{5,4},{6,7},{7,6},{8,9},{9,8},{10,11... | collective-permute-start | bytes 1548296 | tf_op jit(solution)/shard_map/ppermute | solution.py:227
  26.4 23.7 %collective-permute-start = (bf16[2,224,384]{2,1,0:T(8,128)(2,1)S(1)}, bf16[2,224,384]{2,1,0:T(8,128)(2,1)S(1)}, u32[]{:S(2)}, u32[]{:S(2)}) collective-permute-start(bf16[2,224,384]{2,1,0:T(8,128)(2,1)S(1)} %bitcast.17), channel_id=1, source_target_pairs={{0,2},{1,7},{2,0},{3,5},{4,6},{5,3},{6,4},{7,1},{8,10},{9,15},{10,... | collective-permute-start | bytes 1032200 | tf_op jit(solution)/shard_map/ppermute | solution.py:254
  39.3 7.5 %collective-permute-start.4 = (bf16[64,1024]{1,0:T(8,128)(2,1)S(1)}, bf16[64,1024]{1,0:T(8,128)(2,1)S(1)}, u32[]{:S(2)}, u32[]{:S(2)}) collective-permute-start(bf16[64,1024]{1,0:T(8,128)(2,1)S(1)} %get-tuple-element.27), channel_id=1, source_target_pairs={{1,2},{2,1},{3,4},{4,3},{5,6},{6,5},{7,0},{0,7},{9,10},{10,9},{11,... | collective-permute-start | bytes 393224 | tf_op jit(solution)/shard_map/ppermute | solution.py:235
  47.5 7.4 %collective-permute-start.5 = (bf16[64,512]{1,0:T(8,128)(2,1)S(1)}, bf16[64,512]{1,0:T(8,128)(2,1)S(1)}, u32[]{:S(2)}, u32[]{:S(2)}) collective-permute-start(bf16[64,512]{1,0:T(8,128)(2,1)S(1)} %get-tuple-element.29), channel_id=1, source_target_pairs={{0,64},{64,128},{128,192},{192,256},{256,320},{320,384},{384,448},... | collective-permute-start | bytes 196616 | tf_op jit(solution)/shard_map/ppermute | solution.py:243
  50.1 4.8 %copy-start.1 = (f32[384]{0:T(512)S(1)}, f32[384]{0:T(512)}, u32[]{:S(2)}) copy-start(f32[384]{0:T(512)} %bias.2) | copy-start | bytes 4612
  56.4 16.5 %copy-start.2 = (f32[384]{0:T(512)S(1)}, f32[384]{0:T(512)}, u32[]{:S(2)}) copy-start(f32[384]{0:T(512)} %gain.1) | copy-start | bytes 4612
  56.4 16.5 %all-to-all-start.1 = ((bf16[8,48,512]{2,1,0:T(8,128)(2,1)}), bf16[8,48,512]{2,1,0:T(8,128)(2,1)S(1)}, u32[]{:S(2)}, u32[]{:S(2)}) async-start(bf16[8,48,512]{2,1,0:T(8,128)(2,1)} %shard_map.76), calls=%async_computation.1 | async-start | bytes 786432 | tf_op jit(solution)/shard_map/all_to_all | solution.py:307
  60.0 3.8 %collective-permute-start.6 = (bf16[3,224,384]{2,1,0:T(8,128)(2,1)S(1)}, bf16[3,224,384]{2,1,0:T(8,128)(2,1)S(1)}, u32[]{:S(2)}, u32[]{:S(2)}) collective-permute-start(bf16[3,224,384]{2,1,0:T(8,128)(2,1)S(1)} %pad_maximum_fusion.after), channel_id=1, source_target_pairs={{0,1},{1,0},{2,3},{3,2},{4,5},{5,4},{6,7},{7,6},{8,9},{9,8},{10,11... | collective-permute-start | bytes 1548296 | tf_op jit(solution)/shard_map/ppermute | solution.py:227
  75.0 7.5 %collective-permute-start.7 = (bf16[64,1024]{1,0:T(8,128)(2,1)S(1)}, bf16[64,1024]{1,0:T(8,128)(2,1)S(1)}, u32[]{:S(2)}, u32[]{:S(2)}) collective-permute-start(bf16[64,1024]{1,0:T(8,128)(2,1)S(1)} %get-tuple-element.32), channel_id=1, source_target_pairs={{1,2},{2,1},{3,4},{4,3},{5,6},{6,5},{7,0},{0,7},{9,10},{10,9},{11,... | collective-permute-start | bytes 393224 | tf_op jit(solution)/shard_map/ppermute | solution.py:235
  82.5 8.1 %copy-start = (bf16[2,1,32,384]{3,2,1,0:T(8,128)(2,1)S(1)}, bf16[2,1,32,384]{3,2,1,0:T(8,128)(2,1)}, u32[]{:S(2)}) copy-start(bf16[2,1,32,384]{3,2,1,0:T(8,128)(2,1)} %param.7) | copy-start | bytes 147460
  83.2 7.4 %copy-start.3 = (f32[384]{0:T(512)S(1)}, f32[384]{0:T(512)}, u32[]{:S(2)}) copy-start(f32[384]{0:T(512)} %bias.3) | copy-start | bytes 4612
  83.2 7.4 %collective-permute-start.8 = (bf16[64,512]{1,0:T(8,128)(2,1)S(1)}, bf16[64,512]{1,0:T(8,128)(2,1)S(1)}, u32[]{:S(2)}, u32[]{:S(2)}) collective-permute-start(bf16[64,512]{1,0:T(8,128)(2,1)S(1)} %get-tuple-element.34), channel_id=1, source_target_pairs={{0,64},{64,128},{128,192},{192,256},{256,320},{320,384},{384,448},... | collective-permute-start | bytes 196616 | tf_op jit(solution)/shard_map/ppermute | solution.py:243

commit v5 on v4

--- a/solution.py
+++ b/solution.py
@@ -1,3 +1,5 @@
+import functools
+
 import jax
 import jax.numpy as jnp
 from jax import lax
@@ -8,14 +10,15 @@
 
 CHANNELS = 384
 BLOCK = 48
-SLOT = 224
+GROUP = 80
+SLOT = 3 * GROUP
 LANES = 512
 VMEM = 48 * 1024 * 1024
 F32 = jnp.float32
 BF16 = jnp.bfloat16
 
 
-def call(kernel, out_shape, scratch=(), smem=0, hbm=0, anywhere=0, n=0, vmem_limit=VMEM):
+def call(kernel, out_shape, scratch=(), smem=0, hbm=0, anywhere=0, n=0, vmem_limit=VMEM, flops=0):
     specs = [pl.BlockSpec(memory_space=pltpu.SMEM)] * smem
     specs += [pl.BlockSpec(memory_space=pltpu.HBM)] * hbm
     specs += [pl.BlockSpec(memory_space=pl.ANY)] * anywhere
@@ -29,6 +32,7 @@
         out_specs=[vmem] * len(out_shape) if multiple else vmem,
         scratch_shapes=list(scratch),
         compiler_params=pltpu.CompilerParams(vmem_limit_bytes=vmem_limit),
+        cost_estimate=pl.CostEstimate(flops=flops, bytes_accessed=0, transcendentals=0),
     )
 
 
@@ -59,7 +63,8 @@
     for conv, piece in enumerate((piece_one, piece_two)):
         copies[conv].wait()
         for tap in range(27):
-            rows[8 * tap : 8 * tap + 6, :] = weights[conv, tap].astype(F32)
+            at = GROUP * (tap // 3 % 3) + 8 * (3 * (tap // 9) + tap % 3)
+            rows[at : at + 6, :] = weights[conv, tap].astype(F32)
         packed = rows[...].astype(BF16)
         piece[...] = packed
         pieces[conv] = packed
@@ -73,83 +78,96 @@
         hidden[z] = result
 
 
-def place_weights(conv, ids, both, near, far, swapped, whole):
+def place_weights(conv, height, ids, both, near, far, swapped, group):
     x, c = ids[1], ids[2]
-
-    def place(position, value):
-        whole[position] = value
-
     chip = jnp.bitwise_xor(x, 1 + 2 * c)
     other = jnp.bitwise_xor(x, 3 - 2 * c)
     across = jnp.bitwise_xor(x, 2)
+    rows = pl.ds(pl.multiple_of(GROUP * height, 16), GROUP)
     for i in range(2):
-        place(2 * x + i, both[i])
-        place(2 * chip + i, near[i])
-        place(2 * other + i, swapped[i])
-    place(2 * across + c, far[conv])
-    place(2 * across + 1 - c, swapped[2])
-
-
-def taps(ids, products, keep, partner, pair):
-    c = ids[2]
+        group[2 * x + i] = both[i, rows, :]
+        group[2 * chip + i] = near[i, rows, :]
+        group[2 * other + i] = swapped[i, rows, :]
+    group[2 * across + c] = far[conv, rows, :]
+    group[2 * across + 1 - c] = swapped[2, rows, :]
+
+
+def taps(products, first, emit):
     column = lax.rem(iota((8, 2 * LANES), 1), 32)
     half = LANES // 2
     for two in range(4):
-        parts = ([], [], [])
+        rows = []
         for slot in (2 * two, 2 * two + 1):
-            for j in range(3):
-                sums = []
-                for l in range(3):
-                    k = [
-                        products[pl.ds(slot * SLOT + 8 * (9 * i + 3 * j + l), 8), :]
-                        for i in range(3)
-                    ]
-                    frames = [
-                        k[2][:, :half],
-                        k[2][:, half:] + k[1][:, :half],
-                        k[1][:, half:] + k[0][:, :half],
-                        k[0][:, half:],
-                    ]
-                    sums.append(jnp.concatenate(frames, axis=1))
-                left = jnp.where(column == 0, 0.0, pltpu.roll(sums[0], 1, 1))
-                right = jnp.where(column == 31, 0.0, pltpu.roll(sums[2], 2 * LANES - 1, 1))
-                parts[j].append(sums[1] + left + right)
-        below, level, above = [jnp.concatenate(p, axis=0) for p in parts]
-        at = pl.ds(16 * two, 16)
-        keep[at, :] = level
-        partner[at, :] = jnp.where(c == 0, below, above).astype(BF16)
-        pair[at, :] = jnp.where(c == 0, above, below).astype(BF16)
-
-
-def conv_one_kernel(ids, gathered, *rest):
-    *pieces, keep, partner, pair, whole, field, products = rest
-    place_weights(0, ids, *pieces, whole)
+            sums = []
+            for l in range(3):
+                k = [products[pl.ds(first(slot) + 8 * (3 * i + l), 8), :] for i in range(3)]
+                frames = [
+                    k[2][:, :half],
+                    k[2][:, half:] + k[1][:, :half],
+                    k[1][:, half:] + k[0][:, :half],
+                    k[0][:, half:],
+                ]
+                sums.append(jnp.concatenate(frames, axis=1))
+            left = jnp.where(column == 0, 0.0, pltpu.roll(sums[0], 1, 1))
+            right = jnp.where(column == 31, 0.0, pltpu.roll(sums[2], 2 * LANES - 1, 1))
+            rows.append(sums[1] + left + right)
+        emit(pl.ds(16 * two, 16), jnp.concatenate(rows, axis=0))
+
+
+def multiply(axis, group, field):
+    return lax.dot_general(
+        group, field, (((1,), (axis,)), ((), ())), preferred_element_type=F32
+    )
+
+
+def pair_sums(conv, axis, ids, field, pieces, pair, group, products):
+    place_weights(conv, 2 - 2 * ids[2], ids, *pieces, group)
+    products[...] = multiply(axis, group[...].reshape(8 * GROUP, CHANNELS), field)
+
+    def emit(at, value):
+        pair[at, :] = value.astype(BF16)
+
+    taps(products, lambda slot: slot * GROUP, emit)
+
+
+def field_kernel(gathered, field):
     for z in range(8):
         for f in range(2):
             field[pl.ds(256 * f + 32 * z, 32), :] = gathered[z, pl.ds(32 * f, 32), :]
-    products[...] = lax.dot_general(
-        whole[...].reshape(8 * SLOT, CHANNELS),
-        field[...],
-        (((1,), (1,)), ((), ())),
-        preferred_element_type=F32,
-    )
-    taps(ids, products, keep, partner, pair)
-
-
-def conv_two_kernel(ids, gathered, gain, *rest):
-    *pieces, keep, partner, pair, whole, products = rest
-    place_weights(1, ids, *pieces, whole)
+
+
+def pair_one_kernel(ids, field, *rest):
+    *pieces, pair, group, products = rest
+    pair_sums(0, 1, ids, field[...], pieces, pair, group, products)
+
+
+def pair_two_kernel(ids, gathered, gain, *rest):
+    *pieces, pair, field, group, products = rest
     values = gathered[...].reshape(CHANNELS, LANES).astype(F32)
     mean = jnp.mean(values * values, axis=0, keepdims=True)
     square = (CHANNELS, CHANNELS)
     same = iota(square, 0) == iota(square, 1)
     gains = jnp.where(same, gain[...].reshape(1, CHANNELS), 0.0)
     scale = jnp.sum(gains, axis=1, keepdims=True)
-    field = silu(values * lax.rsqrt(mean + 1e-6) * scale).astype(BF16)
-    products[...] = jnp.dot(
-        whole[...].reshape(8 * SLOT, CHANNELS), field, preferred_element_type=F32
-    )
-    taps(ids, products, keep, partner, pair)
+    hidden = silu(values * lax.rsqrt(mean + 1e-6) * scale).astype(BF16)
+    field[...] = hidden
+    pair_sums(1, 0, ids, hidden, pieces, pair, group, products)
+
+
+def rest_kernel(conv, axis, ids, field, *rest):
+    *pieces, keep, partner, groups, products = rest
+    place_weights(conv, 1, ids, *pieces, groups.at[0])
+    place_weights(conv, 2 * ids[2], ids, *pieces, groups.at[1])
+    products[...] = multiply(axis, groups[...].reshape(16 * GROUP, CHANNELS), field[...])
+
+    def emit_keep(at, value):
+        keep[at, :] = value
+
+    def emit_partner(at, value):
+        partner[at, :] = value.astype(BF16)
+
+    taps(products, lambda slot: (8 + slot) * GROUP, emit_partner)
+    taps(products, lambda slot: slot * GROUP, emit_keep)
 
 
 def rows_kernel(ids, keep, partners, pair, own, later):
@@ -227,12 +245,15 @@
     return lax.ppermute(value, "core", [(0, 1), (1, 0)])
 
 
-def exchange(ids, keep, partner, pair):
+def swap_chips(pair):
     swaps = []
     for x in range(4):
         last, first = 2 * x + 1, 2 * ((x + 1) % 4)
         swaps += [(last, first), (first, last)]
-    pair = lax.ppermute(pair, ("x", "core"), swaps)
+    return lax.ppermute(pair, ("x", "core"), swaps)
+
+
+def exchange(ids, pair, keep, partner):
     partners = lax.all_gather(partner, "core", axis=0)
     own, later = call(
         rows_kernel,
@@ -249,8 +270,9 @@
         hops += [(2 * x, 2 * (x ^ 1)), (2 * x + 1, 2 * (x ^ 3) + 1)]
     far = lax.ppermute(pieces, "x", [(x, x ^ 2) for x in range(4)])
     result = []
+    chip = lax.all_gather(pieces, "core", axis=1)
     for conv, piece in enumerate((piece_one, piece_two)):
-        both = lax.all_gather(piece, "core", axis=0)
+        both = chip[conv]
         near = lax.ppermute(both, ("x", "core"), hops)
         result.append(((both, near, far), jnp.concatenate([near, far[conv : conv + 1]])))
     return result
@@ -264,13 +286,15 @@
         for w in (weight_one, weight_two)
     ]
     piece = shape((SLOT, CHANNELS), BF16)
-    sums = [
-        shape((64, 2 * LANES), F32),
-        shape((64, 2 * LANES), BF16),
-        shape((64, 2 * LANES), BF16),
-    ]
-    whole = pltpu.VMEM((8, SLOT, CHANNELS), BF16)
-    products = pltpu.VMEM((8 * SLOT, LANES), F32)
+    half = shape((64, 2 * LANES), BF16)
+    sums = [shape((64, 2 * LANES), F32), half]
+    group = pltpu.VMEM((8, GROUP, CHANNELS), BF16)
+    groups = pltpu.VMEM((2, 8, GROUP, CHANNELS), BF16)
+    products = pltpu.VMEM((8 * GROUP, LANES), F32)
+    products_rest = pltpu.VMEM((16 * GROUP, LANES), F32)
+    rest = lambda conv, axis: call(
+        functools.partial(rest_kernel, conv, axis), sums, [groups, products_rest], smem=1, n=6
+    )
 
     hidden, *pieces = call(
         first_kernel,
@@ -293,22 +317,23 @@
     )(latent, weight_one, weight_two, gain_one)
     (weights_one, packed_one), (weights_two, packed_two) = gather_weights(*pieces)
     gathered = lax.all_to_all(hidden, "z", 0, 0)
-    sums_one = call(
-        conv_one_kernel,
-        sums,
-        [whole, pltpu.VMEM((LANES, CHANNELS), BF16), products],
-        smem=1,
-        n=6,
-    )(ids, gathered, *weights_one, swap_cores(packed_one))
-    own, earlier = exchange(ids, *sums_one)
+    field = call(field_kernel, shape((LANES, CHANNELS), BF16), n=1, flops=10**11)(gathered)
+    weights_one += (swap_cores(packed_one),)
+    pair = call(pair_one_kernel, half, [group, products], smem=1, n=6)(ids, field, *weights_one)
+    own, earlier = exchange(ids, swap_chips(pair), *rest(0, 1)(ids, field, *weights_one))
     middle = call(middle_kernel, shape((8, BLOCK, LANES), BF16), smem=1, anywhere=1, n=5)(
         ids, packed_two, own, earlier, bias_one
     )
     gathered = lax.all_to_all(middle, "z", 0, 0)
-    sums_two = call(conv_two_kernel, sums, [whole, products], smem=1, n=7)(
-        ids, gathered, gain_two, *weights_two, swap_cores(packed_two)
-    )
-    own, earlier = exchange(ids, *sums_two)
+    weights_two += (swap_cores(packed_two),)
+    pair, field = call(
+        pair_two_kernel,
+        [half, shape((CHANNELS, LANES), BF16)],
+        [group, products],
+        smem=1,
+        n=7,
+    )(ids, gathered, gain_two, *weights_two)
+    own, earlier = exchange(ids, swap_chips(pair), *rest(1, 0)(ids, field, *weights_two))
     pieces, kept = call(
         spread_kernel,
         [shape((8, 24, 128), BF16), shape((64, CHANNELS), BF16)],

time: 104 us -> 102 us (0.981)
  waiting for transfers between devices: 32.6 us -> 28.6 us
  starting transfers between devices: 40.3 us -> 42.6 us
  blocking collectives: 18.9 us -> 16.9 us
  Pallas kernels: 10.7 us -> 12.4 us
    all_to_all x1, waiting for transfers between devices: 7.6 us -> 0.4 us  [per_device(): gathered = lax.all_to_all(hidden, 'z', 0, 0)]
    all_to_all x1, starting transfers between devices: 3.58 us -> 7.32 us  [per_device(): gathered = lax.all_to_all(middle, 'z', 0, 0)]
    ppermute x2, waiting for transfers between devices: 0.01 us -> 3.42 us  [gather_weights(): near = lax.ppermute(both, ('x', 'core'), hops)]
    all_gather x2 -> x1, blocking collectives: 4.32 us -> 2.33 us  [gather_weights(): chip = lax.all_gather(pieces, 'core', axis=1)]
    pallas_call x2 -> x5, Pallas kernels: 3.93 us -> 5.65 us  [the longest x1 1.53 us: per_device(): rest(0, 1)(ids, field, *weights_one)]
    ppermute x2, starting transfers between devices: 7.14 us -> 5.51 us  [swap_chips(): return lax.ppermute(pair, ('x', 'core'), swaps)]
    ppermute x2, waiting for transfers between devices: 3.84 us -> 2.4 us  [swap_chips(): return lax.ppermute(pair, ('x', 'core'), swaps)]
    ppermute x2, waiting for transfers between devices: 1.87 us -> 3.21 us  [swap_cores(): return lax.ppermute(value, 'core', [(0, 1), (1, 0)])]
  transfers between devices with their start and end apart: 11 -> 11, of which waited for: 7 -> 9; matrix products, arithmetic and copies ran while one was open for 0% -> 0% of each run, Pallas kernels for 2% -> 5%
where the time goes in v5:
time: 102 us; the launch traced here: 101 us
  starting transfers between devices  42.6 us (42%)
  waiting for transfers between devices  28.6 us (28%)
  blocking collectives  16.9 us (17%)
  Pallas kernels  12.4 us (12%)
    all_to_all x1, blocking collectives, per_device(): pieces = lax.all_to_all(pieces, 'z', 0, 0)  10.6 us
    all_to_all x1, starting transfers between devices, per_device(): gathered = lax.all_to_all(hidden, 'z', 0, 0)  10.5 us
    ppermute x2, waiting for transfers between devices, exchange(): return (own, lax.ppermute(later, 't', [(i, i + 1) for i in range(7)]))  10.1 us
    all_to_all x1, waiting for transfers between devices, per_device(): gathered = lax.all_to_all(middle, 'z', 0, 0)  9.07 us
    all_to_all x1, starting transfers between devices, per_device(): gathered = lax.all_to_all(middle, 'z', 0, 0)  7.32 us
    ppermute x2, starting transfers between devices, gather_weights(): near = lax.ppermute(both, ('x', 'core'), hops)  5.84 us
    ppermute x2, starting transfers between devices, swap_chips(): return lax.ppermute(pair, ('x', 'core'), swaps)  5.51 us
    ppermute x1, starting transfers between devices, gather_weights(): far = lax.ppermute(pieces, 'x', [(x, x ^ 2) for x in range(4)])  4.93 us
  transfers between devices with their start and end apart: 11, of which 9 were waited for; matrix products, arithmetic and copies ran while one was open for 0% of the time, Pallas kernels for 5%

profile of v5, /device:TPU:32, one launch (start us, length us, event | category | flops | bytes accessed | tf_op | source)
XLA Modules:
  0.0 101.1 jit_solution(18240620768528326186)
XLA Ops:
  0.0 2.1 %shard_map.73 = (bf16[8,64,384]{2,1,0:T(8,128)(2,1)}, bf16[240,384]{1,0:T(8,128)(2,1)}, bf16[240,384]{1,0:T(8,128)(2,1)}, bf16[2,240,384]{2,1,0:T(8,128)(2,1)}) custom-call(bf16[64,384]{1,0:T(8,128)(2,1)} %bitcast.25, bf16[27,6,384]{2,1,0:T(8,128)(2,1)} %bitcast.27, bf16[27,6,384]{2,1,0:T(8,128)(2,1)} %bitcast.28, f32[384]{0:T(512)} %gain_hbm.1), custom_call_target="tpu_custom_call" | custom-call | tf_op jit(solution)/shard_map/pallas_call | solution.py:299
  2.1 4.9 %collective-permute-start.1 = (bf16[2,240,384]{2,1,0:T(8,128)(2,1)}, bf16[2,240,384]{2,1,0:T(8,128)(2,1)S(1)}, u32[]{:S(2)}, u32[]{:S(2)}) collective-permute-start(bf16[2,240,384]{2,1,0:T(8,128)(2,1)} %get-tuple-element.19), channel_id=1, source_target_pairs={{0,4},{2,6},{4,0},{6,2},{1,5},{3,7},{5,1},{7,3},{8,12},{10,14},{12... | collective-permute-start | bytes 1105928 | tf_op jit(solution)/shard_map/ppermute | solution.py:271
  7.1 10.5 %all-to-all-start = ((bf16[8,64,384]{2,1,0:T(8,128)(2,1)}), bf16[8,64,384]{2,1,0:T(8,128)(2,1)S(1)}, u32[]{:S(2)}, u32[]{:S(2)}) async-start(bf16[8,64,384]{2,1,0:T(8,128)(2,1)} %get-tuple-element.20), calls=%async_computation | async-start | bytes 786432 | tf_op jit(solution)/shard_map/all_to_all | solution.py:319
  17.5 2.3 %all-gather = bf16[2,480,384]{2,1,0:T(8,128)(2,1)S(1)} all-gather(bf16[2,240,384]{2,1,0:T(8,128)(2,1)S(1)} %copy-done.4), channel_id=2, replica_groups=mesh['t'=8,'z'=8,'x'=4,'core'=2] {'core'}, dimensions={1}, use_global_device_ids=true | all-gather | bytes 1105920 | tf_op jit(solution)/shard_map/all_gather | solution.py:273
  19.9 2.5 %collective-permute-start.2 = (bf16[2,240,384]{2,1,0:T(8,128)(2,1)S(1)}, bf16[2,240,384]{2,1,0:T(8,128)(2,1)S(1)}, u32[]{:S(2)}, u32[]{:S(2)}) collective-permute-start(bf16[2,240,384]{2,1,0:T(8,128)(2,1)S(1)} %bitcast.17), channel_id=1, source_target_pairs={{0,2},{1,7},{2,0},{3,5},{4,6},{5,3},{6,4},{7,1},{8,10},{9,15},{10,... | collective-permute-start | bytes 1105928 | tf_op jit(solution)/shard_map/ppermute | solution.py:276
  22.4 3.3 %collective-permute-start = (bf16[2,240,384]{2,1,0:T(8,128)(2,1)S(1)}, bf16[2,240,384]{2,1,0:T(8,128)(2,1)S(1)}, u32[]{:S(2)}, u32[]{:S(2)}) collective-permute-start(bf16[2,240,384]{2,1,0:T(8,128)(2,1)S(1)} %bitcast.20), channel_id=1, source_target_pairs={{0,2},{1,7},{2,0},{3,5},{4,6},{5,3},{6,4},{7,1},{8,10},{9,15},{10,... | collective-permute-start | bytes 1105928 | tf_op jit(solution)/shard_map/ppermute | solution.py:276
  25.9 3.4 %collective-permute-done.2.rest_1_ = bf16[2,240,384]{2,1,0:T(8,128)(2,1)S(1)} collective-permute-done((bf16[2,240,384]{2,1,0:T(8,128)(2,1)S(1)}, bf16[2,240,384]{2,1,0:T(8,128)(2,1)S(1)}, u32[]{:S(2)}, u32[]{:S(2)}) %collective-permute-start.2) | collective-permute-done | bytes 368672 | tf_op jit(solution)/shard_map/ppermute | solution.py:276
  29.4 2.1 %collective-permute-start.3 = (bf16[3,240,384]{2,1,0:T(8,128)(2,1)S(1)}, bf16[3,240,384]{2,1,0:T(8,128)(2,1)S(1)}, u32[]{:S(2)}, u32[]{:S(2)}) collective-permute-start(bf16[3,240,384]{2,1,0:T(8,128)(2,1)S(1)} %pad_maximum_fusion.1), channel_id=1, source_target_pairs={{0,1},{1,0},{2,3},{3,2},{4,5},{5,4},{6,7},{7,6},{8,9},{9,8},{10,11... | collective-permute-start | bytes 1658888 | tf_op jit(solution)/shard_map/ppermute | solution.py:245
  32.0 1.3 %collective-permute-done.3.rest_3_ = bf16[3,240,384]{2,1,0:T(8,128)(2,1)S(1)} collective-permute-done((bf16[3,240,384]{2,1,0:T(8,128)(2,1)S(1)}, bf16[3,240,384]{2,1,0:T(8,128)(2,1)S(1)}, u32[]{:S(2)}, u32[]{:S(2)}) %collective-permute-start.3) | collective-permute-done | bytes 552992 | tf_op jit(solution)/shard_map/ppermute | solution.py:245
  33.3 1.2 %shard_map.76 = bf16[64,1024]{1,0:T(8,128)(2,1)S(1)} custom-call(s32[3]{0:T(128)S(1)} %pad_add_fusion.ids, bf16[512,384]{1,0:T(8,128)(2,1)S(1)} %shard_map.74.field, bf16[2,240,384]{2,1,0:T(8,128)(2,1)S(1)} %bitcast.18, bf16[2,240,384]{2,1,0:T(8,128)(2,1)S(1)} %collective-permute-done.2.rest_1_, bf16[2,240,384]{2,1,0:T(8,128)(2,1)S(1)} %collective-permute-done.1.rest_2_, ...), custom_call_target="tpu_custom_call" | custom-call | tf_op jit(solution)/shard_map/pallas_call | solution.py:322
  34.4 2.9 %collective-permute-start.4 = (bf16[64,1024]{1,0:T(8,128)(2,1)S(1)}, bf16[64,1024]{1,0:T(8,128)(2,1)S(1)}, u32[]{:S(2)}, u32[]{:S(2)}) collective-permute-start(bf16[64,1024]{1,0:T(8,128)(2,1)S(1)} %shard_map.76), channel_id=1, source_target_pairs={{1,2},{2,1},{3,4},{4,3},{5,6},{6,5},{7,0},{0,7},{9,10},{10,9},{11,... | collective-permute-start | bytes 393224 | tf_op jit(solution)/shard_map/ppermute | solution.py:253
  37.3 1.5 %shard_map.75 = (f32[64,1024]{1,0:T(8,128)S(1)}, bf16[64,1024]{1,0:T(8,128)(2,1)S(1)}) custom-call(s32[3]{0:T(128)S(1)} %pad_add_fusion.ids, bf16[512,384]{1,0:T(8,128)(2,1)S(1)} %shard_map.74.field, bf16[2,240,384]{2,1,0:T(8,128)(2,1)S(1)} %bitcast.19, bf16[2,240,384]{2,1,0:T(8,128)(2,1)S(1)} %collective-permute-done.2.rest_1_, ...), custom_call_target="tpu_custom_call" | custom-call | tf_op jit(solution)/shard_map/pallas_call | solution.py:323
  38.8 2.0 %all-gather.1 = bf16[128,1024]{1,0:T(8,128)(2,1)S(1)} all-gather(bf16[64,1024]{1,0:T(8,128)(2,1)S(1)} %get-tuple-element.22), channel_id=3, replica_groups=mesh['t'=8,'z'=8,'x'=4,'core'=2] {'core'}, dimensions={0}, use_global_device_ids=true | all-gather | bytes 393216 | tf_op jit(solution)/shard_map/all_gather | solution.py:257
  40.8 1.1 %collective-permute-done.4.pair = bf16[64,1024]{1,0:T(8,128)(2,1)S(1)} collective-permute-done((bf16[64,1024]{1,0:T(8,128)(2,1)S(1)}, bf16[64,1024]{1,0:T(8,128)(2,1)S(1)}, u32[]{:S(2)}, u32[]{:S(2)}) %collective-permute-start.4) | collective-permute-done | bytes 131104 | tf_op jit(solution)/shard_map/ppermute | solution.py:253
  41.9 0.7 shard_map.77
  42.6 2.6 %collective-permute-start.5 = (bf16[64,512]{1,0:T(8,128)(2,1)S(1)}, bf16[64,512]{1,0:T(8,128)(2,1)S(1)}, u32[]{:S(2)}, u32[]{:S(2)}) collective-permute-start(bf16[64,512]{1,0:T(8,128)(2,1)S(1)} %get-tuple-element.24), channel_id=1, source_target_pairs={{0,64},{64,128},{128,192},{192,256},{256,320},{320,384},{384,448},... | collective-permute-start | bytes 196616 | tf_op jit(solution)/shard_map/ppermute | solution.py:264
  45.3 4.7 %collective-permute-done.5.earlier = bf16[64,512]{1,0:T(8,128)(2,1)S(1)} collective-permute-done((bf16[64,512]{1,0:T(8,128)(2,1)S(1)}, bf16[64,512]{1,0:T(8,128)(2,1)S(1)}, u32[]{:S(2)}, u32[]{:S(2)}) %collective-permute-start.5) | collective-permute-done | bytes 65568 | tf_op jit(solution)/shard_map/ppermute | solution.py:264
  50.0 1.5 %shard_map.78 = bf16[8,48,512]{2,1,0:T(8,128)(2,1)} custom-call(s32[3]{0:T(128)S(1)} %pad_add_fusion.ids, bf16[3,240,384]{2,1,0:T(8,128)(2,1)S(1)} %pad_maximum_fusion.after, f32[64,512]{1,0:T(8,128)S(1)} %get-tuple-element.23.own, bf16[64,512]{1,0:T(8,128)(2,1)S(1)} %collective-permute-done.5.earlier, f32[384]{0:T(512)S(1)} %copy-done.1), custom_call_target="tpu_custom_call" | custom-call | tf_op jit(solution)/shard_map/pallas_call | solution.py:324
  51.5 7.3 %all-to-all-start.1 = ((bf16[8,48,512]{2,1,0:T(8,128)(2,1)}), bf16[8,48,512]{2,1,0:T(8,128)(2,1)S(1)}, u32[]{:S(2)}, u32[]{:S(2)}) async-start(bf16[8,48,512]{2,1,0:T(8,128)(2,1)} %shard_map.78), calls=%async_computation.1 | async-start | bytes 786432 | tf_op jit(solution)/shard_map/all_to_all | solution.py:327
  58.8 1.9 %collective-permute-start.6 = (bf16[3,240,384]{2,1,0:T(8,128)(2,1)S(1)}, bf16[3,240,384]{2,1,0:T(8,128)(2,1)S(1)}, u32[]{:S(2)}, u32[]{:S(2)}) collective-permute-start(bf16[3,240,384]{2,1,0:T(8,128)(2,1)S(1)} %pad_maximum_fusion.after), channel_id=1, source_target_pairs={{0,1},{1,0},{2,3},{3,2},{4,5},{5,4},{6,7},{7,6},{8,9},{9,8},{10,11... | collective-permute-start | bytes 1658888 | tf_op jit(solution)/shard_map/ppermute | solution.py:245
  60.8 1.9 %collective-permute-done.6.rest_3_ = bf16[3,240,384]{2,1,0:T(8,128)(2,1)S(1)} collective-permute-done((bf16[3,240,384]{2,1,0:T(8,128)(2,1)S(1)}, bf16[3,240,384]{2,1,0:T(8,128)(2,1)S(1)}, u32[]{:S(2)}, u32[]{:S(2)}) %collective-permute-start.6) | collective-permute-done | bytes 552992 | tf_op jit(solution)/shard_map/ppermute | solution.py:245
  62.7 9.1 %all-to-all-done.1.gathered = bf16[8,48,512]{2,1,0:T(8,128)(2,1)S(1)} async-done(((bf16[8,48,512]{2,1,0:T(8,128)(2,1)}), bf16[8,48,512]{2,1,0:T(8,128)(2,1)S(1)}, u32[]{:S(2)}, u32[]{:S(2)}) %all-to-all-start.1) | async-done | bytes 393248 | tf_op jit(solution)/shard_map/all_to_all | solution.py:327
  71.7 1.4 %shard_map.79 = (bf16[64,1024]{1,0:T(8,128)(2,1)S(1)}, bf16[384,512]{1,0:T(8,128)(2,1)S(1)}) custom-call(s32[3]{0:T(128)S(1)} %pad_add_fusion.ids, bf16[8,48,512]{2,1,0:T(8,128)(2,1)S(1)} %all-to-all-done.1.gathered, f32[384]{0:T(512)S(1)} %copy-done.3, bf16[2,240,384]{2,1,0:T(8,128)(2,1)S(1)} %bitcast.21, ...), custom_call_target="tpu_custom_call" | custom-call | tf_op jit(solution)/shard_map/pallas_call | solution.py:329
  73.2 2.7 %collective-permute-start.7 = (bf16[64,1024]{1,0:T(8,128)(2,1)S(1)}, bf16[64,1024]{1,0:T(8,128)(2,1)S(1)}, u32[]{:S(2)}, u32[]{:S(2)}) collective-permute-start(bf16[64,1024]{1,0:T(8,128)(2,1)S(1)} %get-tuple-element.28), channel_id=1, source_target_pairs={{1,2},{2,1},{3,4},{4,3},{5,6},{6,5},{7,0},{0,7},{9,10},{10,9},{11,... | collective-permute-start | bytes 393224 | tf_op jit(solution)/shard_map/ppermute | solution.py:253
  75.8 1.5 %shard_map.80 = (f32[64,1024]{1,0:T(8,128)S(1)}, bf16[64,1024]{1,0:T(8,128)(2,1)S(1)}) custom-call(s32[3]{0:T(128)S(1)} %pad_add_fusion.ids, bf16[384,512]{1,0:T(8,128)(2,1)S(1)} %get-tuple-element.25.field, bf16[2,240,384]{2,1,0:T(8,128)(2,1)S(1)} %bitcast.22, bf16[2,240,384]{2,1,0:T(8,128)(2,1)S(1)} %collective-permute-done.rest_1_, ...), custom_call_target="tpu_custom_call" | custom-call | tf_op jit(solution)/shard_map/pallas_call | solution.py:336
  77.4 2.0 %all-gather.2 = bf16[128,1024]{1,0:T(8,128)(2,1)S(1)} all-gather(bf16[64,1024]{1,0:T(8,128)(2,1)S(1)} %get-tuple-element.27), channel_id=4, replica_groups=mesh['t'=8,'z'=8,'x'=4,'core'=2] {'core'}, dimensions={0}, use_global_device_ids=true | all-gather | bytes 393216 | tf_op jit(solution)/shard_map/all_gather | solution.py:257
  79.3 1.3 %collective-permute-done.7.pair = bf16[64,1024]{1,0:T(8,128)(2,1)S(1)} collective-permute-done((bf16[64,1024]{1,0:T(8,128)(2,1)S(1)}, bf16[64,1024]{1,0:T(8,128)(2,1)S(1)}, u32[]{:S(2)}, u32[]{:S(2)}) %collective-permute-start.7) | collective-permute-done | bytes 131104 | tf_op jit(solution)/shard_map/ppermute | solution.py:253
  81.4 1.9 %collective-permute-start.8 = (bf16[64,512]{1,0:T(8,128)(2,1)S(1)}, bf16[64,512]{1,0:T(8,128)(2,1)S(1)}, u32[]{:S(2)}, u32[]{:S(2)}) collective-permute-start(bf16[64,512]{1,0:T(8,128)(2,1)S(1)} %get-tuple-element.30), channel_id=1, source_target_pairs={{0,64},{64,128},{128,192},{192,256},{256,320},{320,384},{384,448},... | collective-permute-start | bytes 196616 | tf_op jit(solution)/shard_map/ppermute | solution.py:264
  83.3 5.4 %collective-permute-done.8.earlier = bf16[64,512]{1,0:T(8,128)(2,1)S(1)} collective-permute-done((bf16[64,512]{1,0:T(8,128)(2,1)S(1)}, bf16[64,512]{1,0:T(8,128)(2,1)S(1)}, u32[]{:S(2)}, u32[]{:S(2)}) %collective-permute-start.8) | collective-permute-done | bytes 65568 | tf_op jit(solution)/shard_map/ppermute | solution.py:264
  88.7 0.9 shard_map.82
  89.6 10.6 %all_to_all.15.gathered = bf16[8,24,128]{2,1,0:T(8,128)(2,1)S(1)} all-to-all(bf16[8,24,128]{2,1,0:T(8,128)(2,1)S(1)} %get-tuple-element.32), channel_id=1, replica_groups=mesh['t'=8,'z'=8,'x'=4,'core'=2] {'z'}, dimensions={0} | all-to-all | bytes 98304 | tf_op jit(solution)/shard_map/all_to_all | solution.py:343
  100.2 0.9 shard_map.83
  (20 shorter events, 1.5 us)
Async XLA Ops:
  2.1 23.8 %collective-permute-start.1 = (bf16[2,240,384]{2,1,0:T(8,128)(2,1)}, bf16[2,240,384]{2,1,0:T(8,128)(2,1)S(1)}, u32[]{:S(2)}, u32[]{:S(2)}) collective-permute-start(bf16[2,240,384]{2,1,0:T(8,128)(2,1)} %get-tuple-element.19), channel_id=1, source_target_pairs={{0,4},{2,6},{4,0},{6,2},{1,5},{3,7},{5,1},{7,3},{8,12},{10,14},{12... | collective-permute-start | bytes 1105928 | tf_op jit(solution)/shard_map/ppermute | solution.py:271
  7.0 10.5 %copy-start.4 = (bf16[2,240,384]{2,1,0:T(8,128)(2,1)S(1)}, bf16[2,240,384]{2,1,0:T(8,128)(2,1)}, u32[]{:S(2)}) copy-start(bf16[2,240,384]{2,1,0:T(8,128)(2,1)} %get-tuple-element.19) | copy-start | bytes 1105924
  7.1 24.9 %all-to-all-start = ((bf16[8,64,384]{2,1,0:T(8,128)(2,1)}), bf16[8,64,384]{2,1,0:T(8,128)(2,1)S(1)}, u32[]{:S(2)}, u32[]{:S(2)}) async-start(bf16[8,64,384]{2,1,0:T(8,128)(2,1)} %get-tuple-element.20), calls=%async_computation | async-start | bytes 786432 | tf_op jit(solution)/shard_map/all_to_all | solution.py:319
  19.9 9.4 %collective-permute-start.2 = (bf16[2,240,384]{2,1,0:T(8,128)(2,1)S(1)}, bf16[2,240,384]{2,1,0:T(8,128)(2,1)S(1)}, u32[]{:S(2)}, u32[]{:S(2)}) collective-permute-start(bf16[2,240,384]{2,1,0:T(8,128)(2,1)S(1)} %bitcast.17), channel_id=1, source_target_pairs={{0,2},{1,7},{2,0},{3,5},{4,6},{5,3},{6,4},{7,1},{8,10},{9,15},{10,... | collective-permute-start | bytes 1105928 | tf_op jit(solution)/shard_map/ppermute | solution.py:276
  22.4 22.8 %collective-permute-start = (bf16[2,240,384]{2,1,0:T(8,128)(2,1)S(1)}, bf16[2,240,384]{2,1,0:T(8,128)(2,1)S(1)}, u32[]{:S(2)}, u32[]{:S(2)}) collective-permute-start(bf16[2,240,384]{2,1,0:T(8,128)(2,1)S(1)} %bitcast.20), channel_id=1, source_target_pairs={{0,2},{1,7},{2,0},{3,5},{4,6},{5,3},{6,4},{7,1},{8,10},{9,15},{10,... | collective-permute-start | bytes 1105928 | tf_op jit(solution)/shard_map/ppermute | solution.py:276
  29.4 3.8 %collective-permute-start.3 = (bf16[3,240,384]{2,1,0:T(8,128)(2,1)S(1)}, bf16[3,240,384]{2,1,0:T(8,128)(2,1)S(1)}, u32[]{:S(2)}, u32[]{:S(2)}) collective-permute-start(bf16[3,240,384]{2,1,0:T(8,128)(2,1)S(1)} %pad_maximum_fusion.1), channel_id=1, source_target_pairs={{0,1},{1,0},{2,3},{3,2},{4,5},{5,4},{6,7},{7,6},{8,9},{9,8},{10,11... | collective-permute-start | bytes 1658888 | tf_op jit(solution)/shard_map/ppermute | solution.py:245
  34.4 7.5 %collective-permute-start.4 = (bf16[64,1024]{1,0:T(8,128)(2,1)S(1)}, bf16[64,1024]{1,0:T(8,128)(2,1)S(1)}, u32[]{:S(2)}, u32[]{:S(2)}) collective-permute-start(bf16[64,1024]{1,0:T(8,128)(2,1)S(1)} %shard_map.76), channel_id=1, source_target_pairs={{1,2},{2,1},{3,4},{4,3},{5,6},{6,5},{7,0},{0,7},{9,10},{10,9},{11,... | collective-permute-start | bytes 393224 | tf_op jit(solution)/shard_map/ppermute | solution.py:253
  42.6 7.4 %collective-permute-start.5 = (bf16[64,512]{1,0:T(8,128)(2,1)S(1)}, bf16[64,512]{1,0:T(8,128)(2,1)S(1)}, u32[]{:S(2)}, u32[]{:S(2)}) collective-permute-start(bf16[64,512]{1,0:T(8,128)(2,1)S(1)} %get-tuple-element.24), channel_id=1, source_target_pairs={{0,64},{64,128},{128,192},{192,256},{256,320},{320,384},{384,448},... | collective-permute-start | bytes 196616 | tf_op jit(solution)/shard_map/ppermute | solution.py:264
  45.2 4.8 %copy-start.1 = (f32[384]{0:T(512)S(1)}, f32[384]{0:T(512)}, u32[]{:S(2)}) copy-start(f32[384]{0:T(512)} %bias.2) | copy-start | bytes 4612
  51.5 20.2 %copy-start.3 = (f32[384]{0:T(512)S(1)}, f32[384]{0:T(512)}, u32[]{:S(2)}) copy-start(f32[384]{0:T(512)} %gain.1) | copy-start | bytes 4612
  51.5 20.2 %all-to-all-start.1 = ((bf16[8,48,512]{2,1,0:T(8,128)(2,1)}), bf16[8,48,512]{2,1,0:T(8,128)(2,1)S(1)}, u32[]{:S(2)}, u32[]{:S(2)}) async-start(bf16[8,48,512]{2,1,0:T(8,128)(2,1)} %shard_map.78), calls=%async_computation.1 | async-start | bytes 786432 | tf_op jit(solution)/shard_map/all_to_all | solution.py:327
  58.8 3.8 %collective-permute-start.6 = (bf16[3,240,384]{2,1,0:T(8,128)(2,1)S(1)}, bf16[3,240,384]{2,1,0:T(8,128)(2,1)S(1)}, u32[]{:S(2)}, u32[]{:S(2)}) collective-permute-start(bf16[3,240,384]{2,1,0:T(8,128)(2,1)S(1)} %pad_maximum_fusion.after), channel_id=1, source_target_pairs={{0,1},{1,0},{2,3},{3,2},{4,5},{5,4},{6,7},{7,6},{8,9},{9,8},{10,11... | collective-permute-start | bytes 1658888 | tf_op jit(solution)/shard_map/ppermute | solution.py:245
  73.2 7.5 %collective-permute-start.7 = (bf16[64,1024]{1,0:T(8,128)(2,1)S(1)}, bf16[64,1024]{1,0:T(8,128)(2,1)S(1)}, u32[]{:S(2)}, u32[]{:S(2)}) collective-permute-start(bf16[64,1024]{1,0:T(8,128)(2,1)S(1)} %get-tuple-element.28), channel_id=1, source_target_pairs={{1,2},{2,1},{3,4},{4,3},{5,6},{6,5},{7,0},{0,7},{9,10},{10,9},{11,... | collective-permute-start | bytes 393224 | tf_op jit(solution)/shard_map/ppermute | solution.py:253
  80.6 8.1 %copy-start = (bf16[2,1,32,384]{3,2,1,0:T(8,128)(2,1)S(1)}, bf16[2,1,32,384]{3,2,1,0:T(8,128)(2,1)}, u32[]{:S(2)}) copy-start(bf16[2,1,32,384]{3,2,1,0:T(8,128)(2,1)} %param.7) | copy-start | bytes 147460
  81.3 7.4 %copy-start.2 = (f32[384]{0:T(512)S(1)}, f32[384]{0:T(512)}, u32[]{:S(2)}) copy-start(f32[384]{0:T(512)} %bias.3) | copy-start | bytes 4612
  81.4 7.4 %collective-permute-start.8 = (bf16[64,512]{1,0:T(8,128)(2,1)S(1)}, bf16[64,512]{1,0:T(8,128)(2,1)S(1)}, u32[]{:S(2)}, u32[]{:S(2)}) collective-permute-start(bf16[64,512]{1,0:T(8,128)(2,1)S(1)} %get-tuple-element.30), channel_id=1, source_target_pairs={{0,64},{64,128},{128,192},{192,256},{256,320},{320,384},{384,448},... | collective-permute-start | bytes 196616 | tf_op jit(solution)/shard_map/ppermute | solution.py:264

commit v6 on v5

--- a/solution.py
+++ b/solution.py
@@ -49,7 +49,7 @@
 
 
 def first_kernel(
-    latent_hbm, one_hbm, two_hbm, gain_hbm, hidden, piece_one, piece_two, pieces, latent, gain, weights, rows, sems
+    latent_hbm, one_hbm, two_hbm, gain_hbm, hidden, pieces, latent, gain, weights, rows, sems
 ):
     copies = [
         pltpu.make_async_copy(one_hbm, weights.at[0], sems.at[0]),
@@ -60,14 +60,12 @@
     for copy in copies:
         copy.start()
     rows[...] = jnp.zeros_like(rows)
-    for conv, piece in enumerate((piece_one, piece_two)):
+    for conv in range(2):
         copies[conv].wait()
         for tap in range(27):
             at = GROUP * (tap // 3 % 3) + 8 * (3 * (tap // 9) + tap % 3)
             rows[at : at + 6, :] = weights[conv, tap].astype(F32)
-        packed = rows[...].astype(BF16)
-        piece[...] = packed
-        pieces[conv] = packed
+        pieces[conv] = rows[...].astype(BF16)
     copies[2].wait()
     copies[3].wait()
     values = latent[...].astype(F32)
@@ -78,18 +76,16 @@
         hidden[z] = result
 
 
-def place_weights(conv, height, ids, both, near, far, swapped, group):
+def place_weights(conv, height, ids, both, near, far, other, group):
     x, c = ids[1], ids[2]
-    chip = jnp.bitwise_xor(x, 1 + 2 * c)
-    other = jnp.bitwise_xor(x, 3 - 2 * c)
     across = jnp.bitwise_xor(x, 2)
     rows = pl.ds(pl.multiple_of(GROUP * height, 16), GROUP)
     for i in range(2):
         group[2 * x + i] = both[i, rows, :]
-        group[2 * chip + i] = near[i, rows, :]
-        group[2 * other + i] = swapped[i, rows, :]
+        group[2 * jnp.bitwise_xor(x, 1) + i] = near[0, i, rows, :]
+        group[2 * jnp.bitwise_xor(x, 3) + i] = near[1, i, rows, :]
     group[2 * across + c] = far[conv, rows, :]
-    group[2 * across + 1 - c] = swapped[2, rows, :]
+    group[2 * across + 1 - c] = other[conv, rows, :]
 
 
 def taps(products, first, emit):
@@ -170,51 +166,51 @@
     taps(products, lambda slot: slot * GROUP, emit_keep)
 
 
-def rows_kernel(ids, keep, partners, pair, own, later):
+def rows_kernel(ids, keep, partners, pair, bias, own, later):
     c = ids[2]
     position = 2 * ids[1] + c
     total = keep[...] + partners[1 - c].astype(F32)
-    place = lax.rem(iota((64, 2 * LANES), 1) // 32, 8)
-
-    def finish(got):
-        result = total + got
-        own[...] = result[:, :LANES]
-        later[...] = result[:, LANES:].astype(BF16)
-
-    @pl.when((position > 0) & (position < 7))
-    def _():
-        finish(pair[...].astype(F32))
-
-    @pl.when(position == 0)
-    def _():
-        finish(jnp.where(place == 0, 0.0, pltpu.roll(pair[...].astype(F32), 32, 1)))
-
-    @pl.when(position == 7)
-    def _():
-        got = pltpu.roll(pair[...].astype(F32), 2 * LANES - 32, 1)
-        finish(jnp.where(place == 7, 0.0, got))
-
-
-def block_values(ids, own, earlier, bias):
     row = iota((64, CHANNELS), 0)
     wanted = BLOCK * ids[0] + 6 * (row // 8) + lax.rem(row, 8)
     chosen = (iota((64, CHANNELS), 1) == wanted) & (lax.rem(row, 8) < 6)
     biases = jnp.where(chosen, bias[...].reshape(1, CHANNELS), 0.0)
     column = jnp.sum(biases, axis=1, keepdims=True)
-    total = (own[...] + earlier[...].astype(F32) + column).astype(BF16)
+    place = lax.rem(iota((64, 2 * LANES), 1) // 32, 8)
+
+    def finish(got):
+        result = total + got
+        own[...] = result[:, :LANES] + column
+        later[...] = result[:, LANES:].astype(BF16)
+
+    @pl.when((position > 0) & (position < 7))
+    def _():
+        finish(pair[...].astype(F32))
+
+    @pl.when(position == 0)
+    def _():
+        finish(jnp.where(place == 0, 0.0, pltpu.roll(pair[...].astype(F32), 32, 1)))
+
+    @pl.when(position == 7)
+    def _():
+        got = pltpu.roll(pair[...].astype(F32), 2 * LANES - 32, 1)
+        finish(jnp.where(place == 7, 0.0, got))
+
+
+def block_values(own, earlier):
+    total = (own[...] + earlier[...].astype(F32)).astype(BF16)
     to, frm = iota((BLOCK, 64), 0), iota((BLOCK, 64), 1)
     pick = (frm == 8 * (to // 6) + lax.rem(to, 6)).astype(BF16)
     return jnp.dot(pick, total, preferred_element_type=F32).astype(BF16)
 
 
-def middle_kernel(ids, after, own, earlier, bias, middle):
-    result = block_values(ids, own, earlier, bias)
+def middle_kernel(after, own, earlier, middle):
+    result = block_values(own, earlier)
     for z in range(8):
         middle[z] = result
 
 
-def spread_kernel(ids, own, earlier, bias, latent, pieces, kept):
-    result = block_values(ids, own, earlier, bias)
+def spread_kernel(own, earlier, latent, pieces, kept):
+    result = block_values(own, earlier)
     result = result.astype(F32)
     for z in range(8):
         parts = []
@@ -253,28 +249,28 @@
     return lax.ppermute(pair, ("x", "core"), swaps)
 
 
-def exchange(ids, pair, keep, partner):
+def exchange(ids, bias, pair, keep, partner):
     partners = lax.all_gather(partner, "core", axis=0)
     own, later = call(
         rows_kernel,
         [shape((64, LANES), F32), shape((64, LANES), BF16)],
         smem=1,
-        n=4,
-    )(ids, keep, partners, pair)
+        n=5,
+    )(ids, keep, partners, pair, bias)
     return own, lax.ppermute(later, "t", [(i, i + 1) for i in range(7)])
 
 
-def gather_weights(piece_one, piece_two, pieces):
+def gather_weights(pieces):
     hops = []
     for x in range(4):
         hops += [(2 * x, 2 * (x ^ 1)), (2 * x + 1, 2 * (x ^ 3) + 1)]
     far = lax.ppermute(pieces, "x", [(x, x ^ 2) for x in range(4)])
+    other = swap_cores(far)
+    chip = lax.all_gather(pieces, "core", axis=1)
     result = []
-    chip = lax.all_gather(pieces, "core", axis=1)
-    for conv, piece in enumerate((piece_one, piece_two)):
-        both = chip[conv]
-        near = lax.ppermute(both, ("x", "core"), hops)
-        result.append(((both, near, far), jnp.concatenate([near, far[conv : conv + 1]])))
+    for both in (chip[0], chip[1]):
+        near = lax.all_gather(lax.ppermute(both, ("x", "core"), hops), "core", axis=0)
+        result.append((both, near, far, other))
     return result
 
 
@@ -285,7 +281,6 @@
         jnp.transpose(w, (0, 1, 2, 4, 3)).reshape(27, 6, CHANNELS)
         for w in (weight_one, weight_two)
     ]
-    piece = shape((SLOT, CHANNELS), BF16)
     half = shape((64, 2 * LANES), BF16)
     sums = [shape((64, 2 * LANES), F32), half]
     group = pltpu.VMEM((8, GROUP, CHANNELS), BF16)
@@ -296,12 +291,10 @@
         functools.partial(rest_kernel, conv, axis), sums, [groups, products_rest], smem=1, n=6
     )
 
-    hidden, *pieces = call(
+    hidden, pieces = call(
         first_kernel,
         [
             shape((8, 64, CHANNELS), BF16),
-            piece,
-            piece,
             shape((2, SLOT, CHANNELS), BF16),
         ],
         [
@@ -315,17 +308,15 @@
         n=4,
         vmem_limit=60 * 1024 * 1024,
     )(latent, weight_one, weight_two, gain_one)
-    (weights_one, packed_one), (weights_two, packed_two) = gather_weights(*pieces)
+    weights_one, weights_two = gather_weights(pieces)
     gathered = lax.all_to_all(hidden, "z", 0, 0)
     field = call(field_kernel, shape((LANES, CHANNELS), BF16), n=1, flops=10**11)(gathered)
-    weights_one += (swap_cores(packed_one),)
     pair = call(pair_one_kernel, half, [group, products], smem=1, n=6)(ids, field, *weights_one)
-    own, earlier = exchange(ids, swap_chips(pair), *rest(0, 1)(ids, field, *weights_one))
-    middle = call(middle_kernel, shape((8, BLOCK, LANES), BF16), smem=1, anywhere=1, n=5)(
-        ids, packed_two, own, earlier, bias_one
+    own, earlier = exchange(ids, bias_one, swap_chips(pair), *rest(0, 1)(ids, field, *weights_one))
+    middle = call(middle_kernel, shape((8, BLOCK, LANES), BF16), anywhere=1, n=3)(
+        weights_two[1], own, earlier
     )
     gathered = lax.all_to_all(middle, "z", 0, 0)
-    weights_two += (swap_cores(packed_two),)
     pair, field = call(
         pair_two_kernel,
         [half, shape((CHANNELS, LANES), BF16)],
@@ -333,13 +324,12 @@
         smem=1,
         n=7,
     )(ids, gathered, gain_two, *weights_two)
-    own, earlier = exchange(ids, swap_chips(pair), *rest(1, 0)(ids, field, *weights_two))
+    own, earlier = exchange(ids, bias_two, swap_chips(pair), *rest(1, 0)(ids, field, *weights_two))
     pieces, kept = call(
         spread_kernel,
         [shape((8, 24, 128), BF16), shape((64, CHANNELS), BF16)],
-        smem=1,
-        n=5,
-    )(ids, own, earlier, bias_two, latent)
+        n=3,
+    )(own, earlier, latent)
     pieces = lax.all_to_all(pieces, "z", 0, 0)
     out = call(finish_kernel, shape((64, CHANNELS), BF16), n=2)(kept, pieces)
     return out.reshape(2, 1, 32, CHANNELS)

time: 102 us -> 98.4 us (0.965)
  the two profiles are of different devices: /device:TPU:32 before, /device:TPU:24 now
where the time goes in v6:
time: 98.4 us; the launch traced here: 97.8 us
  blocking collectives  43.4 us (44%)
  starting transfers between devices  36.5 us (37%)
  Pallas kernels  10.5 us (11%)
  waiting for transfers between devices  7.13 us (7%)
    all_to_all x1, blocking collectives, per_device(): gathered = lax.all_to_all(middle, 'z', 0, 0)  21.7 us
    all_to_all x1, blocking collectives, per_device(): pieces = lax.all_to_all(pieces, 'z', 0, 0)  10.6 us
    all_to_all x1, starting transfers between devices, per_device(): gathered = lax.all_to_all(hidden, 'z', 0, 0)  10.5 us
    ppermute x2, starting transfers between devices, exchange(): return (own, lax.ppermute(later, 't', [(i, i + 1) for i in range(7)]))  8.05 us
    ppermute x2, starting transfers between devices, gather_weights(): lax.ppermute(both, ('x', 'core'), hops)  5.84 us
    ppermute x1, starting transfers between devices, gather_weights(): far = lax.ppermute(pieces, 'x', [(x, x ^ 2) for x in range(4)])  4.93 us
    all_gather x2, blocking collectives, gather_weights(): lax.all_gather(lax.ppermute(both, ('x', 'core'), hops), 'core', axis=0)  4.65 us
    ppermute x2, starting transfers between devices, swap_chips(): return lax.ppermute(pair, ('x', 'core'), swaps)  4.53 us
  transfers between devices with their start and end apart: 9, of which 5 were waited for; matrix products, arithmetic and copies ran while one was open for 0% of the time, Pallas kernels for 5%

profile of v6, /device:TPU:24, one launch (start us, length us, event | category | flops | bytes accessed | tf_op | source)
XLA Modules:
  0.0 97.8 jit_solution(4972309375798646506)
XLA Ops:
  0.0 2.0 %shard_map.73 = (bf16[8,64,384]{2,1,0:T(8,128)(2,1)}, bf16[2,240,384]{2,1,0:T(8,128)(2,1)}) custom-call(bf16[64,384]{1,0:T(8,128)(2,1)} %bitcast.32, bf16[27,6,384]{2,1,0:T(8,128)(2,1)} %bitcast.34, bf16[27,6,384]{2,1,0:T(8,128)(2,1)} %bitcast.35, f32[384]{0:T(512)} %gain_hbm.1), custom_call_target="tpu_custom_call" | custom-call | tf_op jit(solution)/shard_map/pallas_call | solution.py:294
  2.0 4.9 %collective-permute-start.2 = (bf16[2,240,384]{2,1,0:T(8,128)(2,1)}, bf16[2,240,384]{2,1,0:T(8,128)(2,1)S(1)}, u32[]{:S(2)}, u32[]{:S(2)}) collective-permute-start(bf16[2,240,384]{2,1,0:T(8,128)(2,1)} %get-tuple-element.19), channel_id=1, source_target_pairs={{0,4},{2,6},{4,0},{6,2},{1,5},{3,7},{5,1},{7,3},{8,12},{10,14},{12... | collective-permute-start | bytes 1105928 | tf_op jit(solution)/shard_map/ppermute | solution.py:267
  6.9 10.5 %all-to-all-start = ((bf16[8,64,384]{2,1,0:T(8,128)(2,1)}), bf16[8,64,384]{2,1,0:T(8,128)(2,1)S(1)}, u32[]{:S(2)}, u32[]{:S(2)}) async-start(bf16[8,64,384]{2,1,0:T(8,128)(2,1)} %get-tuple-element.20), calls=%async_computation | async-start | bytes 786432 | tf_op jit(solution)/shard_map/all_to_all | solution.py:312
  17.4 2.3 %all-gather = bf16[2,480,384]{2,1,0:T(8,128)(2,1)S(1)} all-gather(bf16[2,240,384]{2,1,0:T(8,128)(2,1)S(1)} %copy-done.4), channel_id=2, replica_groups=mesh['t'=8,'z'=8,'x'=4,'core'=2] {'core'}, dimensions={1}, use_global_device_ids=true | all-gather | bytes 1105920 | tf_op jit(solution)/shard_map/all_gather | solution.py:269
  19.8 2.5 %collective-permute-start.1 = (bf16[2,240,384]{2,1,0:T(8,128)(2,1)S(1)}, bf16[2,240,384]{2,1,0:T(8,128)(2,1)S(1)}, u32[]{:S(2)}, u32[]{:S(2)}) collective-permute-start(bf16[2,240,384]{2,1,0:T(8,128)(2,1)S(1)} %bitcast.27), channel_id=1, source_target_pairs={{0,2},{1,7},{2,0},{3,5},{4,6},{5,3},{6,4},{7,1},{8,10},{9,15},{10,... | collective-permute-start | bytes 1105928 | tf_op jit(solution)/shard_map/ppermute | solution.py:272
  22.3 3.3 %collective-permute-start = (bf16[2,240,384]{2,1,0:T(8,128)(2,1)S(1)}, bf16[2,240,384]{2,1,0:T(8,128)(2,1)S(1)}, u32[]{:S(2)}, u32[]{:S(2)}) collective-permute-start(bf16[2,240,384]{2,1,0:T(8,128)(2,1)S(1)} %bitcast.24), channel_id=1, source_target_pairs={{0,2},{1,7},{2,0},{3,5},{4,6},{5,3},{6,4},{7,1},{8,10},{9,15},{10,... | collective-permute-start | bytes 1105928 | tf_op jit(solution)/shard_map/ppermute | solution.py:272
  25.7 0.1 pad_add_fusion.ids
  25.8 2.7 %collective-permute-start.3 = (bf16[2,240,384]{2,1,0:T(8,128)(2,1)S(1)}, bf16[2,240,384]{2,1,0:T(8,128)(2,1)S(1)}, u32[]{:S(2)}, u32[]{:S(2)}) collective-permute-start(bf16[2,240,384]{2,1,0:T(8,128)(2,1)S(1)} %collective-permute-done.2.rest_2_), channel_id=1, source_target_pairs={{0,1},{1,0},{2,3},{3,2},{4,5},{5,4},{6,7},{7,6},{8,9},{9,8},{10,11... | collective-permute-start | bytes 1105928 | tf_op jit(solution)/shard_map/ppermute | solution.py:241
  28.5 0.8 collective-permute-done.1
  29.2 2.3 %all-gather.2 = bf16[4,240,384]{2,1,0:T(8,128)(2,1)S(1)} all-gather(bf16[2,240,384]{2,1,0:T(8,128)(2,1)S(1)} %collective-permute-done.1), channel_id=4, replica_groups=mesh['t'=8,'z'=8,'x'=4,'core'=2] {'core'}, dimensions={0}, use_global_device_ids=true | all-gather | bytes 1105920 | tf_op jit(solution)/shard_map/all_gather | solution.py:272
  31.5 0.3 all-to-all-done.gathered
  31.9 1.2 %shard_map.76 = bf16[64,1024]{1,0:T(8,128)(2,1)S(1)} custom-call(s32[3]{0:T(128)S(1)} %pad_add_fusion.ids, bf16[512,384]{1,0:T(8,128)(2,1)S(1)} %shard_map.74.field, bf16[2,240,384]{2,1,0:T(8,128)(2,1)S(1)} %bitcast.28, bf16[2,2,240,384]{3,2,1,0:T(8,128)(2,1)S(1)} %bitcast.22, bf16[2,240,384]{2,1,0:T(8,128)(2,1)S(1)} %collective-permute-done.2.rest_2_, ...), custom_call_target="tpu_custom_call" | custom-call | tf_op jit(solution)/shard_map/pallas_call | solution.py:314
  33.0 2.6 %collective-permute-start.4 = (bf16[64,1024]{1,0:T(8,128)(2,1)S(1)}, bf16[64,1024]{1,0:T(8,128)(2,1)S(1)}, u32[]{:S(2)}, u32[]{:S(2)}) collective-permute-start(bf16[64,1024]{1,0:T(8,128)(2,1)S(1)} %shard_map.76), channel_id=1, source_target_pairs={{1,2},{2,1},{3,4},{4,3},{5,6},{6,5},{7,0},{0,7},{9,10},{10,9},{11,... | collective-permute-start | bytes 393224 | tf_op jit(solution)/shard_map/ppermute | solution.py:249
  35.6 1.5 %shard_map.75 = (f32[64,1024]{1,0:T(8,128)S(1)}, bf16[64,1024]{1,0:T(8,128)(2,1)S(1)}) custom-call(s32[3]{0:T(128)S(1)} %pad_add_fusion.ids, bf16[512,384]{1,0:T(8,128)(2,1)S(1)} %shard_map.74.field, bf16[2,240,384]{2,1,0:T(8,128)(2,1)S(1)} %bitcast.29, bf16[2,2,240,384]{3,2,1,0:T(8,128)(2,1)S(1)} %bitcast.23, ...), custom_call_target="tpu_custom_call" | custom-call | tf_op jit(solution)/shard_map/pallas_call | solution.py:315
  37.1 2.0 %all-gather.3 = bf16[128,1024]{1,0:T(8,128)(2,1)S(1)} all-gather(bf16[64,1024]{1,0:T(8,128)(2,1)S(1)} %get-tuple-element.22), channel_id=5, replica_groups=mesh['t'=8,'z'=8,'x'=4,'core'=2] {'core'}, dimensions={0}, use_global_device_ids=true | all-gather | bytes 393216 | tf_op jit(solution)/shard_map/all_gather | solution.py:253
  39.1 1.4 %collective-permute-done.4.pair = bf16[64,1024]{1,0:T(8,128)(2,1)S(1)} collective-permute-done((bf16[64,1024]{1,0:T(8,128)(2,1)S(1)}, bf16[64,1024]{1,0:T(8,128)(2,1)S(1)}, u32[]{:S(2)}, u32[]{:S(2)}) %collective-permute-start.4) | collective-permute-done | bytes 131104 | tf_op jit(solution)/shard_map/ppermute | solution.py:249
  40.5 0.8 shard_map.77
  41.3 4.7 %collective-permute-start.5 = (bf16[64,512]{1,0:T(8,128)(2,1)S(1)}, bf16[64,512]{1,0:T(8,128)(2,1)S(1)}, u32[]{:S(2)}, u32[]{:S(2)}) collective-permute-start(bf16[64,512]{1,0:T(8,128)(2,1)S(1)} %get-tuple-element.24), channel_id=1, source_target_pairs={{0,64},{64,128},{128,192},{192,256},{256,320},{320,384},{384,448},... | collective-permute-start | bytes 196616 | tf_op jit(solution)/shard_map/ppermute | solution.py:260
  46.0 2.3 %all-gather.1 = bf16[4,240,384]{2,1,0:T(8,128)(2,1)S(1)} all-gather(bf16[2,240,384]{2,1,0:T(8,128)(2,1)S(1)} %collective-permute-done), channel_id=3, replica_groups=mesh['t'=8,'z'=8,'x'=4,'core'=2] {'core'}, dimensions={0}, use_global_device_ids=true | all-gather | bytes 1105920 | tf_op jit(solution)/shard_map/all_gather | solution.py:272
  48.3 0.2 shard_map.78
  48.5 21.7 %all_to_all.15.gathered = bf16[8,48,512]{2,1,0:T(8,128)(2,1)S(1)} all-to-all(bf16[8,48,512]{2,1,0:T(8,128)(2,1)S(1)} %shard_map.78), channel_id=1, replica_groups=mesh['t'=8,'z'=8,'x'=4,'core'=2] {'z'}, dimensions={0} | all-to-all | bytes 786432 | tf_op jit(solution)/shard_map/all_to_all | solution.py:319
  70.2 1.4 %shard_map.79 = (bf16[64,1024]{1,0:T(8,128)(2,1)S(1)}, bf16[384,512]{1,0:T(8,128)(2,1)S(1)}) custom-call(s32[3]{0:T(128)S(1)} %pad_add_fusion.ids, bf16[8,48,512]{2,1,0:T(8,128)(2,1)S(1)} %all_to_all.15.gathered, f32[384]{0:T(512)S(1)} %copy-done.3, bf16[2,240,384]{2,1,0:T(8,128)(2,1)S(1)} %bitcast.25, bf16[2,2,240,384]{3,2,1,0:T(8,128)(2,1)S(1)} %bitcast.20, ...), custom_call_target="tpu_custom_call" | custom-call | tf_op jit(solution)/shard_map/pallas_call | solution.py:320
  71.6 1.9 %collective-permute-start.6 = (bf16[64,1024]{1,0:T(8,128)(2,1)S(1)}, bf16[64,1024]{1,0:T(8,128)(2,1)S(1)}, u32[]{:S(2)}, u32[]{:S(2)}) collective-permute-start(bf16[64,1024]{1,0:T(8,128)(2,1)S(1)} %get-tuple-element.28), channel_id=1, source_target_pairs={{1,2},{2,1},{3,4},{4,3},{5,6},{6,5},{7,0},{0,7},{9,10},{10,9},{11,... | collective-permute-start | bytes 393224 | tf_op jit(solution)/shard_map/ppermute | solution.py:249
  73.6 1.5 %shard_map.80 = (f32[64,1024]{1,0:T(8,128)S(1)}, bf16[64,1024]{1,0:T(8,128)(2,1)S(1)}) custom-call(s32[3]{0:T(128)S(1)} %pad_add_fusion.ids, bf16[384,512]{1,0:T(8,128)(2,1)S(1)} %get-tuple-element.25.field, bf16[2,240,384]{2,1,0:T(8,128)(2,1)S(1)} %bitcast.26, bf16[2,2,240,384]{3,2,1,0:T(8,128)(2,1)S(1)} %bitcast.21, ...), custom_call_target="tpu_custom_call" | custom-call | tf_op jit(solution)/shard_map/pallas_call | solution.py:327
  75.1 2.1 %all-gather.4 = bf16[128,1024]{1,0:T(8,128)(2,1)S(1)} all-gather(bf16[64,1024]{1,0:T(8,128)(2,1)S(1)} %get-tuple-element.27), channel_id=6, replica_groups=mesh['t'=8,'z'=8,'x'=4,'core'=2] {'core'}, dimensions={0}, use_global_device_ids=true | all-gather | bytes 393216 | tf_op jit(solution)/shard_map/all_gather | solution.py:253
  77.2 1.9 %collective-permute-done.6.pair = bf16[64,1024]{1,0:T(8,128)(2,1)S(1)} collective-permute-done((bf16[64,1024]{1,0:T(8,128)(2,1)S(1)}, bf16[64,1024]{1,0:T(8,128)(2,1)S(1)}, u32[]{:S(2)}, u32[]{:S(2)}) %collective-permute-start.6) | collective-permute-done | bytes 131104 | tf_op jit(solution)/shard_map/ppermute | solution.py:249
  79.2 0.8 shard_map.81
  79.9 3.4 %collective-permute-start.7 = (bf16[64,512]{1,0:T(8,128)(2,1)S(1)}, bf16[64,512]{1,0:T(8,128)(2,1)S(1)}, u32[]{:S(2)}, u32[]{:S(2)}) collective-permute-start(bf16[64,512]{1,0:T(8,128)(2,1)S(1)} %get-tuple-element.30), channel_id=1, source_target_pairs={{0,64},{64,128},{128,192},{192,256},{256,320},{320,384},{384,448},... | collective-permute-start | bytes 196616 | tf_op jit(solution)/shard_map/ppermute | solution.py:260
  83.3 2.8 %collective-permute-done.7.earlier = bf16[64,512]{1,0:T(8,128)(2,1)S(1)} collective-permute-done((bf16[64,512]{1,0:T(8,128)(2,1)S(1)}, bf16[64,512]{1,0:T(8,128)(2,1)S(1)}, u32[]{:S(2)}, u32[]{:S(2)}) %collective-permute-start.7) | collective-permute-done | bytes 65568 | tf_op jit(solution)/shard_map/ppermute | solution.py:260
  86.1 0.2 shard_map.82
  86.3 10.6 %all_to_all.16.gathered = bf16[8,24,128]{2,1,0:T(8,128)(2,1)S(1)} all-to-all(bf16[8,24,128]{2,1,0:T(8,128)(2,1)S(1)} %get-tuple-element.32), channel_id=1, replica_groups=mesh['t'=8,'z'=8,'x'=4,'core'=2] {'z'}, dimensions={0} | all-to-all | bytes 98304 | tf_op jit(solution)/shard_map/all_to_all | solution.py:333
  96.9 0.9 shard_map.83
  (16 shorter events, 0.1 us)
Async XLA Ops:
  2.0 23.8 %collective-permute-start.2 = (bf16[2,240,384]{2,1,0:T(8,128)(2,1)}, bf16[2,240,384]{2,1,0:T(8,128)(2,1)S(1)}, u32[]{:S(2)}, u32[]{:S(2)}) collective-permute-start(bf16[2,240,384]{2,1,0:T(8,128)(2,1)} %get-tuple-element.19), channel_id=1, source_target_pairs={{0,4},{2,6},{4,0},{6,2},{1,5},{3,7},{5,1},{7,3},{8,12},{10,14},{12... | collective-permute-start | bytes 1105928 | tf_op jit(solution)/shard_map/ppermute | solution.py:267
  6.9 10.5 %copy-start.4 = (bf16[2,240,384]{2,1,0:T(8,128)(2,1)S(1)}, bf16[2,240,384]{2,1,0:T(8,128)(2,1)}, u32[]{:S(2)}) copy-start(bf16[2,240,384]{2,1,0:T(8,128)(2,1)} %get-tuple-element.19) | copy-start | bytes 1105924
  6.9 24.9 %all-to-all-start = ((bf16[8,64,384]{2,1,0:T(8,128)(2,1)}), bf16[8,64,384]{2,1,0:T(8,128)(2,1)S(1)}, u32[]{:S(2)}, u32[]{:S(2)}) async-start(bf16[8,64,384]{2,1,0:T(8,128)(2,1)} %get-tuple-element.20), calls=%async_computation | async-start | bytes 786432 | tf_op jit(solution)/shard_map/all_to_all | solution.py:312
  19.8 9.4 %collective-permute-start.1 = (bf16[2,240,384]{2,1,0:T(8,128)(2,1)S(1)}, bf16[2,240,384]{2,1,0:T(8,128)(2,1)S(1)}, u32[]{:S(2)}, u32[]{:S(2)}) collective-permute-start(bf16[2,240,384]{2,1,0:T(8,128)(2,1)S(1)} %bitcast.27), channel_id=1, source_target_pairs={{0,2},{1,7},{2,0},{3,5},{4,6},{5,3},{6,4},{7,1},{8,10},{9,15},{10,... | collective-permute-start | bytes 1105928 | tf_op jit(solution)/shard_map/ppermute | solution.py:272
  22.3 23.7 %collective-permute-start = (bf16[2,240,384]{2,1,0:T(8,128)(2,1)S(1)}, bf16[2,240,384]{2,1,0:T(8,128)(2,1)S(1)}, u32[]{:S(2)}, u32[]{:S(2)}) collective-permute-start(bf16[2,240,384]{2,1,0:T(8,128)(2,1)S(1)} %bitcast.24), channel_id=1, source_target_pairs={{0,2},{1,7},{2,0},{3,5},{4,6},{5,3},{6,4},{7,1},{8,10},{9,15},{10,... | collective-permute-start | bytes 1105928 | tf_op jit(solution)/shard_map/ppermute | solution.py:272
  25.8 6.1 %collective-permute-start.3 = (bf16[2,240,384]{2,1,0:T(8,128)(2,1)S(1)}, bf16[2,240,384]{2,1,0:T(8,128)(2,1)S(1)}, u32[]{:S(2)}, u32[]{:S(2)}) collective-permute-start(bf16[2,240,384]{2,1,0:T(8,128)(2,1)S(1)} %collective-permute-done.2.rest_2_), channel_id=1, source_target_pairs={{0,1},{1,0},{2,3},{3,2},{4,5},{5,4},{6,7},{7,6},{8,9},{9,8},{10,11... | collective-permute-start | bytes 1105928 | tf_op jit(solution)/shard_map/ppermute | solution.py:241
  33.0 7.5 %collective-permute-start.4 = (bf16[64,1024]{1,0:T(8,128)(2,1)S(1)}, bf16[64,1024]{1,0:T(8,128)(2,1)S(1)}, u32[]{:S(2)}, u32[]{:S(2)}) collective-permute-start(bf16[64,1024]{1,0:T(8,128)(2,1)S(1)} %shard_map.76), channel_id=1, source_target_pairs={{1,2},{2,1},{3,4},{4,3},{5,6},{6,5},{7,0},{0,7},{9,10},{10,9},{11,... | collective-permute-start | bytes 393224 | tf_op jit(solution)/shard_map/ppermute | solution.py:249
  39.1 1.4 %copy-start.1 = (f32[384]{0:T(512)S(1)}, f32[384]{0:T(512)}, u32[]{:S(2)}) copy-start(f32[384]{0:T(512)} %bias.2) | copy-start | bytes 4612
  41.3 7.1 %collective-permute-start.5 = (bf16[64,512]{1,0:T(8,128)(2,1)S(1)}, bf16[64,512]{1,0:T(8,128)(2,1)S(1)}, u32[]{:S(2)}, u32[]{:S(2)}) collective-permute-start(bf16[64,512]{1,0:T(8,128)(2,1)S(1)} %get-tuple-element.24), channel_id=1, source_target_pairs={{0,64},{64,128},{128,192},{192,256},{256,320},{320,384},{384,448},... | collective-permute-start | bytes 196616 | tf_op jit(solution)/shard_map/ppermute | solution.py:260
  48.5 21.7 %copy-start.3 = (f32[384]{0:T(512)S(1)}, f32[384]{0:T(512)}, u32[]{:S(2)}) copy-start(f32[384]{0:T(512)} %gain.1) | copy-start | bytes 4612
  71.6 7.5 %collective-permute-start.6 = (bf16[64,1024]{1,0:T(8,128)(2,1)S(1)}, bf16[64,1024]{1,0:T(8,128)(2,1)S(1)}, u32[]{:S(2)}, u32[]{:S(2)}) collective-permute-start(bf16[64,1024]{1,0:T(8,128)(2,1)S(1)} %get-tuple-element.28), channel_id=1, source_target_pairs={{1,2},{2,1},{3,4},{4,3},{5,6},{6,5},{7,0},{0,7},{9,10},{10,9},{11,... | collective-permute-start | bytes 393224 | tf_op jit(solution)/shard_map/ppermute | solution.py:249
  77.2 1.9 %copy-start.2 = (f32[384]{0:T(512)S(1)}, f32[384]{0:T(512)}, u32[]{:S(2)}) copy-start(f32[384]{0:T(512)} %bias.3) | copy-start | bytes 4612
  79.1 6.9 %copy-start = (bf16[2,1,32,384]{3,2,1,0:T(8,128)(2,1)S(1)}, bf16[2,1,32,384]{3,2,1,0:T(8,128)(2,1)}, u32[]{:S(2)}) copy-start(bf16[2,1,32,384]{3,2,1,0:T(8,128)(2,1)} %param.7) | copy-start | bytes 147460
  79.9 6.2 %collective-permute-start.7 = (bf16[64,512]{1,0:T(8,128)(2,1)S(1)}, bf16[64,512]{1,0:T(8,128)(2,1)S(1)}, u32[]{:S(2)}, u32[]{:S(2)}) collective-permute-start(bf16[64,512]{1,0:T(8,128)(2,1)S(1)} %get-tuple-element.30), channel_id=1, source_target_pairs={{0,64},{64,128},{128,192},{192,256},{256,320},{320,384},{384,448},... | collective-permute-start | bytes 196616 | tf_op jit(solution)/shard_map/ppermute | solution.py:260

commit v7 on v6

--- a/solution.py
+++ b/solution.py
@@ -126,7 +126,8 @@
     taps(products, lambda slot: slot * GROUP, emit)
 
 
-def field_kernel(gathered, field):
+def field_kernel(gathered, bias, field, kept):
+    kept[...] = bias[...]
     for z in range(8):
         for f in range(2):
             field[pl.ds(256 * f + 32 * z, 32), :] = gathered[z, pl.ds(32 * f, 32), :]
@@ -137,8 +138,9 @@
     pair_sums(0, 1, ids, field[...], pieces, pair, group, products)
 
 
-def pair_two_kernel(ids, gathered, gain, *rest):
-    *pieces, pair, field, group, products = rest
+def pair_two_kernel(ids, gathered, gain, bias, *rest):
+    *pieces, pair, field, kept, group, products = rest
+    kept[...] = bias[...]
     values = gathered[...].reshape(CHANNELS, LANES).astype(F32)
     mean = jnp.mean(values * values, axis=0, keepdims=True)
     square = (CHANNELS, CHANNELS)
@@ -310,20 +312,25 @@
     )(latent, weight_one, weight_two, gain_one)
     weights_one, weights_two = gather_weights(pieces)
     gathered = lax.all_to_all(hidden, "z", 0, 0)
-    field = call(field_kernel, shape((LANES, CHANNELS), BF16), n=1, flops=10**11)(gathered)
+    field, bias_one = call(
+        field_kernel,
+        [shape((LANES, CHANNELS), BF16), shape((CHANNELS,), F32)],
+        n=2,
+        flops=10**11,
+    )(gathered, bias_one)
     pair = call(pair_one_kernel, half, [group, products], smem=1, n=6)(ids, field, *weights_one)
     own, earlier = exchange(ids, bias_one, swap_chips(pair), *rest(0, 1)(ids, field, *weights_one))
     middle = call(middle_kernel, shape((8, BLOCK, LANES), BF16), anywhere=1, n=3)(
         weights_two[1], own, earlier
     )
     gathered = lax.all_to_all(middle, "z", 0, 0)
-    pair, field = call(
+    pair, field, bias_two = call(
         pair_two_kernel,
-        [half, shape((CHANNELS, LANES), BF16)],
+        [half, shape((CHANNELS, LANES), BF16), shape((CHANNELS,), F32)],
         [group, products],
         smem=1,
-        n=7,
-    )(ids, gathered, gain_two, *weights_two)
+        n=8,
+    )(ids, gathered, gain_two, bias_two, *weights_two)
     own, earlier = exchange(ids, bias_two, swap_chips(pair), *rest(1, 0)(ids, field, *weights_two))
     pieces, kept = call(
         spread_kernel,

time: 98.4 us -> 98.4 us (level)
  no operation moved by 1% of the time
where the time goes in v7:
time: 98.4 us; the launch traced here: 97.8 us
  blocking collectives  43.3 us (44%)
  starting transfers between devices  36.2 us (37%)
  Pallas kernels  10.5 us (11%)
  waiting for transfers between devices  7.54 us (8%)
    all_to_all x1, blocking collectives, per_device(): gathered = lax.all_to_all(middle, 'z', 0, 0)  21.7 us
    all_to_all x1, blocking collectives, per_device(): pieces = lax.all_to_all(pieces, 'z', 0, 0)  10.6 us
    all_to_all x1, starting transfers between devices, per_device(): gathered = lax.all_to_all(hidden, 'z', 0, 0)  10.5 us
    ppermute x2, starting transfers between devices, exchange(): return (own, lax.ppermute(later, 't', [(i, i + 1) for i in range(7)]))  7.61 us
    ppermute x2, starting transfers between devices, gather_weights(): lax.ppermute(both, ('x', 'core'), hops)  5.84 us
    ppermute x1, starting transfers between devices, gather_weights(): far = lax.ppermute(pieces, 'x', [(x, x ^ 2) for x in range(4)])  4.93 us
    all_gather x2, blocking collectives, gather_weights(): lax.all_gather(lax.ppermute(both, ('x', 'core'), hops), 'core', axis=0)  4.65 us
    ppermute x2, starting transfers between devices, swap_chips(): return lax.ppermute(pair, ('x', 'core'), swaps)  4.51 us
  transfers between devices with their start and end apart: 9, of which 5 were waited for; matrix products, arithmetic and copies ran while one was open for 0% of the time, Pallas kernels for 5%

profile of v7, /device:TPU:24, one launch (start us, length us, event | category | flops | bytes accessed | tf_op | source)
XLA Modules:
  0.0 97.8 jit_solution(7857985602783806084)
XLA Ops:
  0.0 2.0 %shard_map.73 = (bf16[8,64,384]{2,1,0:T(8,128)(2,1)}, bf16[2,240,384]{2,1,0:T(8,128)(2,1)}) custom-call(bf16[64,384]{1,0:T(8,128)(2,1)} %bitcast.32, bf16[27,6,384]{2,1,0:T(8,128)(2,1)} %bitcast.34, bf16[27,6,384]{2,1,0:T(8,128)(2,1)} %bitcast.35, f32[384]{0:T(512)} %gain_hbm.1), custom_call_target="tpu_custom_call" | custom-call | tf_op jit(solution)/shard_map/pallas_call | solution.py:296
  2.0 4.9 %collective-permute-start.2 = (bf16[2,240,384]{2,1,0:T(8,128)(2,1)}, bf16[2,240,384]{2,1,0:T(8,128)(2,1)S(1)}, u32[]{:S(2)}, u32[]{:S(2)}) collective-permute-start(bf16[2,240,384]{2,1,0:T(8,128)(2,1)} %get-tuple-element.22), channel_id=1, source_target_pairs={{0,4},{2,6},{4,0},{6,2},{1,5},{3,7},{5,1},{7,3},{8,12},{10,14},{12... | collective-permute-start | bytes 1105928 | tf_op jit(solution)/shard_map/ppermute | solution.py:269
  6.9 10.5 %all-to-all-start = ((bf16[8,64,384]{2,1,0:T(8,128)(2,1)}), bf16[8,64,384]{2,1,0:T(8,128)(2,1)S(1)}, u32[]{:S(2)}, u32[]{:S(2)}) async-start(bf16[8,64,384]{2,1,0:T(8,128)(2,1)} %get-tuple-element.23), calls=%async_computation | async-start | bytes 786432 | tf_op jit(solution)/shard_map/all_to_all | solution.py:314
  17.4 2.3 %all-gather = bf16[2,480,384]{2,1,0:T(8,128)(2,1)S(1)} all-gather(bf16[2,240,384]{2,1,0:T(8,128)(2,1)S(1)} %copy-done.4), channel_id=2, replica_groups=mesh['t'=8,'z'=8,'x'=4,'core'=2] {'core'}, dimensions={1}, use_global_device_ids=true | all-gather | bytes 1105920 | tf_op jit(solution)/shard_map/all_gather | solution.py:271
  19.8 2.5 %collective-permute-start.1 = (bf16[2,240,384]{2,1,0:T(8,128)(2,1)S(1)}, bf16[2,240,384]{2,1,0:T(8,128)(2,1)S(1)}, u32[]{:S(2)}, u32[]{:S(2)}) collective-permute-start(bf16[2,240,384]{2,1,0:T(8,128)(2,1)S(1)} %bitcast.27), channel_id=1, source_target_pairs={{0,2},{1,7},{2,0},{3,5},{4,6},{5,3},{6,4},{7,1},{8,10},{9,15},{10,... | collective-permute-start | bytes 1105928 | tf_op jit(solution)/shard_map/ppermute | solution.py:274
  22.3 3.3 %collective-permute-start = (bf16[2,240,384]{2,1,0:T(8,128)(2,1)S(1)}, bf16[2,240,384]{2,1,0:T(8,128)(2,1)S(1)}, u32[]{:S(2)}, u32[]{:S(2)}) collective-permute-start(bf16[2,240,384]{2,1,0:T(8,128)(2,1)S(1)} %bitcast.24), channel_id=1, source_target_pairs={{0,2},{1,7},{2,0},{3,5},{4,6},{5,3},{6,4},{7,1},{8,10},{9,15},{10,... | collective-permute-start | bytes 1105928 | tf_op jit(solution)/shard_map/ppermute | solution.py:274
  25.7 0.1 pad_add_fusion.ids
  25.8 2.8 %collective-permute-start.3 = (bf16[2,240,384]{2,1,0:T(8,128)(2,1)S(1)}, bf16[2,240,384]{2,1,0:T(8,128)(2,1)S(1)}, u32[]{:S(2)}, u32[]{:S(2)}) collective-permute-start(bf16[2,240,384]{2,1,0:T(8,128)(2,1)S(1)} %collective-permute-done.2.rest_2_), channel_id=1, source_target_pairs={{0,1},{1,0},{2,3},{3,2},{4,5},{5,4},{6,7},{7,6},{8,9},{9,8},{10,11... | collective-permute-start | bytes 1105928 | tf_op jit(solution)/shard_map/ppermute | solution.py:243
  28.6 0.6 collective-permute-done.1
  29.2 2.3 %all-gather.2 = bf16[4,240,384]{2,1,0:T(8,128)(2,1)S(1)} all-gather(bf16[2,240,384]{2,1,0:T(8,128)(2,1)S(1)} %collective-permute-done.1), channel_id=4, replica_groups=mesh['t'=8,'z'=8,'x'=4,'core'=2] {'core'}, dimensions={0}, use_global_device_ids=true | all-gather | bytes 1105920 | tf_op jit(solution)/shard_map/all_gather | solution.py:274
  31.5 0.3 all-to-all-done.gathered
  31.9 1.2 %shard_map.76 = bf16[64,1024]{1,0:T(8,128)(2,1)S(1)} custom-call(s32[3]{0:T(128)S(1)} %pad_add_fusion.ids, bf16[512,384]{1,0:T(8,128)(2,1)S(1)} %get-tuple-element.24.field, bf16[2,240,384]{2,1,0:T(8,128)(2,1)S(1)} %bitcast.28, bf16[2,2,240,384]{3,2,1,0:T(8,128)(2,1)S(1)} %bitcast.22, bf16[2,240,384]{2,1,0:T(8,128)(2,1)S(1)} %collective-permute-done.2.rest_2_, ...), custom_call_target="tpu_custom_call" | custom-call | tf_op jit(solution)/shard_map/pallas_call | solution.py:321
  33.0 2.6 %collective-permute-start.4 = (bf16[64,1024]{1,0:T(8,128)(2,1)S(1)}, bf16[64,1024]{1,0:T(8,128)(2,1)S(1)}, u32[]{:S(2)}, u32[]{:S(2)}) collective-permute-start(bf16[64,1024]{1,0:T(8,128)(2,1)S(1)} %shard_map.76), channel_id=1, source_target_pairs={{1,2},{2,1},{3,4},{4,3},{5,6},{6,5},{7,0},{0,7},{9,10},{10,9},{11,... | collective-permute-start | bytes 393224 | tf_op jit(solution)/shard_map/ppermute | solution.py:251
  35.6 1.5 %shard_map.75 = (f32[64,1024]{1,0:T(8,128)S(1)}, bf16[64,1024]{1,0:T(8,128)(2,1)S(1)}) custom-call(s32[3]{0:T(128)S(1)} %pad_add_fusion.ids, bf16[512,384]{1,0:T(8,128)(2,1)S(1)} %get-tuple-element.24.field, bf16[2,240,384]{2,1,0:T(8,128)(2,1)S(1)} %bitcast.29, bf16[2,2,240,384]{3,2,1,0:T(8,128)(2,1)S(1)} %bitcast.23, ...), custom_call_target="tpu_custom_call" | custom-call | tf_op jit(solution)/shard_map/pallas_call | solution.py:322
  37.2 2.0 %all-gather.3 = bf16[128,1024]{1,0:T(8,128)(2,1)S(1)} all-gather(bf16[64,1024]{1,0:T(8,128)(2,1)S(1)} %get-tuple-element.26), channel_id=5, replica_groups=mesh['t'=8,'z'=8,'x'=4,'core'=2] {'core'}, dimensions={0}, use_global_device_ids=true | all-gather | bytes 393216 | tf_op jit(solution)/shard_map/all_gather | solution.py:255
  39.1 1.4 %collective-permute-done.4.pair = bf16[64,1024]{1,0:T(8,128)(2,1)S(1)} collective-permute-done((bf16[64,1024]{1,0:T(8,128)(2,1)S(1)}, bf16[64,1024]{1,0:T(8,128)(2,1)S(1)}, u32[]{:S(2)}, u32[]{:S(2)}) %collective-permute-start.4) | collective-permute-done | bytes 131104 | tf_op jit(solution)/shard_map/ppermute | solution.py:251
  40.5 0.8 shard_map.77
  41.3 4.7 %collective-permute-start.5 = (bf16[64,512]{1,0:T(8,128)(2,1)S(1)}, bf16[64,512]{1,0:T(8,128)(2,1)S(1)}, u32[]{:S(2)}, u32[]{:S(2)}) collective-permute-start(bf16[64,512]{1,0:T(8,128)(2,1)S(1)} %get-tuple-element.29), channel_id=1, source_target_pairs={{0,64},{64,128},{128,192},{192,256},{256,320},{320,384},{384,448},... | collective-permute-start | bytes 196616 | tf_op jit(solution)/shard_map/ppermute | solution.py:262
  46.0 2.3 %all-gather.1 = bf16[4,240,384]{2,1,0:T(8,128)(2,1)S(1)} all-gather(bf16[2,240,384]{2,1,0:T(8,128)(2,1)S(1)} %collective-permute-done), channel_id=3, replica_groups=mesh['t'=8,'z'=8,'x'=4,'core'=2] {'core'}, dimensions={0}, use_global_device_ids=true | all-gather | bytes 1105920 | tf_op jit(solution)/shard_map/all_gather | solution.py:274
  48.3 0.2 shard_map.78
  48.5 21.7 %all_to_all.15.gathered = bf16[8,48,512]{2,1,0:T(8,128)(2,1)S(1)} all-to-all(bf16[8,48,512]{2,1,0:T(8,128)(2,1)S(1)} %shard_map.78), channel_id=1, replica_groups=mesh['t'=8,'z'=8,'x'=4,'core'=2] {'z'}, dimensions={0} | all-to-all | bytes 786432 | tf_op jit(solution)/shard_map/all_to_all | solution.py:326
  70.3 1.4 %shard_map.79 = (bf16[64,1024]{1,0:T(8,128)(2,1)S(1)}, bf16[384,512]{1,0:T(8,128)(2,1)S(1)}, f32[384]{0:T(512)S(1)}) custom-call(s32[3]{0:T(128)S(1)} %pad_add_fusion.ids, bf16[8,48,512]{2,1,0:T(8,128)(2,1)S(1)} %all_to_all.15.gathered, f32[384]{0:T(512)S(1)} %copy-done.1, f32[384]{0:T(512)S(1)} %copy-done.2, bf16[2,240,384]{2,1,0:T(8,128)(2,1)S(1)} %bitcast.25, ...), custom_call_target="tpu_custom_call" | custom-call | tf_op jit(solution)/shard_map/pallas_call | solution.py:327
  71.7 1.9 %collective-permute-start.6 = (bf16[64,1024]{1,0:T(8,128)(2,1)S(1)}, bf16[64,1024]{1,0:T(8,128)(2,1)S(1)}, u32[]{:S(2)}, u32[]{:S(2)}) collective-permute-start(bf16[64,1024]{1,0:T(8,128)(2,1)S(1)} %get-tuple-element.33), channel_id=1, source_target_pairs={{1,2},{2,1},{3,4},{4,3},{5,6},{6,5},{7,0},{0,7},{9,10},{10,9},{11,... | collective-permute-start | bytes 393224 | tf_op jit(solution)/shard_map/ppermute | solution.py:251
  73.6 1.5 %shard_map.80 = (f32[64,1024]{1,0:T(8,128)S(1)}, bf16[64,1024]{1,0:T(8,128)(2,1)S(1)}) custom-call(s32[3]{0:T(128)S(1)} %pad_add_fusion.ids, bf16[384,512]{1,0:T(8,128)(2,1)S(1)} %get-tuple-element.30.field, bf16[2,240,384]{2,1,0:T(8,128)(2,1)S(1)} %bitcast.26, bf16[2,2,240,384]{3,2,1,0:T(8,128)(2,1)S(1)} %bitcast.21, ...), custom_call_target="tpu_custom_call" | custom-call | tf_op jit(solution)/shard_map/pallas_call | solution.py:334
  75.1 2.0 %all-gather.4 = bf16[128,1024]{1,0:T(8,128)(2,1)S(1)} all-gather(bf16[64,1024]{1,0:T(8,128)(2,1)S(1)} %get-tuple-element.32), channel_id=6, replica_groups=mesh['t'=8,'z'=8,'x'=4,'core'=2] {'core'}, dimensions={0}, use_global_device_ids=true | all-gather | bytes 393216 | tf_op jit(solution)/shard_map/all_gather | solution.py:255
  77.1 2.0 %collective-permute-done.6.pair = bf16[64,1024]{1,0:T(8,128)(2,1)S(1)} collective-permute-done((bf16[64,1024]{1,0:T(8,128)(2,1)S(1)}, bf16[64,1024]{1,0:T(8,128)(2,1)S(1)}, u32[]{:S(2)}, u32[]{:S(2)}) %collective-permute-start.6) | collective-permute-done | bytes 131104 | tf_op jit(solution)/shard_map/ppermute | solution.py:251
  79.2 0.8 shard_map.81
  79.9 2.9 %collective-permute-start.7 = (bf16[64,512]{1,0:T(8,128)(2,1)S(1)}, bf16[64,512]{1,0:T(8,128)(2,1)S(1)}, u32[]{:S(2)}, u32[]{:S(2)}) collective-permute-start(bf16[64,512]{1,0:T(8,128)(2,1)S(1)} %get-tuple-element.36), channel_id=1, source_target_pairs={{0,64},{64,128},{128,192},{192,256},{256,320},{320,384},{384,448},... | collective-permute-start | bytes 196616 | tf_op jit(solution)/shard_map/ppermute | solution.py:262
  82.9 3.2 %collective-permute-done.7.earlier = bf16[64,512]{1,0:T(8,128)(2,1)S(1)} collective-permute-done((bf16[64,512]{1,0:T(8,128)(2,1)S(1)}, bf16[64,512]{1,0:T(8,128)(2,1)S(1)}, u32[]{:S(2)}, u32[]{:S(2)}) %collective-permute-start.7) | collective-permute-done | bytes 65568 | tf_op jit(solution)/shard_map/ppermute | solution.py:262
  86.1 0.2 shard_map.82
  86.3 10.6 %all_to_all.16.gathered = bf16[8,24,128]{2,1,0:T(8,128)(2,1)S(1)} all-to-all(bf16[8,24,128]{2,1,0:T(8,128)(2,1)S(1)} %get-tuple-element.38), channel_id=1, replica_groups=mesh['t'=8,'z'=8,'x'=4,'core'=2] {'z'}, dimensions={0} | all-to-all | bytes 98304 | tf_op jit(solution)/shard_map/all_to_all | solution.py:340
  96.9 0.9 shard_map.83
  (16 shorter events, 0.1 us)
Async XLA Ops:
  2.0 23.8 %collective-permute-start.2 = (bf16[2,240,384]{2,1,0:T(8,128)(2,1)}, bf16[2,240,384]{2,1,0:T(8,128)(2,1)S(1)}, u32[]{:S(2)}, u32[]{:S(2)}) collective-permute-start(bf16[2,240,384]{2,1,0:T(8,128)(2,1)} %get-tuple-element.22), channel_id=1, source_target_pairs={{0,4},{2,6},{4,0},{6,2},{1,5},{3,7},{5,1},{7,3},{8,12},{10,14},{12... | collective-permute-start | bytes 1105928 | tf_op jit(solution)/shard_map/ppermute | solution.py:269
  6.9 10.5 %copy-start.4 = (bf16[2,240,384]{2,1,0:T(8,128)(2,1)S(1)}, bf16[2,240,384]{2,1,0:T(8,128)(2,1)}, u32[]{:S(2)}) copy-start(bf16[2,240,384]{2,1,0:T(8,128)(2,1)} %get-tuple-element.22) | copy-start | bytes 1105924
  6.9 24.9 %all-to-all-start = ((bf16[8,64,384]{2,1,0:T(8,128)(2,1)}), bf16[8,64,384]{2,1,0:T(8,128)(2,1)S(1)}, u32[]{:S(2)}, u32[]{:S(2)}) async-start(bf16[8,64,384]{2,1,0:T(8,128)(2,1)} %get-tuple-element.23), calls=%async_computation | async-start | bytes 786432 | tf_op jit(solution)/shard_map/all_to_all | solution.py:314
  19.8 9.4 %collective-permute-start.1 = (bf16[2,240,384]{2,1,0:T(8,128)(2,1)S(1)}, bf16[2,240,384]{2,1,0:T(8,128)(2,1)S(1)}, u32[]{:S(2)}, u32[]{:S(2)}) collective-permute-start(bf16[2,240,384]{2,1,0:T(8,128)(2,1)S(1)} %bitcast.27), channel_id=1, source_target_pairs={{0,2},{1,7},{2,0},{3,5},{4,6},{5,3},{6,4},{7,1},{8,10},{9,15},{10,... | collective-permute-start | bytes 1105928 | tf_op jit(solution)/shard_map/ppermute | solution.py:274
  22.3 23.7 %collective-permute-start = (bf16[2,240,384]{2,1,0:T(8,128)(2,1)S(1)}, bf16[2,240,384]{2,1,0:T(8,128)(2,1)S(1)}, u32[]{:S(2)}, u32[]{:S(2)}) collective-permute-start(bf16[2,240,384]{2,1,0:T(8,128)(2,1)S(1)} %bitcast.24), channel_id=1, source_target_pairs={{0,2},{1,7},{2,0},{3,5},{4,6},{5,3},{6,4},{7,1},{8,10},{9,15},{10,... | collective-permute-start | bytes 1105928 | tf_op jit(solution)/shard_map/ppermute | solution.py:274
  25.8 6.0 %copy-start.3 = (f32[384]{0:T(512)S(1)}, f32[384]{0:T(512)}, u32[]{:S(2)}) copy-start(f32[384]{0:T(512)} %bias.2) | copy-start | bytes 4612
  25.8 6.1 %collective-permute-start.3 = (bf16[2,240,384]{2,1,0:T(8,128)(2,1)S(1)}, bf16[2,240,384]{2,1,0:T(8,128)(2,1)S(1)}, u32[]{:S(2)}, u32[]{:S(2)}) collective-permute-start(bf16[2,240,384]{2,1,0:T(8,128)(2,1)S(1)} %collective-permute-done.2.rest_2_), channel_id=1, source_target_pairs={{0,1},{1,0},{2,3},{3,2},{4,5},{5,4},{6,7},{7,6},{8,9},{9,8},{10,11... | collective-permute-start | bytes 1105928 | tf_op jit(solution)/shard_map/ppermute | solution.py:243
  33.0 7.5 %collective-permute-start.4 = (bf16[64,1024]{1,0:T(8,128)(2,1)S(1)}, bf16[64,1024]{1,0:T(8,128)(2,1)S(1)}, u32[]{:S(2)}, u32[]{:S(2)}) collective-permute-start(bf16[64,1024]{1,0:T(8,128)(2,1)S(1)} %shard_map.76), channel_id=1, source_target_pairs={{1,2},{2,1},{3,4},{4,3},{5,6},{6,5},{7,0},{0,7},{9,10},{10,9},{11,... | collective-permute-start | bytes 393224 | tf_op jit(solution)/shard_map/ppermute | solution.py:251
  41.3 7.1 %collective-permute-start.5 = (bf16[64,512]{1,0:T(8,128)(2,1)S(1)}, bf16[64,512]{1,0:T(8,128)(2,1)S(1)}, u32[]{:S(2)}, u32[]{:S(2)}) collective-permute-start(bf16[64,512]{1,0:T(8,128)(2,1)S(1)} %get-tuple-element.29), channel_id=1, source_target_pairs={{0,64},{64,128},{128,192},{192,256},{256,320},{320,384},{384,448},... | collective-permute-start | bytes 196616 | tf_op jit(solution)/shard_map/ppermute | solution.py:262
  48.5 21.7 %copy-start.1 = (f32[384]{0:T(512)S(1)}, f32[384]{0:T(512)}, u32[]{:S(2)}) copy-start(f32[384]{0:T(512)} %gain.1) | copy-start | bytes 4612
  48.5 21.7 %copy-start.2 = (f32[384]{0:T(512)S(1)}, f32[384]{0:T(512)}, u32[]{:S(2)}) copy-start(f32[384]{0:T(512)} %bias.3) | copy-start | bytes 4612
  71.7 7.5 %collective-permute-start.6 = (bf16[64,1024]{1,0:T(8,128)(2,1)S(1)}, bf16[64,1024]{1,0:T(8,128)(2,1)S(1)}, u32[]{:S(2)}, u32[]{:S(2)}) collective-permute-start(bf16[64,1024]{1,0:T(8,128)(2,1)S(1)} %get-tuple-element.33), channel_id=1, source_target_pairs={{1,2},{2,1},{3,4},{4,3},{5,6},{6,5},{7,0},{0,7},{9,10},{10,9},{11,... | collective-permute-start | bytes 393224 | tf_op jit(solution)/shard_map/ppermute | solution.py:251
  79.2 6.9 %copy-start = (bf16[2,1,32,384]{3,2,1,0:T(8,128)(2,1)S(1)}, bf16[2,1,32,384]{3,2,1,0:T(8,128)(2,1)}, u32[]{:S(2)}) copy-start(bf16[2,1,32,384]{3,2,1,0:T(8,128)(2,1)} %param.7) | copy-start | bytes 147460
  79.9 6.2 %collective-permute-start.7 = (bf16[64,512]{1,0:T(8,128)(2,1)S(1)}, bf16[64,512]{1,0:T(8,128)(2,1)S(1)}, u32[]{:S(2)}, u32[]{:S(2)}) collective-permute-start(bf16[64,512]{1,0:T(8,128)(2,1)S(1)} %get-tuple-element.36), channel_id=1, source_target_pairs={{0,64},{64,128},{128,192},{192,256},{256,320},{320,384},{384,448},... | collective-permute-start | bytes 196616 | tf_op jit(solution)/shard_map/ppermute | solution.py:262

commit v8 on v7

--- a/solution.py
+++ b/solution.py
@@ -18,9 +18,8 @@
 BF16 = jnp.bfloat16
 
 
-def call(kernel, out_shape, scratch=(), smem=0, hbm=0, anywhere=0, n=0, vmem_limit=VMEM, flops=0):
+def call(kernel, out_shape, scratch=(), smem=0, anywhere=0, n=0, vmem_limit=VMEM, flops=0):
     specs = [pl.BlockSpec(memory_space=pltpu.SMEM)] * smem
-    specs += [pl.BlockSpec(memory_space=pltpu.HBM)] * hbm
     specs += [pl.BlockSpec(memory_space=pl.ANY)] * anywhere
     specs += [pl.BlockSpec(memory_space=pltpu.VMEM)] * (n - len(specs))
     multiple = isinstance(out_shape, (list, tuple))
@@ -48,26 +47,13 @@
     return v / (1.0 + jnp.exp(-v))
 
 
-def first_kernel(
-    latent_hbm, one_hbm, two_hbm, gain_hbm, hidden, pieces, latent, gain, weights, rows, sems
-):
-    copies = [
-        pltpu.make_async_copy(one_hbm, weights.at[0], sems.at[0]),
-        pltpu.make_async_copy(two_hbm, weights.at[1], sems.at[1]),
-        pltpu.make_async_copy(latent_hbm, latent, sems.at[2]),
-        pltpu.make_async_copy(gain_hbm, gain, sems.at[3]),
-    ]
-    for copy in copies:
-        copy.start()
+def first_kernel(latent, weight_one, weight_two, gain, hidden, pieces, rows):
     rows[...] = jnp.zeros_like(rows)
-    for conv in range(2):
-        copies[conv].wait()
+    for conv, weight in enumerate((weight_one, weight_two)):
         for tap in range(27):
             at = GROUP * (tap // 3 % 3) + 8 * (3 * (tap // 9) + tap % 3)
-            rows[at : at + 6, :] = weights[conv, tap].astype(F32)
+            rows[at : at + 6, :] = weight[tap].astype(F32)
         pieces[conv] = rows[...].astype(BF16)
-    copies[2].wait()
-    copies[3].wait()
     values = latent[...].astype(F32)
     mean = jnp.mean(values * values, axis=1, keepdims=True)
     scale = lax.rsqrt(mean + 1e-6) * gain[...].reshape(1, CHANNELS)
@@ -213,29 +199,21 @@
 
 def spread_kernel(own, earlier, latent, pieces, kept):
     result = block_values(own, earlier)
-    result = result.astype(F32)
     for z in range(8):
-        parts = []
-        for first in (0, 24):
-            for f in range(2):
-                at = 256 * f + 32 * z
-                parts.append(result[first : first + 24, at : at + 32])
-        pieces[z] = jnp.concatenate(parts, axis=1).astype(BF16)
+        frames = [result[:, 256 * f + 32 * z : 256 * f + 32 * z + 32] for f in range(2)]
+        pieces[z] = jnp.concatenate(frames, axis=1)
     kept[...] = latent[...]
 
 
 def finish_kernel(latent, gathered, out):
-    halves = gathered[...].reshape(8 * 24, 128)
-    frm, to = iota((8 * 24, CHANNELS), 0), iota((8 * 24, CHANNELS), 1)
-    conv = jnp.zeros((64, CHANNELS), F32)
-    for half in range(2):
-        pick = (to == BLOCK * (frm // 24) + lax.rem(frm, 24) + 24 * half).astype(F32).astype(BF16)
-        conv += lax.dot_general(
-            halves[:, 64 * half : 64 * half + 64],
-            pick,
-            (((0,), (0,)), ((), ())),
-            preferred_element_type=F32,
-        )
+    square = (CHANNELS, CHANNELS)
+    same = iota(square, 0) == iota(square, 1)
+    conv = lax.dot_general(
+        gathered[...].reshape(CHANNELS, 64),
+        same.astype(BF16),
+        (((0,), (0,)), ((), ())),
+        preferred_element_type=F32,
+    )
     out[...] = (latent[...].astype(F32) + conv).astype(BF16)
 
 
@@ -295,18 +273,8 @@
 
     hidden, pieces = call(
         first_kernel,
-        [
-            shape((8, 64, CHANNELS), BF16),
-            shape((2, SLOT, CHANNELS), BF16),
-        ],
-        [
-            pltpu.VMEM((64, CHANNELS), BF16),
-            pltpu.VMEM((CHANNELS,), F32),
-            pltpu.VMEM((2, 27, 6, CHANNELS), BF16),
-            pltpu.VMEM((SLOT, CHANNELS), F32),
-            pltpu.SemaphoreType.DMA((4,)),
-        ],
-        hbm=4,
+        [shape((8, 64, CHANNELS), BF16), shape((2, SLOT, CHANNELS), BF16)],
+        [pltpu.VMEM((SLOT, CHANNELS), F32)],
         n=4,
         vmem_limit=60 * 1024 * 1024,
     )(latent, weight_one, weight_two, gain_one)
@@ -334,7 +302,7 @@
     own, earlier = exchange(ids, bias_two, swap_chips(pair), *rest(1, 0)(ids, field, *weights_two))
     pieces, kept = call(
         spread_kernel,
-        [shape((8, 24, 128), BF16), shape((64, CHANNELS), BF16)],
+        [shape((8, BLOCK, 64), BF16), shape((64, CHANNELS), BF16)],
         n=3,
     )(own, earlier, latent)
     pieces = lax.all_to_all(pieces, "z", 0, 0)

time: 98.4 us -> 98.6 us (level)
  no operation moved by 1% of the time
where the time goes in v8:
time: 98.6 us; the launch traced here: 98 us
  blocking collectives  43.3 us (44%)
  starting transfers between devices  36.2 us (37%)
  Pallas kernels  10.4 us (11%)
  waiting for transfers between devices  7.55 us (8%)
    all_to_all x1, blocking collectives, per_device(): gathered = lax.all_to_all(middle, 'z', 0, 0)  21.7 us
    all_to_all x1, blocking collectives, per_device(): pieces = lax.all_to_all(pieces, 'z', 0, 0)  10.6 us
    all_to_all x1, starting transfers between devices, per_device(): gathered = lax.all_to_all(hidden, 'z', 0, 0)  10.5 us
    ppermute x2, starting transfers between devices, exchange(): return (own, lax.ppermute(later, 't', [(i, i + 1) for i in range(7)]))  7.62 us
    ppermute x2, starting transfers between devices, gather_weights(): lax.ppermute(both, ('x', 'core'), hops)  5.84 us
    ppermute x1, starting transfers between devices, gather_weights(): far = lax.ppermute(pieces, 'x', [(x, x ^ 2) for x in range(4)])  4.92 us
    all_gather x2, blocking collectives, gather_weights(): lax.all_gather(lax.ppermute(both, ('x', 'core'), hops), 'core', axis=0)  4.65 us
    ppermute x2, starting transfers between devices, swap_chips(): return lax.ppermute(pair, ('x', 'core'), swaps)  4.51 us
  transfers between devices with their start and end apart: 9, of which 5 were waited for; matrix products, arithmetic and copies ran while one was open for 0% of the time, Pallas kernels for 5%

profile of v8, /device:TPU:24, one launch (start us, length us, event | category | flops | bytes accessed | tf_op | source)
XLA Modules:
  0.0 98.0 jit_solution(4677835021388244623)
XLA Ops:
  0.0 2.0 %shard_map.73 = (bf16[8,64,384]{2,1,0:T(8,128)(2,1)}, bf16[2,240,384]{2,1,0:T(8,128)(2,1)}) custom-call(bf16[64,384]{1,0:T(8,128)(2,1)} %bitcast.32, bf16[27,6,384]{2,1,0:T(8,128)(2,1)} %bitcast.34, bf16[27,6,384]{2,1,0:T(8,128)(2,1)} %bitcast.35, f32[384]{0:T(512)} %gain.2), custom_call_target="tpu_custom_call" | custom-call | tf_op jit(solution)/shard_map/pallas_call | solution.py:274
  2.0 4.9 %collective-permute-start.2 = (bf16[2,240,384]{2,1,0:T(8,128)(2,1)}, bf16[2,240,384]{2,1,0:T(8,128)(2,1)S(1)}, u32[]{:S(2)}, u32[]{:S(2)}) collective-permute-start(bf16[2,240,384]{2,1,0:T(8,128)(2,1)} %get-tuple-element.22), channel_id=1, source_target_pairs={{0,4},{2,6},{4,0},{6,2},{1,5},{3,7},{5,1},{7,3},{8,12},{10,14},{12... | collective-permute-start | bytes 1105928 | tf_op jit(solution)/shard_map/ppermute | solution.py:247
  7.0 10.5 %all-to-all-start = ((bf16[8,64,384]{2,1,0:T(8,128)(2,1)}), bf16[8,64,384]{2,1,0:T(8,128)(2,1)S(1)}, u32[]{:S(2)}, u32[]{:S(2)}) async-start(bf16[8,64,384]{2,1,0:T(8,128)(2,1)} %get-tuple-element.23), calls=%async_computation | async-start | bytes 786432 | tf_op jit(solution)/shard_map/all_to_all | solution.py:282
  17.4 2.3 %all-gather = bf16[2,480,384]{2,1,0:T(8,128)(2,1)S(1)} all-gather(bf16[2,240,384]{2,1,0:T(8,128)(2,1)S(1)} %copy-done.4), channel_id=2, replica_groups=mesh['t'=8,'z'=8,'x'=4,'core'=2] {'core'}, dimensions={1}, use_global_device_ids=true | all-gather | bytes 1105920 | tf_op jit(solution)/shard_map/all_gather | solution.py:249
  19.8 2.5 %collective-permute-start.1 = (bf16[2,240,384]{2,1,0:T(8,128)(2,1)S(1)}, bf16[2,240,384]{2,1,0:T(8,128)(2,1)S(1)}, u32[]{:S(2)}, u32[]{:S(2)}) collective-permute-start(bf16[2,240,384]{2,1,0:T(8,128)(2,1)S(1)} %bitcast.27), channel_id=1, source_target_pairs={{0,2},{1,7},{2,0},{3,5},{4,6},{5,3},{6,4},{7,1},{8,10},{9,15},{10,... | collective-permute-start | bytes 1105928 | tf_op jit(solution)/shard_map/ppermute | solution.py:252
  22.4 3.3 %collective-permute-start = (bf16[2,240,384]{2,1,0:T(8,128)(2,1)S(1)}, bf16[2,240,384]{2,1,0:T(8,128)(2,1)S(1)}, u32[]{:S(2)}, u32[]{:S(2)}) collective-permute-start(bf16[2,240,384]{2,1,0:T(8,128)(2,1)S(1)} %bitcast.24), channel_id=1, source_target_pairs={{0,2},{1,7},{2,0},{3,5},{4,6},{5,3},{6,4},{7,1},{8,10},{9,15},{10,... | collective-permute-start | bytes 1105928 | tf_op jit(solution)/shard_map/ppermute | solution.py:252
  25.8 2.8 %collective-permute-start.3 = (bf16[2,240,384]{2,1,0:T(8,128)(2,1)S(1)}, bf16[2,240,384]{2,1,0:T(8,128)(2,1)S(1)}, u32[]{:S(2)}, u32[]{:S(2)}) collective-permute-start(bf16[2,240,384]{2,1,0:T(8,128)(2,1)S(1)} %collective-permute-done.2.rest_2_), channel_id=1, source_target_pairs={{0,1},{1,0},{2,3},{3,2},{4,5},{5,4},{6,7},{7,6},{8,9},{9,8},{10,11... | collective-permute-start | bytes 1105928 | tf_op jit(solution)/shard_map/ppermute | solution.py:221
  28.6 0.6 collective-permute-done.1
  29.3 2.3 %all-gather.2 = bf16[4,240,384]{2,1,0:T(8,128)(2,1)S(1)} all-gather(bf16[2,240,384]{2,1,0:T(8,128)(2,1)S(1)} %collective-permute-done.1), channel_id=4, replica_groups=mesh['t'=8,'z'=8,'x'=4,'core'=2] {'core'}, dimensions={0}, use_global_device_ids=true | all-gather | bytes 1105920 | tf_op jit(solution)/shard_map/all_gather | solution.py:252
  31.6 0.3 all-to-all-done.gathered
  31.9 1.2 %shard_map.76 = bf16[64,1024]{1,0:T(8,128)(2,1)S(1)} custom-call(s32[3]{0:T(128)S(1)} %pad_add_fusion.ids, bf16[512,384]{1,0:T(8,128)(2,1)S(1)} %get-tuple-element.24.field, bf16[2,240,384]{2,1,0:T(8,128)(2,1)S(1)} %bitcast.28, bf16[2,2,240,384]{3,2,1,0:T(8,128)(2,1)S(1)} %bitcast.22, bf16[2,240,384]{2,1,0:T(8,128)(2,1)S(1)} %collective-permute-done.2.rest_2_, ...), custom_call_target="tpu_custom_call" | custom-call | tf_op jit(solution)/shard_map/pallas_call | solution.py:289
  33.0 2.6 %collective-permute-start.4 = (bf16[64,1024]{1,0:T(8,128)(2,1)S(1)}, bf16[64,1024]{1,0:T(8,128)(2,1)S(1)}, u32[]{:S(2)}, u32[]{:S(2)}) collective-permute-start(bf16[64,1024]{1,0:T(8,128)(2,1)S(1)} %shard_map.76), channel_id=1, source_target_pairs={{1,2},{2,1},{3,4},{4,3},{5,6},{6,5},{7,0},{0,7},{9,10},{10,9},{11,... | collective-permute-start | bytes 393224 | tf_op jit(solution)/shard_map/ppermute | solution.py:229
  35.6 1.5 %shard_map.75 = (f32[64,1024]{1,0:T(8,128)S(1)}, bf16[64,1024]{1,0:T(8,128)(2,1)S(1)}) custom-call(s32[3]{0:T(128)S(1)} %pad_add_fusion.ids, bf16[512,384]{1,0:T(8,128)(2,1)S(1)} %get-tuple-element.24.field, bf16[2,240,384]{2,1,0:T(8,128)(2,1)S(1)} %bitcast.29, bf16[2,2,240,384]{3,2,1,0:T(8,128)(2,1)S(1)} %bitcast.23, ...), custom_call_target="tpu_custom_call" | custom-call | tf_op jit(solution)/shard_map/pallas_call | solution.py:290
  37.2 2.0 %all-gather.3 = bf16[128,1024]{1,0:T(8,128)(2,1)S(1)} all-gather(bf16[64,1024]{1,0:T(8,128)(2,1)S(1)} %get-tuple-element.26), channel_id=5, replica_groups=mesh['t'=8,'z'=8,'x'=4,'core'=2] {'core'}, dimensions={0}, use_global_device_ids=true | all-gather | bytes 393216 | tf_op jit(solution)/shard_map/all_gather | solution.py:233
  39.2 1.4 %collective-permute-done.4.pair = bf16[64,1024]{1,0:T(8,128)(2,1)S(1)} collective-permute-done((bf16[64,1024]{1,0:T(8,128)(2,1)S(1)}, bf16[64,1024]{1,0:T(8,128)(2,1)S(1)}, u32[]{:S(2)}, u32[]{:S(2)}) %collective-permute-start.4) | collective-permute-done | bytes 131104 | tf_op jit(solution)/shard_map/ppermute | solution.py:229
  40.5 0.8 shard_map.77
  41.3 4.7 %collective-permute-start.5 = (bf16[64,512]{1,0:T(8,128)(2,1)S(1)}, bf16[64,512]{1,0:T(8,128)(2,1)S(1)}, u32[]{:S(2)}, u32[]{:S(2)}) collective-permute-start(bf16[64,512]{1,0:T(8,128)(2,1)S(1)} %get-tuple-element.29), channel_id=1, source_target_pairs={{0,64},{64,128},{128,192},{192,256},{256,320},{320,384},{384,448},... | collective-permute-start | bytes 196616 | tf_op jit(solution)/shard_map/ppermute | solution.py:240
  46.0 2.3 %all-gather.1 = bf16[4,240,384]{2,1,0:T(8,128)(2,1)S(1)} all-gather(bf16[2,240,384]{2,1,0:T(8,128)(2,1)S(1)} %collective-permute-done), channel_id=3, replica_groups=mesh['t'=8,'z'=8,'x'=4,'core'=2] {'core'}, dimensions={0}, use_global_device_ids=true | all-gather | bytes 1105920 | tf_op jit(solution)/shard_map/all_gather | solution.py:252
  48.4 0.2 shard_map.78
  48.6 21.7 %all_to_all.15.gathered = bf16[8,48,512]{2,1,0:T(8,128)(2,1)S(1)} all-to-all(bf16[8,48,512]{2,1,0:T(8,128)(2,1)S(1)} %shard_map.78), channel_id=1, replica_groups=mesh['t'=8,'z'=8,'x'=4,'core'=2] {'z'}, dimensions={0} | all-to-all | bytes 786432 | tf_op jit(solution)/shard_map/all_to_all | solution.py:294
  70.3 1.4 %shard_map.79 = (bf16[64,1024]{1,0:T(8,128)(2,1)S(1)}, bf16[384,512]{1,0:T(8,128)(2,1)S(1)}, f32[384]{0:T(512)S(1)}) custom-call(s32[3]{0:T(128)S(1)} %pad_add_fusion.ids, bf16[8,48,512]{2,1,0:T(8,128)(2,1)S(1)} %all_to_all.15.gathered, f32[384]{0:T(512)S(1)} %copy-done.1, f32[384]{0:T(512)S(1)} %copy-done.2, bf16[2,240,384]{2,1,0:T(8,128)(2,1)S(1)} %bitcast.25, ...), custom_call_target="tpu_custom_call" | custom-call | tf_op jit(solution)/shard_map/pallas_call | solution.py:295
  71.7 1.9 %collective-permute-start.6 = (bf16[64,1024]{1,0:T(8,128)(2,1)S(1)}, bf16[64,1024]{1,0:T(8,128)(2,1)S(1)}, u32[]{:S(2)}, u32[]{:S(2)}) collective-permute-start(bf16[64,1024]{1,0:T(8,128)(2,1)S(1)} %get-tuple-element.33), channel_id=1, source_target_pairs={{1,2},{2,1},{3,4},{4,3},{5,6},{6,5},{7,0},{0,7},{9,10},{10,9},{11,... | collective-permute-start | bytes 393224 | tf_op jit(solution)/shard_map/ppermute | solution.py:229
  73.6 1.5 %shard_map.80 = (f32[64,1024]{1,0:T(8,128)S(1)}, bf16[64,1024]{1,0:T(8,128)(2,1)S(1)}) custom-call(s32[3]{0:T(128)S(1)} %pad_add_fusion.ids, bf16[384,512]{1,0:T(8,128)(2,1)S(1)} %get-tuple-element.30.field, bf16[2,240,384]{2,1,0:T(8,128)(2,1)S(1)} %bitcast.26, bf16[2,2,240,384]{3,2,1,0:T(8,128)(2,1)S(1)} %bitcast.21, ...), custom_call_target="tpu_custom_call" | custom-call | tf_op jit(solution)/shard_map/pallas_call | solution.py:302
  75.2 2.0 %all-gather.4 = bf16[128,1024]{1,0:T(8,128)(2,1)S(1)} all-gather(bf16[64,1024]{1,0:T(8,128)(2,1)S(1)} %get-tuple-element.32), channel_id=6, replica_groups=mesh['t'=8,'z'=8,'x'=4,'core'=2] {'core'}, dimensions={0}, use_global_device_ids=true | all-gather | bytes 393216 | tf_op jit(solution)/shard_map/all_gather | solution.py:233
  77.1 2.0 %collective-permute-done.6.pair = bf16[64,1024]{1,0:T(8,128)(2,1)S(1)} collective-permute-done((bf16[64,1024]{1,0:T(8,128)(2,1)S(1)}, bf16[64,1024]{1,0:T(8,128)(2,1)S(1)}, u32[]{:S(2)}, u32[]{:S(2)}) %collective-permute-start.6) | collective-permute-done | bytes 131104 | tf_op jit(solution)/shard_map/ppermute | solution.py:229
  79.2 0.8 shard_map.81
  80.0 2.9 %collective-permute-start.7 = (bf16[64,512]{1,0:T(8,128)(2,1)S(1)}, bf16[64,512]{1,0:T(8,128)(2,1)S(1)}, u32[]{:S(2)}, u32[]{:S(2)}) collective-permute-start(bf16[64,512]{1,0:T(8,128)(2,1)S(1)} %get-tuple-element.36), channel_id=1, source_target_pairs={{0,64},{64,128},{128,192},{192,256},{256,320},{320,384},{384,448},... | collective-permute-start | bytes 196616 | tf_op jit(solution)/shard_map/ppermute | solution.py:240
  82.9 3.2 %collective-permute-done.7.earlier = bf16[64,512]{1,0:T(8,128)(2,1)S(1)} collective-permute-done((bf16[64,512]{1,0:T(8,128)(2,1)S(1)}, bf16[64,512]{1,0:T(8,128)(2,1)S(1)}, u32[]{:S(2)}, u32[]{:S(2)}) %collective-permute-start.7) | collective-permute-done | bytes 65568 | tf_op jit(solution)/shard_map/ppermute | solution.py:240
  86.1 0.2 shard_map.82
  86.5 10.6 %all_to_all.16 = bf16[8,2,1536]{2,1,0:T(2,128)(2,1)S(1)} all-to-all(bf16[8,2,1536]{2,1,0:T(2,128)(2,1)S(1)} %reshape.25), channel_id=1, replica_groups=mesh['t'=8,'z'=8,'x'=4,'core'=2] {'z'}, dimensions={0} | all-to-all | bytes 98304 | tf_op jit(solution)/shard_map/all_to_all | solution.py:308
  97.1 0.1 reshape.26.gathered
  97.2 0.8 shard_map.83
  (18 shorter events, 0.3 us)
Async XLA Ops:
  2.0 23.8 %collective-permute-start.2 = (bf16[2,240,384]{2,1,0:T(8,128)(2,1)}, bf16[2,240,384]{2,1,0:T(8,128)(2,1)S(1)}, u32[]{:S(2)}, u32[]{:S(2)}) collective-permute-start(bf16[2,240,384]{2,1,0:T(8,128)(2,1)} %get-tuple-element.22), channel_id=1, source_target_pairs={{0,4},{2,6},{4,0},{6,2},{1,5},{3,7},{5,1},{7,3},{8,12},{10,14},{12... | collective-permute-start | bytes 1105928 | tf_op jit(solution)/shard_map/ppermute | solution.py:247
  7.0 10.5 %copy-start.4 = (bf16[2,240,384]{2,1,0:T(8,128)(2,1)S(1)}, bf16[2,240,384]{2,1,0:T(8,128)(2,1)}, u32[]{:S(2)}) copy-start(bf16[2,240,384]{2,1,0:T(8,128)(2,1)} %get-tuple-element.22) | copy-start | bytes 1105924
  7.0 24.9 %all-to-all-start = ((bf16[8,64,384]{2,1,0:T(8,128)(2,1)}), bf16[8,64,384]{2,1,0:T(8,128)(2,1)S(1)}, u32[]{:S(2)}, u32[]{:S(2)}) async-start(bf16[8,64,384]{2,1,0:T(8,128)(2,1)} %get-tuple-element.23), calls=%async_computation | async-start | bytes 786432 | tf_op jit(solution)/shard_map/all_to_all | solution.py:282
  19.8 9.4 %collective-permute-start.1 = (bf16[2,240,384]{2,1,0:T(8,128)(2,1)S(1)}, bf16[2,240,384]{2,1,0:T(8,128)(2,1)S(1)}, u32[]{:S(2)}, u32[]{:S(2)}) collective-permute-start(bf16[2,240,384]{2,1,0:T(8,128)(2,1)S(1)} %bitcast.27), channel_id=1, source_target_pairs={{0,2},{1,7},{2,0},{3,5},{4,6},{5,3},{6,4},{7,1},{8,10},{9,15},{10,... | collective-permute-start | bytes 1105928 | tf_op jit(solution)/shard_map/ppermute | solution.py:252
  22.4 23.7 %collective-permute-start = (bf16[2,240,384]{2,1,0:T(8,128)(2,1)S(1)}, bf16[2,240,384]{2,1,0:T(8,128)(2,1)S(1)}, u32[]{:S(2)}, u32[]{:S(2)}) collective-permute-start(bf16[2,240,384]{2,1,0:T(8,128)(2,1)S(1)} %bitcast.24), channel_id=1, source_target_pairs={{0,2},{1,7},{2,0},{3,5},{4,6},{5,3},{6,4},{7,1},{8,10},{9,15},{10,... | collective-permute-start | bytes 1105928 | tf_op jit(solution)/shard_map/ppermute | solution.py:252
  25.8 6.0 %copy-start.3 = (f32[384]{0:T(512)S(1)}, f32[384]{0:T(512)}, u32[]{:S(2)}) copy-start(f32[384]{0:T(512)} %bias.2) | copy-start | bytes 4612
  25.8 6.1 %collective-permute-start.3 = (bf16[2,240,384]{2,1,0:T(8,128)(2,1)S(1)}, bf16[2,240,384]{2,1,0:T(8,128)(2,1)S(1)}, u32[]{:S(2)}, u32[]{:S(2)}) collective-permute-start(bf16[2,240,384]{2,1,0:T(8,128)(2,1)S(1)} %collective-permute-done.2.rest_2_), channel_id=1, source_target_pairs={{0,1},{1,0},{2,3},{3,2},{4,5},{5,4},{6,7},{7,6},{8,9},{9,8},{10,11... | collective-permute-start | bytes 1105928 | tf_op jit(solution)/shard_map/ppermute | solution.py:221
  33.0 7.5 %collective-permute-start.4 = (bf16[64,1024]{1,0:T(8,128)(2,1)S(1)}, bf16[64,1024]{1,0:T(8,128)(2,1)S(1)}, u32[]{:S(2)}, u32[]{:S(2)}) collective-permute-start(bf16[64,1024]{1,0:T(8,128)(2,1)S(1)} %shard_map.76), channel_id=1, source_target_pairs={{1,2},{2,1},{3,4},{4,3},{5,6},{6,5},{7,0},{0,7},{9,10},{10,9},{11,... | collective-permute-start | bytes 393224 | tf_op jit(solution)/shard_map/ppermute | solution.py:229
  41.3 7.0 %collective-permute-start.5 = (bf16[64,512]{1,0:T(8,128)(2,1)S(1)}, bf16[64,512]{1,0:T(8,128)(2,1)S(1)}, u32[]{:S(2)}, u32[]{:S(2)}) collective-permute-start(bf16[64,512]{1,0:T(8,128)(2,1)S(1)} %get-tuple-element.29), channel_id=1, source_target_pairs={{0,64},{64,128},{128,192},{192,256},{256,320},{320,384},{384,448},... | collective-permute-start | bytes 196616 | tf_op jit(solution)/shard_map/ppermute | solution.py:240
  48.5 21.7 %copy-start.1 = (f32[384]{0:T(512)S(1)}, f32[384]{0:T(512)}, u32[]{:S(2)}) copy-start(f32[384]{0:T(512)} %gain.3) | copy-start | bytes 4612
  48.5 21.7 %copy-start.2 = (f32[384]{0:T(512)S(1)}, f32[384]{0:T(512)}, u32[]{:S(2)}) copy-start(f32[384]{0:T(512)} %bias.3) | copy-start | bytes 4612
  71.7 7.5 %collective-permute-start.6 = (bf16[64,1024]{1,0:T(8,128)(2,1)S(1)}, bf16[64,1024]{1,0:T(8,128)(2,1)S(1)}, u32[]{:S(2)}, u32[]{:S(2)}) collective-permute-start(bf16[64,1024]{1,0:T(8,128)(2,1)S(1)} %get-tuple-element.33), channel_id=1, source_target_pairs={{1,2},{2,1},{3,4},{4,3},{5,6},{6,5},{7,0},{0,7},{9,10},{10,9},{11,... | collective-permute-start | bytes 393224 | tf_op jit(solution)/shard_map/ppermute | solution.py:229
  79.2 6.9 %copy-start = (bf16[2,1,32,384]{3,2,1,0:T(8,128)(2,1)S(1)}, bf16[2,1,32,384]{3,2,1,0:T(8,128)(2,1)}, u32[]{:S(2)}) copy-start(bf16[2,1,32,384]{3,2,1,0:T(8,128)(2,1)} %param.7) | copy-start | bytes 147460
  80.0 6.2 %collective-permute-start.7 = (bf16[64,512]{1,0:T(8,128)(2,1)S(1)}, bf16[64,512]{1,0:T(8,128)(2,1)S(1)}, u32[]{:S(2)}, u32[]{:S(2)}) collective-permute-start(bf16[64,512]{1,0:T(8,128)(2,1)S(1)} %get-tuple-element.36), channel_id=1, source_target_pairs={{0,64},{64,128},{128,192},{192,256},{256,320},{320,384},{384,448},... | collective-permute-start | bytes 196616 | tf_op jit(solution)/shard_map/ppermute | solution.py:240

commit v9 on v8

--- a/solution.py
+++ b/solution.py
@@ -289,7 +289,7 @@
     pair = call(pair_one_kernel, half, [group, products], smem=1, n=6)(ids, field, *weights_one)
     own, earlier = exchange(ids, bias_one, swap_chips(pair), *rest(0, 1)(ids, field, *weights_one))
     middle = call(middle_kernel, shape((8, BLOCK, LANES), BF16), anywhere=1, n=3)(
-        weights_two[1], own, earlier
+        weights_two[2], own, earlier
     )
     gathered = lax.all_to_all(middle, "z", 0, 0)
     pair, field, bias_two = call(

time: 98.6 us -> 103 us (1.045)
  the two profiles are of different devices: /device:TPU:24 before, /device:TPU:32 now
where the time goes in v9:
time: 103 us; the launch traced here: 102 us
  starting transfers between devices  41.2 us (40%)
  waiting for transfers between devices  25.2 us (24%)
  blocking collectives  24.4 us (24%)
  Pallas kernels  11.2 us (11%)
    all_to_all x1, blocking collectives, per_device(): pieces = lax.all_to_all(pieces, 'z', 0, 0)  13.3 us
    all_to_all x1, starting transfers between devices, per_device(): gathered = lax.all_to_all(hidden, 'z', 0, 0)  10.4 us
    ppermute x2, waiting for transfers between devices, exchange(): return (own, lax.ppermute(later, 't', [(i, i + 1) for i in range(7)]))  10.2 us
    ppermute x2, waiting for transfers between devices, gather_weights(): lax.ppermute(both, ('x', 'core'), hops)  9.5 us
    ppermute x2, starting transfers between devices, swap_chips(): return lax.ppermute(pair, ('x', 'core'), swaps)  7.95 us
    all_to_all x1, starting transfers between devices, per_device(): gathered = lax.all_to_all(middle, 'z', 0, 0)  6.91 us
    ppermute x1, starting transfers between devices, gather_weights(): far = lax.ppermute(pieces, 'x', [(x, x ^ 2) for x in range(4)])  4.93 us
    all_gather x2, blocking collectives, gather_weights(): lax.all_gather(lax.ppermute(both, ('x', 'core'), hops), 'core', axis=0)  4.77 us
  transfers between devices with their start and end apart: 10, of which 6 were waited for; matrix products, arithmetic and copies ran while one was open for 0% of the time, Pallas kernels for 3%

profile of v9, /device:TPU:32, one launch (start us, length us, event | category | flops | bytes accessed | tf_op | source)
XLA Modules:
  0.0 102.4 jit_solution(8316920838975801883)
XLA Ops:
  0.0 2.0 %shard_map.73 = (bf16[8,64,384]{2,1,0:T(8,128)(2,1)}, bf16[2,240,384]{2,1,0:T(8,128)(2,1)}) custom-call(bf16[64,384]{1,0:T(8,128)(2,1)} %bitcast.31, bf16[27,6,384]{2,1,0:T(8,128)(2,1)} %bitcast.33, bf16[27,6,384]{2,1,0:T(8,128)(2,1)} %bitcast.34, f32[384]{0:T(512)} %gain.2), custom_call_target="tpu_custom_call" | custom-call | tf_op jit(solution)/shard_map/pallas_call | solution.py:274
  2.0 10.4 %all-to-all-start = ((bf16[8,64,384]{2,1,0:T(8,128)(2,1)}), bf16[8,64,384]{2,1,0:T(8,128)(2,1)S(1)}, u32[]{:S(2)}, u32[]{:S(2)}) async-start(bf16[8,64,384]{2,1,0:T(8,128)(2,1)} %get-tuple-element.23), calls=%async_computation | async-start | bytes 786432 | tf_op jit(solution)/shard_map/all_to_all | solution.py:282
  12.5 4.9 %collective-permute-start = (bf16[2,240,384]{2,1,0:T(8,128)(2,1)S(1)}, bf16[2,240,384]{2,1,0:T(8,128)(2,1)S(1)}, u32[]{:S(2)}, u32[]{:S(2)}) collective-permute-start(bf16[2,240,384]{2,1,0:T(8,128)(2,1)S(1)} %copy-done.4), channel_id=1, source_target_pairs={{0,4},{2,6},{4,0},{6,2},{1,5},{3,7},{5,1},{7,3},{8,12},{10,14},{12... | collective-permute-start | bytes 1105928 | tf_op jit(solution)/shard_map/ppermute | solution.py:247
  17.4 2.3 %all-gather = bf16[2,480,384]{2,1,0:T(8,128)(2,1)S(1)} all-gather(bf16[2,240,384]{2,1,0:T(8,128)(2,1)S(1)} %copy-done.4), channel_id=2, replica_groups=mesh['t'=8,'z'=8,'x'=4,'core'=2] {'core'}, dimensions={1}, use_global_device_ids=true | all-gather | bytes 1105920 | tf_op jit(solution)/shard_map/all_gather | solution.py:249
  19.8 2.5 %collective-permute-start.1 = (bf16[2,240,384]{2,1,0:T(8,128)(2,1)S(1)}, bf16[2,240,384]{2,1,0:T(8,128)(2,1)S(1)}, u32[]{:S(2)}, u32[]{:S(2)}) collective-permute-start(bf16[2,240,384]{2,1,0:T(8,128)(2,1)S(1)} %bitcast.26), channel_id=1, source_target_pairs={{0,2},{1,7},{2,0},{3,5},{4,6},{5,3},{6,4},{7,1},{8,10},{9,15},{10,... | collective-permute-start | bytes 1105928 | tf_op jit(solution)/shard_map/ppermute | solution.py:252
  22.4 3.5 %collective-permute-done.rest_2_.after = bf16[2,240,384]{2,1,0:T(8,128)(2,1)S(1)} collective-permute-done((bf16[2,240,384]{2,1,0:T(8,128)(2,1)S(1)}, bf16[2,240,384]{2,1,0:T(8,128)(2,1)S(1)}, u32[]{:S(2)}, u32[]{:S(2)}) %collective-permute-start) | collective-permute-done | bytes 368672 | tf_op jit(solution)/shard_map/ppermute | solution.py:247
  25.9 1.9 %collective-permute-start.2 = (bf16[2,240,384]{2,1,0:T(8,128)(2,1)S(1)}, bf16[2,240,384]{2,1,0:T(8,128)(2,1)S(1)}, u32[]{:S(2)}, u32[]{:S(2)}) collective-permute-start(bf16[2,240,384]{2,1,0:T(8,128)(2,1)S(1)} %collective-permute-done.rest_2_.after), channel_id=1, source_target_pairs={{0,1},{1,0},{2,3},{3,2},{4,5},{5,4},{6,7},{7,6},{8,9},{9,8},{10,11... | collective-permute-start | bytes 1105928 | tf_op jit(solution)/shard_map/ppermute | solution.py:221
  27.8 2.1 %collective-permute-done.1 = bf16[2,240,384]{2,1,0:T(8,128)(2,1)S(1)} collective-permute-done((bf16[2,240,384]{2,1,0:T(8,128)(2,1)S(1)}, bf16[2,240,384]{2,1,0:T(8,128)(2,1)S(1)}, u32[]{:S(2)}, u32[]{:S(2)}) %collective-permute-start.1) | collective-permute-done | bytes 368672 | tf_op jit(solution)/shard_map/ppermute | solution.py:252
  30.0 2.3 %all-gather.1 = bf16[4,240,384]{2,1,0:T(8,128)(2,1)S(1)} all-gather(bf16[2,240,384]{2,1,0:T(8,128)(2,1)S(1)} %collective-permute-done.1), channel_id=3, replica_groups=mesh['t'=8,'z'=8,'x'=4,'core'=2] {'core'}, dimensions={0}, use_global_device_ids=true | all-gather | bytes 1105920 | tf_op jit(solution)/shard_map/all_gather | solution.py:252
  32.4 1.2 %shard_map.76 = bf16[64,1024]{1,0:T(8,128)(2,1)S(1)} custom-call(s32[3]{0:T(128)S(1)} %pad_add_fusion.ids, bf16[512,384]{1,0:T(8,128)(2,1)S(1)} %get-tuple-element.24.field, bf16[2,240,384]{2,1,0:T(8,128)(2,1)S(1)} %bitcast.27, bf16[2,2,240,384]{3,2,1,0:T(8,128)(2,1)S(1)} %bitcast.19, bf16[2,240,384]{2,1,0:T(8,128)(2,1)S(1)} %collective-permute-done.rest_2_.after, ...), custom_call_target="tpu_custom_call" | custom-call | tf_op jit(solution)/shard_map/pallas_call | solution.py:289
  33.5 4.0 %collective-permute-start.3 = (bf16[64,1024]{1,0:T(8,128)(2,1)S(1)}, bf16[64,1024]{1,0:T(8,128)(2,1)S(1)}, u32[]{:S(2)}, u32[]{:S(2)}) collective-permute-start(bf16[64,1024]{1,0:T(8,128)(2,1)S(1)} %shard_map.76), channel_id=1, source_target_pairs={{1,2},{2,1},{3,4},{4,3},{5,6},{6,5},{7,0},{0,7},{9,10},{10,9},{11,... | collective-permute-start | bytes 393224 | tf_op jit(solution)/shard_map/ppermute | solution.py:229
  37.5 1.5 %shard_map.75 = (f32[64,1024]{1,0:T(8,128)S(1)}, bf16[64,1024]{1,0:T(8,128)(2,1)S(1)}) custom-call(s32[3]{0:T(128)S(1)} %pad_add_fusion.ids, bf16[512,384]{1,0:T(8,128)(2,1)S(1)} %get-tuple-element.24.field, bf16[2,240,384]{2,1,0:T(8,128)(2,1)S(1)} %bitcast.28, bf16[2,2,240,384]{3,2,1,0:T(8,128)(2,1)S(1)} %bitcast.20, ...), custom_call_target="tpu_custom_call" | custom-call | tf_op jit(solution)/shard_map/pallas_call | solution.py:290
  39.0 2.0 %all-gather.2 = bf16[128,1024]{1,0:T(8,128)(2,1)S(1)} all-gather(bf16[64,1024]{1,0:T(8,128)(2,1)S(1)} %get-tuple-element.26), channel_id=4, replica_groups=mesh['t'=8,'z'=8,'x'=4,'core'=2] {'core'}, dimensions={0}, use_global_device_ids=true | all-gather | bytes 393216 | tf_op jit(solution)/shard_map/all_gather | solution.py:233
  41.0 0.8 shard_map.77
  41.8 2.6 %collective-permute-start.4 = (bf16[64,512]{1,0:T(8,128)(2,1)S(1)}, bf16[64,512]{1,0:T(8,128)(2,1)S(1)}, u32[]{:S(2)}, u32[]{:S(2)}) collective-permute-start(bf16[64,512]{1,0:T(8,128)(2,1)S(1)} %get-tuple-element.29), channel_id=1, source_target_pairs={{0,64},{64,128},{128,192},{192,256},{256,320},{320,384},{384,448},... | collective-permute-start | bytes 196616 | tf_op jit(solution)/shard_map/ppermute | solution.py:240
  44.4 4.8 %collective-permute-done.4.earlier = bf16[64,512]{1,0:T(8,128)(2,1)S(1)} collective-permute-done((bf16[64,512]{1,0:T(8,128)(2,1)S(1)}, bf16[64,512]{1,0:T(8,128)(2,1)S(1)}, u32[]{:S(2)}, u32[]{:S(2)}) %collective-permute-start.4) | collective-permute-done | bytes 65568 | tf_op jit(solution)/shard_map/ppermute | solution.py:240
  49.2 0.9 shard_map.78
  50.1 6.9 %all-to-all-start.1 = ((bf16[8,48,512]{2,1,0:T(8,128)(2,1)}), bf16[8,48,512]{2,1,0:T(8,128)(2,1)S(1)}, u32[]{:S(2)}, u32[]{:S(2)}) async-start(bf16[8,48,512]{2,1,0:T(8,128)(2,1)} %shard_map.78), calls=%async_computation.1 | async-start | bytes 786432 | tf_op jit(solution)/shard_map/all_to_all | solution.py:294
  57.0 2.0 %collective-permute-start.5 = (bf16[2,240,384]{2,1,0:T(8,128)(2,1)S(1)}, bf16[2,240,384]{2,1,0:T(8,128)(2,1)S(1)}, u32[]{:S(2)}, u32[]{:S(2)}) collective-permute-start(bf16[2,240,384]{2,1,0:T(8,128)(2,1)S(1)} %bitcast.23), channel_id=1, source_target_pairs={{0,2},{1,7},{2,0},{3,5},{4,6},{5,3},{6,4},{7,1},{8,10},{9,15},{10,... | collective-permute-start | bytes 1105928 | tf_op jit(solution)/shard_map/ppermute | solution.py:252
  59.0 7.4 %collective-permute-done.5 = bf16[2,240,384]{2,1,0:T(8,128)(2,1)S(1)} collective-permute-done((bf16[2,240,384]{2,1,0:T(8,128)(2,1)S(1)}, bf16[2,240,384]{2,1,0:T(8,128)(2,1)S(1)}, u32[]{:S(2)}, u32[]{:S(2)}) %collective-permute-start.5) | collective-permute-done | bytes 368672 | tf_op jit(solution)/shard_map/ppermute | solution.py:252
  66.4 2.5 %all-gather.3 = bf16[4,240,384]{2,1,0:T(8,128)(2,1)S(1)} all-gather(bf16[2,240,384]{2,1,0:T(8,128)(2,1)S(1)} %collective-permute-done.5), channel_id=5, replica_groups=mesh['t'=8,'z'=8,'x'=4,'core'=2] {'core'}, dimensions={0}, use_global_device_ids=true | all-gather | bytes 1105920 | tf_op jit(solution)/shard_map/all_gather | solution.py:252
  68.8 1.9 %all-to-all-done.1.gathered = bf16[8,48,512]{2,1,0:T(8,128)(2,1)S(1)} async-done(((bf16[8,48,512]{2,1,0:T(8,128)(2,1)}), bf16[8,48,512]{2,1,0:T(8,128)(2,1)S(1)}, u32[]{:S(2)}, u32[]{:S(2)}) %all-to-all-start.1) | async-done | bytes 393248 | tf_op jit(solution)/shard_map/all_to_all | solution.py:294
  70.7 1.4 %shard_map.79 = (bf16[64,1024]{1,0:T(8,128)(2,1)S(1)}, bf16[384,512]{1,0:T(8,128)(2,1)S(1)}, f32[384]{0:T(512)S(1)}) custom-call(s32[3]{0:T(128)S(1)} %pad_add_fusion.ids, bf16[8,48,512]{2,1,0:T(8,128)(2,1)S(1)} %all-to-all-done.1.gathered, f32[384]{0:T(512)S(1)} %copy-done.1, f32[384]{0:T(512)S(1)} %copy-done.2, bf16[2,240,384]{2,1,0:T(8,128)(2,1)S(1)} %bitcast.24, ...), custom_call_target="tpu_custom_call" | custom-call | tf_op jit(solution)/shard_map/pallas_call | solution.py:295
  72.2 4.0 %collective-permute-start.6 = (bf16[64,1024]{1,0:T(8,128)(2,1)S(1)}, bf16[64,1024]{1,0:T(8,128)(2,1)S(1)}, u32[]{:S(2)}, u32[]{:S(2)}) collective-permute-start(bf16[64,1024]{1,0:T(8,128)(2,1)S(1)} %get-tuple-element.33), channel_id=1, source_target_pairs={{1,2},{2,1},{3,4},{4,3},{5,6},{6,5},{7,0},{0,7},{9,10},{10,9},{11,... | collective-permute-start | bytes 393224 | tf_op jit(solution)/shard_map/ppermute | solution.py:229
  76.2 1.5 %shard_map.80 = (f32[64,1024]{1,0:T(8,128)S(1)}, bf16[64,1024]{1,0:T(8,128)(2,1)S(1)}) custom-call(s32[3]{0:T(128)S(1)} %pad_add_fusion.ids, bf16[384,512]{1,0:T(8,128)(2,1)S(1)} %get-tuple-element.30.field, bf16[2,240,384]{2,1,0:T(8,128)(2,1)S(1)} %bitcast.25, bf16[2,2,240,384]{3,2,1,0:T(8,128)(2,1)S(1)} %bitcast.22, ...), custom_call_target="tpu_custom_call" | custom-call | tf_op jit(solution)/shard_map/pallas_call | solution.py:302
  77.7 2.0 %all-gather.4 = bf16[128,1024]{1,0:T(8,128)(2,1)S(1)} all-gather(bf16[64,1024]{1,0:T(8,128)(2,1)S(1)} %get-tuple-element.32), channel_id=6, replica_groups=mesh['t'=8,'z'=8,'x'=4,'core'=2] {'core'}, dimensions={0}, use_global_device_ids=true | all-gather | bytes 393216 | tf_op jit(solution)/shard_map/all_gather | solution.py:233
  79.7 0.8 shard_map.81
  80.5 1.9 %collective-permute-start.7 = (bf16[64,512]{1,0:T(8,128)(2,1)S(1)}, bf16[64,512]{1,0:T(8,128)(2,1)S(1)}, u32[]{:S(2)}, u32[]{:S(2)}) collective-permute-start(bf16[64,512]{1,0:T(8,128)(2,1)S(1)} %get-tuple-element.36), channel_id=1, source_target_pairs={{0,64},{64,128},{128,192},{192,256},{256,320},{320,384},{384,448},... | collective-permute-start | bytes 196616 | tf_op jit(solution)/shard_map/ppermute | solution.py:240
  82.4 5.4 %collective-permute-done.7.earlier = bf16[64,512]{1,0:T(8,128)(2,1)S(1)} collective-permute-done((bf16[64,512]{1,0:T(8,128)(2,1)S(1)}, bf16[64,512]{1,0:T(8,128)(2,1)S(1)}, u32[]{:S(2)}, u32[]{:S(2)}) %collective-permute-start.7) | collective-permute-done | bytes 65568 | tf_op jit(solution)/shard_map/ppermute | solution.py:240
  87.8 0.2 shard_map.82
  88.2 13.3 %all_to_all.15 = bf16[8,2,1536]{2,1,0:T(2,128)(2,1)S(1)} all-to-all(bf16[8,2,1536]{2,1,0:T(2,128)(2,1)S(1)} %reshape.25), channel_id=1, replica_groups=mesh['t'=8,'z'=8,'x'=4,'core'=2] {'z'}, dimensions={0} | all-to-all | bytes 98304 | tf_op jit(solution)/shard_map/all_to_all | solution.py:308
  101.6 0.8 shard_map.83
  (19 shorter events, 0.5 us)
Async XLA Ops:
  2.0 10.5 %copy-start.4 = (bf16[2,240,384]{2,1,0:T(8,128)(2,1)S(1)}, bf16[2,240,384]{2,1,0:T(8,128)(2,1)}, u32[]{:S(2)}) copy-start(bf16[2,240,384]{2,1,0:T(8,128)(2,1)} %get-tuple-element.22) | copy-start | bytes 1105924
  2.0 30.3 %all-to-all-start = ((bf16[8,64,384]{2,1,0:T(8,128)(2,1)}), bf16[8,64,384]{2,1,0:T(8,128)(2,1)S(1)}, u32[]{:S(2)}, u32[]{:S(2)}) async-start(bf16[8,64,384]{2,1,0:T(8,128)(2,1)} %get-tuple-element.23), calls=%async_computation | async-start | bytes 786432 | tf_op jit(solution)/shard_map/all_to_all | solution.py:282
  12.5 13.5 %collective-permute-start = (bf16[2,240,384]{2,1,0:T(8,128)(2,1)S(1)}, bf16[2,240,384]{2,1,0:T(8,128)(2,1)S(1)}, u32[]{:S(2)}, u32[]{:S(2)}) collective-permute-start(bf16[2,240,384]{2,1,0:T(8,128)(2,1)S(1)} %copy-done.4), channel_id=1, source_target_pairs={{0,4},{2,6},{4,0},{6,2},{1,5},{3,7},{5,1},{7,3},{8,12},{10,14},{12... | collective-permute-start | bytes 1105928 | tf_op jit(solution)/shard_map/ppermute | solution.py:247
  19.8 10.2 %collective-permute-start.1 = (bf16[2,240,384]{2,1,0:T(8,128)(2,1)S(1)}, bf16[2,240,384]{2,1,0:T(8,128)(2,1)S(1)}, u32[]{:S(2)}, u32[]{:S(2)}) collective-permute-start(bf16[2,240,384]{2,1,0:T(8,128)(2,1)S(1)} %bitcast.26), channel_id=1, source_target_pairs={{0,2},{1,7},{2,0},{3,5},{4,6},{5,3},{6,4},{7,1},{8,10},{9,15},{10,... | collective-permute-start | bytes 1105928 | tf_op jit(solution)/shard_map/ppermute | solution.py:252
  22.4 9.9 %copy-start.3 = (f32[384]{0:T(512)S(1)}, f32[384]{0:T(512)}, u32[]{:S(2)}) copy-start(f32[384]{0:T(512)} %bias.2) | copy-start | bytes 4612
  25.9 6.4 %collective-permute-start.2 = (bf16[2,240,384]{2,1,0:T(8,128)(2,1)S(1)}, bf16[2,240,384]{2,1,0:T(8,128)(2,1)S(1)}, u32[]{:S(2)}, u32[]{:S(2)}) collective-permute-start(bf16[2,240,384]{2,1,0:T(8,128)(2,1)S(1)} %collective-permute-done.rest_2_.after), channel_id=1, source_target_pairs={{0,1},{1,0},{2,3},{3,2},{4,5},{5,4},{6,7},{7,6},{8,9},{9,8},{10,11... | collective-permute-start | bytes 1105928 | tf_op jit(solution)/shard_map/ppermute | solution.py:221
  33.5 7.5 %collective-permute-start.3 = (bf16[64,1024]{1,0:T(8,128)(2,1)S(1)}, bf16[64,1024]{1,0:T(8,128)(2,1)S(1)}, u32[]{:S(2)}, u32[]{:S(2)}) collective-permute-start(bf16[64,1024]{1,0:T(8,128)(2,1)S(1)} %shard_map.76), channel_id=1, source_target_pairs={{1,2},{2,1},{3,4},{4,3},{5,6},{6,5},{7,0},{0,7},{9,10},{10,9},{11,... | collective-permute-start | bytes 393224 | tf_op jit(solution)/shard_map/ppermute | solution.py:229
  41.8 7.4 %collective-permute-start.4 = (bf16[64,512]{1,0:T(8,128)(2,1)S(1)}, bf16[64,512]{1,0:T(8,128)(2,1)S(1)}, u32[]{:S(2)}, u32[]{:S(2)}) collective-permute-start(bf16[64,512]{1,0:T(8,128)(2,1)S(1)} %get-tuple-element.29), channel_id=1, source_target_pairs={{0,64},{64,128},{128,192},{192,256},{256,320},{320,384},{384,448},... | collective-permute-start | bytes 196616 | tf_op jit(solution)/shard_map/ppermute | solution.py:240
  50.1 20.7 %all-to-all-start.1 = ((bf16[8,48,512]{2,1,0:T(8,128)(2,1)}), bf16[8,48,512]{2,1,0:T(8,128)(2,1)S(1)}, u32[]{:S(2)}, u32[]{:S(2)}) async-start(bf16[8,48,512]{2,1,0:T(8,128)(2,1)} %shard_map.78), calls=%async_computation.1 | async-start | bytes 786432 | tf_op jit(solution)/shard_map/all_to_all | solution.py:294
  57.0 9.4 %collective-permute-start.5 = (bf16[2,240,384]{2,1,0:T(8,128)(2,1)S(1)}, bf16[2,240,384]{2,1,0:T(8,128)(2,1)S(1)}, u32[]{:S(2)}, u32[]{:S(2)}) collective-permute-start(bf16[2,240,384]{2,1,0:T(8,128)(2,1)S(1)} %bitcast.23), channel_id=1, source_target_pairs={{0,2},{1,7},{2,0},{3,5},{4,6},{5,3},{6,4},{7,1},{8,10},{9,15},{10,... | collective-permute-start | bytes 1105928 | tf_op jit(solution)/shard_map/ppermute | solution.py:252
  66.4 4.4 %copy-start.1 = (f32[384]{0:T(512)S(1)}, f32[384]{0:T(512)}, u32[]{:S(2)}) copy-start(f32[384]{0:T(512)} %gain.3) | copy-start | bytes 4612
  66.4 4.4 %copy-start.2 = (f32[384]{0:T(512)S(1)}, f32[384]{0:T(512)}, u32[]{:S(2)}) copy-start(f32[384]{0:T(512)} %bias.3) | copy-start | bytes 4612
  72.2 7.5 %collective-permute-start.6 = (bf16[64,1024]{1,0:T(8,128)(2,1)S(1)}, bf16[64,1024]{1,0:T(8,128)(2,1)S(1)}, u32[]{:S(2)}, u32[]{:S(2)}) collective-permute-start(bf16[64,1024]{1,0:T(8,128)(2,1)S(1)} %get-tuple-element.33), channel_id=1, source_target_pairs={{1,2},{2,1},{3,4},{4,3},{5,6},{6,5},{7,0},{0,7},{9,10},{10,9},{11,... | collective-permute-start | bytes 393224 | tf_op jit(solution)/shard_map/ppermute | solution.py:229
  79.7 8.1 %copy-start = (bf16[2,1,32,384]{3,2,1,0:T(8,128)(2,1)S(1)}, bf16[2,1,32,384]{3,2,1,0:T(8,128)(2,1)}, u32[]{:S(2)}) copy-start(bf16[2,1,32,384]{3,2,1,0:T(8,128)(2,1)} %param.7) | copy-start | bytes 147460
  80.5 7.4 %collective-permute-start.7 = (bf16[64,512]{1,0:T(8,128)(2,1)S(1)}, bf16[64,512]{1,0:T(8,128)(2,1)S(1)}, u32[]{:S(2)}, u32[]{:S(2)}) collective-permute-start(bf16[64,512]{1,0:T(8,128)(2,1)S(1)} %get-tuple-element.36), channel_id=1, source_target_pairs={{0,64},{64,128},{128,192},{192,256},{256,320},{320,384},{384,448},... | collective-permute-start | bytes 196616 | tf_op jit(solution)/shard_map/ppermute | solution.py:240
